TPU v7x, 32 devices: a whole 2x2x4 slice. The times are simulated.
32 devices in a mesh: dp: 16 (over z, y, core), seq: 2 (over x).
Axes of the slice: x: 2, y: 2, z: 4, core: 2. Of those that a mesh axis runs over, the one named last changes fastest.
Arguments:
- frames: bfloat16 [64, 512, 1024], P('dp', 'seq'), may hold values from -6 to 6
- cotangent: bfloat16 [64, 512, 1024], P('dp', 'seq'), may hold values from -6 to 6
- lengths: int32 [64], P('dp'), may hold values from 51 to 500, as said below
- qkv_weight: bfloat16 [1024, 3072], replicated, may hold values from -0.1875 to 0.1875
- out_weight: bfloat16 [1024, 1024], replicated, may hold values from -1 to 1
- gate_weight: bfloat16 [1024, 4096], replicated, may hold values from -0.1875 to 0.1875
- up_weight: bfloat16 [1024, 4096], replicated, may hold values from -0.1875 to 0.1875
- down_weight: bfloat16 [4096, 1024], replicated, may hold values from -0.09375 to 0.09375
- gain_table: float32 [1024, 4], replicated, may hold values from 0.1 to 1.9
- bias_table: float32 [1024, 2], replicated, may hold values from -3 to 3
Outputs:
- output: bfloat16 [64, 512, 1024], P('dp', 'seq')
- input_grad: bfloat16 [64, 512, 1024], P('dp', 'seq')
- qkv_grad: float32 [1024, 3072], P('dp', 'seq')
- out_grad: float32 [1024, 1024], P('dp', 'seq')
- gate_grad: float32 [1024, 4096], P('dp', 'seq')
- up_grad: float32 [1024, 4096], P('dp', 'seq')
- down_grad: float32 [4096, 1024], P('dp', 'seq')
- gain_grad: float32 [1024, 4], P('dp', 'seq')
- bias_grad: float32 [1024, 2], P('dp', 'seq')
Inputs may be any that keep to these rules, and one draw needn't show every extreme that they name: `lengths`: in the clips of each index of dp (4 clips), one clip, drawn from the seed, has exactly 500 frames.
All inputs are finite; a program needn't handle non-finite values.
Results may differ from a plain program's by a relative error of at most 0.014.
Values may be sent and summed in bfloat16 or wider, within the bound.
No kernel may reach another device: no remote copies, remote signals or barrier semaphores. Data moves between devices by JAX's collectives and lax.ppermute only.
A program may use at most 256 MiB of HBM per device.

v0:
```python
import math

import jax
import jax.numpy as jnp
from jax import lax
from jax.sharding import PartitionSpec as P

HEADS = 16
WINDOW = 128


NORM_EPS = 1e-05
MASKED = -1e30


def norm_forward(values, gain_col, shift_col):
    row_mean = jnp.mean(values, axis=-1, keepdims=True)
    centred = values - row_mean
    inverse = lax.rsqrt(jnp.mean(centred * centred, axis=-1, keepdims=True) + NORM_EPS)
    normal = centred * inverse
    return (normal * gain_col + shift_col, normal, inverse)


def norm_backward(upstream, normal, inverse, gain_col):
    scaled = upstream * gain_col
    inner_term = (
        scaled
        - jnp.mean(scaled, axis=-1, keepdims=True)
        - normal * jnp.mean(scaled * normal, axis=-1, keepdims=True)
    )
    return (inverse * inner_term, jnp.sum(upstream * normal, axis=0), jnp.sum(upstream, axis=0))


def rotary_tables(places, head_dim):
    pair_count = head_dim // 2
    freq_rates = jnp.exp(
        jnp.arange(pair_count).astype(jnp.float32) * (-2.0 * math.log(10000.0) / head_dim)
    )
    angles = places.astype(jnp.float32)[:, None] * freq_rates[None, :]
    return (jnp.cos(angles), jnp.sin(angles))


def rotate(values, cosine, sine_table, direction):
    pair_count = values.shape[-1] // 2
    leading = values[..., :pair_count]
    trailing = values[..., pair_count:]
    cos_wide = cosine[:, None, :]
    sin_wide = sine_table[:, None, :] * direction
    return jnp.concatenate(
        [leading * cos_wide - trailing * sin_wide, trailing * cos_wide + leading * sin_wide],
        axis=-1,
    )


def inner_rows(left_op, right_op):
    return lax.dot_general(
        left_op, right_op, (((0,), (0,)), ((), ())), preferred_element_type=jnp.float32
    )


def times_transposed(left_op, right_op):
    return lax.dot_general(
        left_op, right_op, (((1,), (1,)), ((), ())), preferred_element_type=jnp.float32
    )


def body(
    frames,
    cotangent,
    lengths,
    qkv_weight,
    out_weight,
    gate_weight,
    up_weight,
    down_weight,
    gain_table,
    bias_table,
):
    seq_parts = lax.axis_size("seq")
    seq_index = lax.axis_index("seq")
    model_width = frames.shape[2]
    clip_len = frames.shape[1] * seq_parts
    head_dim = model_width // HEADS
    score_scale = 1.0 / math.sqrt(head_dim)
    frames_here, tangent_here = (frames, cotangent)
    places = seq_index * frames.shape[1] + jnp.arange(frames.shape[1])
    heads_here = HEADS // seq_parts
    groups, row_len = (frames_here.shape[0], frames_here.shape[1])
    row_count = groups * row_len
    width_here = heads_here * head_dim
    valid_rows = (places[None, :] < lengths[:, None]).astype(jnp.float32).reshape(row_count, 1)
    cosine, sine_table = rotary_tables(places, head_dim)
    full_cosine, full_sine = rotary_tables(jnp.arange(clip_len), head_dim)
    source = frames_here.astype(jnp.float32).reshape(row_count, model_width)
    normed_one, normal_one, inverse_one = norm_forward(source, gain_table[:, 0], bias_table[:, 0])
    normed_one = normed_one.astype(jnp.bfloat16)
    mixed_rows = jnp.dot(normed_one, qkv_weight, preferred_element_type=jnp.float32)
    shaped = mixed_rows.reshape(groups, row_len, 3, HEADS, head_dim)
    queries = (
        rotate(shaped[:, :, 0], cosine, sine_table, 1.0)
        .astype(jnp.bfloat16)
        .reshape(groups, row_len, model_width)
    )
    key_rows = (
        rotate(shaped[:, :, 1], cosine, sine_table, 1.0)
        .astype(jnp.bfloat16)
        .reshape(groups, row_len, model_width)
    )
    values = shaped[:, :, 2].astype(jnp.bfloat16).reshape(groups, row_len, model_width)
    head_queries, head_keys, head_values = (
        lax.all_to_all(queries, "seq", split_axis=2, concat_axis=1, tiled=True),
        lax.all_to_all(key_rows, "seq", split_axis=2, concat_axis=1, tiled=True),
        lax.all_to_all(values, "seq", split_axis=2, concat_axis=1, tiled=True),
    )
    head_queries = head_queries.reshape(groups, clip_len, heads_here, head_dim)
    head_keys = head_keys.reshape(groups, clip_len, heads_here, head_dim)
    head_values = head_values.reshape(groups, clip_len, heads_here, head_dim)
    query_pos = jnp.arange(clip_len)[:, None]
    key_pos = jnp.arange(clip_len)[None, :]
    window_mask = (key_pos <= query_pos) & (key_pos > query_pos - WINDOW)

    def clip_scores(clip_queries, clip_keys, length):
        products = jnp.einsum(
            "qhd,khd->hqk", clip_queries, clip_keys, preferred_element_type=jnp.float32
        )
        allowed = window_mask & (key_pos < length)
        return (jnp.where(allowed[None], products * score_scale, MASKED), allowed)

    def attend(block_item):
        clip_queries, clip_keys, clip_values, length = block_item
        scores, allowed = clip_scores(clip_queries, clip_keys, length)
        top_score = jnp.max(scores, axis=-1, keepdims=True)
        exponent = jnp.exp(scores - top_score)
        row_total = jnp.sum(exponent, axis=-1, keepdims=True)
        weights_low = (exponent / row_total).astype(jnp.bfloat16)
        context = jnp.einsum(
            "hqk,khd->qhd", weights_low, clip_values, preferred_element_type=jnp.float32
        )
        return (context.astype(jnp.bfloat16), top_score + jnp.log(row_total))

    context_heads, log_totals = lax.map(attend, (head_queries, head_keys, head_values, lengths))
    context_heads = context_heads.reshape(groups, clip_len, width_here)
    context = lax.all_to_all(context_heads, "seq", split_axis=1, concat_axis=2, tiled=True).reshape(
        row_count, model_width
    )
    attended = jnp.dot(context, out_weight, preferred_element_type=jnp.float32)
    middle = source + gain_table[:, 2] * attended
    normed_two, normal_two, inverse_two = norm_forward(middle, gain_table[:, 1], bias_table[:, 1])
    normed_two = normed_two.astype(jnp.bfloat16)
    gate_rows = jnp.dot(normed_two, gate_weight, preferred_element_type=jnp.float32)
    upward = jnp.dot(normed_two, up_weight, preferred_element_type=jnp.float32)
    sigmoid_gate = jax.nn.sigmoid(gate_rows)
    activated = gate_rows * sigmoid_gate
    hidden = (activated * upward).astype(jnp.bfloat16)
    branch = jnp.dot(hidden, down_weight, preferred_element_type=jnp.float32)
    output = (
        ((middle + gain_table[:, 3] * branch) * valid_rows)
        .astype(jnp.bfloat16)
        .reshape(groups, row_len, model_width)
    )
    output_delta = tangent_here.astype(jnp.float32).reshape(row_count, model_width) * valid_rows
    branch_delta = (output_delta * gain_table[:, 3]).astype(jnp.bfloat16)
    scale_mlp = jnp.sum(output_delta * branch, axis=0)
    down_grad = inner_rows(hidden, branch_delta)
    hidden_delta = times_transposed(branch_delta, down_weight)
    up_delta = (hidden_delta * activated).astype(jnp.bfloat16)
    gate_delta = (
        hidden_delta * upward * sigmoid_gate * (1.0 + gate_rows * (1.0 - sigmoid_gate))
    ).astype(jnp.bfloat16)
    gate_grad = inner_rows(normed_two, gate_delta)
    up_grad = inner_rows(normed_two, up_delta)
    second_delta = times_transposed(gate_delta, gate_weight) + times_transposed(up_delta, up_weight)
    back_two, gain_two, bias_two = norm_backward(
        second_delta, normal_two, inverse_two, gain_table[:, 1]
    )
    middle_delta = output_delta + back_two
    attended_delta = (middle_delta * gain_table[:, 2]).astype(jnp.bfloat16)
    scale_attn = jnp.sum(middle_delta * attended, axis=0)
    out_grad = inner_rows(context, attended_delta)
    context_delta = (
        times_transposed(attended_delta, out_weight)
        .astype(jnp.bfloat16)
        .reshape(groups, row_len, model_width)
    )
    context_heads_delta = lax.all_to_all(
        context_delta, "seq", split_axis=2, concat_axis=1, tiled=True
    )
    context_heads_delta = context_heads_delta.reshape(groups, clip_len, heads_here, head_dim)

    def attend_back(block_item):
        clip_queries, clip_keys, clip_values, length, log_total, clip_delta = block_item
        scores, allowed = clip_scores(clip_queries, clip_keys, length)
        weights = jnp.exp(scores - log_total)
        weights_low = weights.astype(jnp.bfloat16)
        weight_delta = jnp.einsum(
            "qhd,khd->hqk", clip_delta, clip_values, preferred_element_type=jnp.float32
        )
        row_inner = jnp.sum(weight_delta * weights, axis=-1, keepdims=True)
        product_delta = jnp.where(
            allowed[None], weights * (weight_delta - row_inner) * score_scale, 0.0
        ).astype(jnp.bfloat16)
        query_delta = jnp.einsum(
            "hqk,khd->qhd", product_delta, clip_keys, preferred_element_type=jnp.float32
        )
        key_delta = jnp.einsum(
            "hqk,qhd->khd", product_delta, clip_queries, preferred_element_type=jnp.float32
        )
        value_delta = jnp.einsum(
            "hqk,qhd->khd", weights_low, clip_delta, preferred_element_type=jnp.float32
        )
        query_delta = rotate(query_delta, full_cosine, full_sine, -1.0).astype(jnp.bfloat16)
        key_delta = rotate(key_delta, full_cosine, full_sine, -1.0).astype(jnp.bfloat16)
        return (query_delta, key_delta, value_delta.astype(jnp.bfloat16))

    query_delta, key_delta, value_delta = lax.map(
        attend_back,
        (head_queries, head_keys, head_values, lengths, log_totals, context_heads_delta),
    )
    query_delta = query_delta.reshape(groups, clip_len, width_here)
    key_delta = key_delta.reshape(groups, clip_len, width_here)
    value_delta = value_delta.reshape(groups, clip_len, width_here)
    query_back, key_back, value_back = (
        lax.all_to_all(query_delta, "seq", split_axis=1, concat_axis=2, tiled=True),
        lax.all_to_all(key_delta, "seq", split_axis=1, concat_axis=2, tiled=True),
        lax.all_to_all(value_delta, "seq", split_axis=1, concat_axis=2, tiled=True),
    )
    mixed_delta = jnp.concatenate(
        [
            query_back.reshape(row_count, model_width),
            key_back.reshape(row_count, model_width),
            value_back.reshape(row_count, model_width),
        ],
        axis=1,
    )
    qkv_grad = inner_rows(normed_one, mixed_delta)
    first_delta = times_transposed(mixed_delta, qkv_weight)
    back_one, gain_one, bias_one = norm_backward(
        first_delta, normal_one, inverse_one, gain_table[:, 0]
    )
    input_grad = (
        (middle_delta + back_one).astype(jnp.bfloat16).reshape(groups, row_len, model_width)
    )
    gain_grad = jnp.stack([gain_one, gain_two, scale_attn, scale_mlp], axis=1)
    bias_grad = jnp.stack([bias_one, bias_two], axis=1)
    over_clips = (
        lax.psum_scatter(qkv_grad, "dp", scatter_dimension=0, tiled=True),
        lax.psum_scatter(out_grad, "dp", scatter_dimension=0, tiled=True),
        lax.psum_scatter(gate_grad, "dp", scatter_dimension=0, tiled=True),
        lax.psum_scatter(up_grad, "dp", scatter_dimension=0, tiled=True),
        lax.psum_scatter(down_grad, "dp", scatter_dimension=0, tiled=True),
        lax.psum_scatter(gain_grad, "dp", scatter_dimension=0, tiled=True),
        lax.psum_scatter(bias_grad, "dp", scatter_dimension=0, tiled=True),
    )
    summed = (
        lax.psum_scatter(
            over_clips[0].astype(jnp.bfloat16), "seq", scatter_dimension=1, tiled=True
        ).astype(jnp.float32),
        lax.psum_scatter(
            over_clips[1].astype(jnp.bfloat16), "seq", scatter_dimension=1, tiled=True
        ).astype(jnp.float32),
        lax.psum_scatter(
            over_clips[2].astype(jnp.bfloat16), "seq", scatter_dimension=1, tiled=True
        ).astype(jnp.float32),
        lax.psum_scatter(
            over_clips[3].astype(jnp.bfloat16), "seq", scatter_dimension=1, tiled=True
        ).astype(jnp.float32),
        lax.psum_scatter(
            over_clips[4].astype(jnp.bfloat16), "seq", scatter_dimension=1, tiled=True
        ).astype(jnp.float32),
        lax.psum_scatter(
            over_clips[5].astype(jnp.bfloat16), "seq", scatter_dimension=1, tiled=True
        ).astype(jnp.float32),
        lax.psum_scatter(
            over_clips[6].astype(jnp.bfloat16), "seq", scatter_dimension=1, tiled=True
        ).astype(jnp.float32),
    )
    return (
        output,
        input_grad,
        summed[0],
        summed[1],
        summed[2],
        summed[3],
        summed[4],
        summed[5],
        summed[6],
    )


def solution(mesh):
    placed = (
        P("dp", "seq", None),
        P("dp", "seq", None),
        P("dp"),
        P(),
        P(),
        P(),
        P(),
        P(),
        P(),
        P(),
    )
    return jax.shard_map(
        body,
        mesh=mesh,
        in_specs=placed,
        out_specs=(
            P("dp", "seq", None),
            P("dp", "seq", None),
            P("dp", "seq"),
            P("dp", "seq"),
            P("dp", "seq"),
            P("dp", "seq"),
            P("dp", "seq"),
            P("dp", "seq"),
            P("dp", "seq"),
        ),
        check_vma=False,
    )
```

profile of v0, /device:TPU:0, one launch (start us, length us, event | category | flops | bytes accessed | tf_op | source)
XLA Modules:
  0.0 1592.4 jit_solution(18428473840457559963)
XLA Ops:
  8.2 8.6 copy.79
  22.4 11.0 fusion.144
  41.2 4.9 all-to-all-start
  56.0 16.4 %all-to-all-done = bf16[4,256,1024]{1,0,2:T(4,128)(2,1)} async-done(((bf16[4,256,1024]{1,0,2:T(4,128)(2,1)}), bf16[4,256,1024]{1,0,2:T(4,128)(2,1)}, u32[]{:S(2)}, u32[]{:S(2)}) %all-to-all-start) | async-done | bytes 2097184 | tf_op jit(solution)/shard_map/all_to_all | solution.py:113
  72.4 5.0 all-to-all-start.1
  81.8 20.3 %all-to-all-done.1 = bf16[4,256,1024]{1,0,2:T(4,128)(2,1)} async-done(((bf16[4,256,1024]{1,0,2:T(4,128)(2,1)}), bf16[4,256,1024]{1,0,2:T(4,128)(2,1)}, u32[]{:S(2)}, u32[]{:S(2)}) %all-to-all-start.1) | async-done | bytes 2097184 | tf_op jit(solution)/shard_map/all_to_all | solution.py:111
  102.1 4.8 all-to-all-start.2
  107.5 5.1 copy.81
  117.0 5.1 copy.84
  130.7 5.1 copy.86
  141.7 43.0 %while.30 = (s32[]{:T(128)}, bf16[4,512,8,64]{1,3,2,0:T(8,128)(2,1)}, f32[4,8,512,1]{2,1,3,0:T(8,128)}, bf16[4,512,8,64]{1,3,2,0:T(8,128)(2,1)}, s32[4]{0:T(128)...) while((s32[]{:T(128)}, ...), condition=%wide.region_5.6_spmd.clone, body=%wide.region_2.5_spmd.clone.sunk | while | flops 563343872 | bytes 28447864 | solution.py:141
  189.2 5.2 all-to-all-start.3
  198.0 19.2 %all-to-all-done.3 = bf16[4,512,512]{2,0,1:T(4,128)(2,1)} async-done(((bf16[4,512,512]{2,0,1:T(4,128)(2,1)}), bf16[4,512,512]{2,0,1:T(4,128)(2,1)}, u32[]{:S(2)}, u32[]{:S(2)}) %all-to-all-start.3) | async-done | bytes 2097184 | tf_op jit(solution)/shard_map/all_to_all | solution.py:143
  229.3 11.8 fusion.160
  241.2 11.7 fusion.161
  252.8 30.5 %multiply_convert_fusion = (bf16[1024,4096]{1,0:T(8,128)(2,1)}, bf16[1024,4096]{1,0:T(8,128)(2,1)}, bf16[1024,4096]{1,0:T(8,128)(2,1)}) fusion(f32[1024,4096]{1,0:T(8,128)} %fusion.160, f32[1024,4096]{1,0:T(8,128)} %fusion.161, bf16[1024,1024]{1,0:T(8,128)(2,1)} %fusion.122, bf16[4096,1024]{1,0:T(8,128)(2,1)} %param.21), kind=kOutput, calls=%fused_computation.105 | convolution fusion | flops 8652849152 | bytes 69206016 | tf_op jit(solution)/shard_map/dot_general | solution.py:62
  283.4 13.0 fusion.162
  296.4 16.9 %multiply_reduce_fusion.2 = (f32[1024]{0:T(1024)}, f32[1024]{0:T(1024)S(1)}, f32[1024]{0:T(1024)S(1)}, f32[1024]{0:T(1024)}, f32[1024,1024]{1,0:T(8,128)}) fusion(f32[1024,1024]{1,0:T(8,128)S(1)} %copy-done.6, f32[1024]{0:T(1024)S(1)} %add_rsqrt_fusion, f32[1024]{0:T(1024)S(1)} %broadcast_multiply_fusion.4, f32[1024]{0:T(1024)S(1)} %bitcast.291, ...), kind=kOutput, calls=%fused_computation.143 | convolution fusion | flops 8600416256 | bytes 29388800 | tf_op jit(solution)/shard_map/dot_general | solution.py:62
  313.3 18.5 %fusion.123 = (f32[1024]{0:T(1024)}, bf16[1024,1024]{1,0:T(8,128)(2,1)}, f32[1024]{0:T(1024)}, f32[1024,1024]{1,0:T(8,128)S(1)}) fusion(bf16[4,256,1024]{2,1,0:T(8,128)(2,1)S(1)} %copy-done.14, f32[1024]{0:T(1024)S(1)} %bitcast.294, f32[1024,1024]{1,0:T(8,128)S(1)} %copy-done.6, f32[1024]{0:T(1024)S(1)} %bitcast.296, f32[1024,1024]{1,0:T(8,128)} %get-tuple-element.384, ...), kind=kOutput, calls=%fused_computation.118 | convolution fusion | flops 8608806912 | bytes 37785600 | tf_op jit(solution)/shard_map/dot_general | solution.py:155
  338.7 24.3 %all_to_all.120 = bf16[4,256,1024]{1,0,2:T(4,128)(2,1)S(1)} all-to-all(bf16[4,256,1024]{1,0,2:T(4,128)(2,1)S(1)} %copy.90), channel_id=1, replica_groups=mesh['dp'=16,'seq'=2] {'seq'}, dimensions={2} | all-to-all | bytes 4194304 | tf_op jit(solution)/shard_map/all_to_all | solution.py:185
  374.5 212.2 %while.31 = (s32[]{:T(128)}, bf16[4,512,8,64]{1,3,2,0:T(8,128)(2,1)}, bf16[4,512,8,64]{1,3,2,0:T(8,128)(2,1)}, bf16[4,512,8,64]{1,3,2,0:T(8,128)(2,1)}, bf16[4,5...) while((s32[]{:T(128)}, ...), condition=%wide.region_12.13_spmd.clone.clone.clone, body=%wide.region_10.12_spmd.clone.clone.clone.sunk | while | flops 1406445056 | bytes 122561496 | solution.py:215
  374.7 6.0 fusion.231
  380.7 5.7 fusion.232
  389.3 16.5 %fusion.234 = f32[512,8,64]{0,2,1:T(8,128)S(1)} fusion(f32[8,512,512]{1,2,0:T(8,128)} %fusion.231, f32[8,512,512]{1,2,0:T(8,128)} %fusion.232, f32[8,512]{1,0:T(8,128)S(1)} %dynamic-slice_bitcast_fusion.2, pred[512,512]{0,1:T(8,128)(4,1)S(1)} %fusion.233, bf16[4,512,8,64]{1,3,2,0:T(8,128)(2,1)} %get-tuple-element.600, s32[]{:T(128)S(6)} %copy.136), kind=kOutput, calls=%fused_computation.55.clone.1 | convolution fusion | flops 293605888 | bytes 35684356 | tf_op jit(solution)/shard_map/while/body/eval_jaxpr/hqk,qhd->khd/dot_general | solution.py:205
  406.1 13.4 fusion.235
  421.1 6.6 fusion.237
  427.8 6.0 fusion.231
  433.7 5.7 fusion.232
  442.3 16.5 %fusion.234 = f32[512,8,64]{0,2,1:T(8,128)S(1)} fusion(f32[8,512,512]{1,2,0:T(8,128)} %fusion.231, f32[8,512,512]{1,2,0:T(8,128)} %fusion.232, f32[8,512]{1,0:T(8,128)S(1)} %dynamic-slice_bitcast_fusion.2, pred[512,512]{0,1:T(8,128)(4,1)S(1)} %fusion.233, bf16[4,512,8,64]{1,3,2,0:T(8,128)(2,1)} %get-tuple-element.600, s32[]{:T(128)S(6)} %copy.136), kind=kOutput, calls=%fused_computation.55.clone.1 | convolution fusion | flops 293605888 | bytes 35684356 | tf_op jit(solution)/shard_map/while/body/eval_jaxpr/hqk,qhd->khd/dot_general | solution.py:205
  459.2 13.4 fusion.235
  474.0 6.6 fusion.237
  480.7 6.0 fusion.231
  486.7 5.7 fusion.232
  495.3 16.6 %fusion.234 = f32[512,8,64]{0,2,1:T(8,128)S(1)} fusion(f32[8,512,512]{1,2,0:T(8,128)} %fusion.231, f32[8,512,512]{1,2,0:T(8,128)} %fusion.232, f32[8,512]{1,0:T(8,128)S(1)} %dynamic-slice_bitcast_fusion.2, pred[512,512]{0,1:T(8,128)(4,1)S(1)} %fusion.233, bf16[4,512,8,64]{1,3,2,0:T(8,128)(2,1)} %get-tuple-element.600, s32[]{:T(128)S(6)} %copy.136), kind=kOutput, calls=%fused_computation.55.clone.1 | convolution fusion | flops 293605888 | bytes 35684356 | tf_op jit(solution)/shard_map/while/body/eval_jaxpr/hqk,qhd->khd/dot_general | solution.py:205
  512.2 13.4 fusion.235
  527.0 6.6 fusion.237
  533.7 6.0 fusion.231
  539.7 5.7 fusion.232
  548.3 16.6 %fusion.234 = f32[512,8,64]{0,2,1:T(8,128)S(1)} fusion(f32[8,512,512]{1,2,0:T(8,128)} %fusion.231, f32[8,512,512]{1,2,0:T(8,128)} %fusion.232, f32[8,512]{1,0:T(8,128)S(1)} %dynamic-slice_bitcast_fusion.2, pred[512,512]{0,1:T(8,128)(4,1)S(1)} %fusion.233, bf16[4,512,8,64]{1,3,2,0:T(8,128)(2,1)} %get-tuple-element.600, s32[]{:T(128)S(6)} %copy.136), kind=kOutput, calls=%fused_computation.55.clone.1 | convolution fusion | flops 293605888 | bytes 35684356 | tf_op jit(solution)/shard_map/while/body/eval_jaxpr/hqk,qhd->khd/dot_general | solution.py:205
  565.2 13.4 fusion.235
  580.0 6.6 fusion.237
  599.6 16.3 %all-to-all-done.5 = bf16[4,512,512]{2,0,1:T(4,128)(2,1)S(1)} async-done(((bf16[4,512,512]{2,0,1:T(4,128)(2,1)}), bf16[4,512,512]{2,0,1:T(4,128)(2,1)S(1)}, u32[]{:S(2)}, u32[]{:S(2)}) %all-to-all-start.5) | async-done | bytes 2097184 | tf_op jit(solution)/shard_map/all_to_all | solution.py:223
  615.9 4.9 all-to-all-start.6
  621.1 7.2 fusion.150
  632.8 8.0 all-to-all-done.6
  640.8 4.9 all-to-all-start.7
  655.0 9.8 all-to-all-done.7
  672.3 9.7 fusion.142
  682.0 9.2 fusion.163
  692.8 14.6 fusion.164
  707.5 15.6 fusion.165
  725.0 15.8 fusion.166
  745.5 94.1 %reduce-scatter.17.cloned.1.call-done = f32[64,3072]{1,0:T(8,128)} async-done(((f32[1024,3072]{1,0:T(8,128)}), f32[64,3072]{1,0:T(8,128)}) %reduce-scatter.17.cloned.1.call-update) | async-done | bytes 786448 | tf_op jit(solution)/shard_map/reduce_scatter | solution.py:246
  841.6 180.4 %reduce-scatter.25.cloned.1.call-done = f32[64,4096]{1,0:T(8,128)} async-done(((f32[1024,4096]{1,0:T(8,128)}), f32[64,4096]{1,0:T(8,128)}) %reduce-scatter.25.cloned.1.call-update) | async-done | bytes 1048592 | tf_op jit(solution)/shard_map/reduce_scatter | solution.py:248
  1024.1 180.0 %reduce-scatter.29.cloned.1.call-done = f32[64,4096]{1,0:T(8,128)} async-done(((f32[1024,4096]{1,0:T(8,128)}), f32[64,4096]{1,0:T(8,128)}) %reduce-scatter.29.cloned.1.call-update) | async-done | bytes 1048592 | tf_op jit(solution)/shard_map/reduce_scatter | solution.py:249
  1207.5 178.7 %reduce-scatter.33.cloned.1.call-done = f32[256,1024]{1,0:T(8,128)} async-done(((f32[4096,1024]{1,0:T(8,128)}), f32[256,1024]{1,0:T(8,128)}) %reduce-scatter.33.cloned.1.call-update) | async-done | bytes 1048592 | tf_op jit(solution)/shard_map/reduce_scatter | solution.py:250
  1388.4 6.0 fusion.139
  1394.4 50.5 %reduce-scatter.39.cloned.1.call-done = f32[64,2]{1,0:T(8,128)} async-done(((f32[1024,2]{1,0:T(8,128)}), f32[64,2]{1,0:T(8,128)}) %reduce-scatter.39.cloned.1.call-update) | async-done | bytes 528
  1445.7 58.2 %reduce-scatter.37.cloned.1.call-done = f32[64,4]{1,0:T(8,128)} async-done(((f32[1024,4]{1,0:T(8,128)}), f32[64,4]{1,0:T(8,128)}) %reduce-scatter.37.cloned.1.call-update) | async-done | bytes 1040
  1504.7 4.9 all-reduce.2
  1517.5 14.6 reduce-scatter.19.cloned.1.call-done
  1533.8 15.6 reduce-scatter.27.cloned.1.call-done
  1551.1 15.7 reduce-scatter.31.cloned.1.call-done
  1568.6 14.9 reduce-scatter.35.cloned.1.call-done
  (293 shorter events, 215.7 us)
Async XLA Ops:
  7.2 214.8 %copy-start = (bf16[1024,1024]{1,0:T(8,128)(2,1)S(1)}, bf16[1024,1024]{1,0:T(8,128)(2,1)}, u32[]{:S(2)}) copy-start(bf16[1024,1024]{1,0:T(8,128)(2,1)} %param.18) | copy-start | bytes 6291460
  8.1 14.3 copy-start.25
  8.1 213.8 %copy-start.33 = (f32[1024,1]{0,1:T(1,128)}, f32[1024,1]{0,1:T(1,128)S(1)}, u32[]{:S(2)}) copy-start(f32[1024,1]{0,1:T(1,128)S(1)} %get-tuple-element.374) | copy-start | bytes 12292
  8.2 8.7 copy-start.29
  16.8 5.6 copy-start.2
  16.8 16.6 %copy-start.30 = (f32[1024,1]{0,1:T(1,128)}, f32[1024,1]{0,1:T(1,128)S(1)}, u32[]{:S(2)}) copy-start(f32[1024,1]{0,1:T(1,128)S(1)} %get-tuple-element.377) | copy-start | bytes 12292
  33.4 4.5 copy-start.9
  41.2 31.2 %all-to-all-start = ((bf16[4,256,1024]{1,0,2:T(4,128)(2,1)}), bf16[4,256,1024]{1,0,2:T(4,128)(2,1)}, u32[]{:S(2)}, u32[]{:S(2)}) async-start(bf16[4,256,1024]{1,0,2:T(4,128)(2,1)} %copy.80), calls=%async_computation | async-start | bytes 4194304 | tf_op jit(solution)/shard_map/all_to_all | solution.py:113
  72.4 29.7 %all-to-all-start.1 = ((bf16[4,256,1024]{1,0,2:T(4,128)(2,1)}), bf16[4,256,1024]{1,0,2:T(4,128)(2,1)}, u32[]{:S(2)}, u32[]{:S(2)}) async-start(bf16[4,256,1024]{1,0,2:T(4,128)(2,1)} %copy.83), calls=%async_computation.1 | async-start | bytes 4194304 | tf_op jit(solution)/shard_map/all_to_all | solution.py:111
  102.1 28.5 %all-to-all-start.2 = ((bf16[4,256,1024]{1,0,2:T(4,128)(2,1)}), bf16[4,256,1024]{1,0,2:T(4,128)(2,1)}, u32[]{:S(2)}, u32[]{:S(2)}) async-start(bf16[4,256,1024]{1,0,2:T(4,128)(2,1)} %copy.85), calls=%async_computation.2 | async-start | bytes 4194304 | tf_op jit(solution)/shard_map/all_to_all | solution.py:112
  135.7 6.0 copy-start.39
  189.2 28.0 %all-to-all-start.3 = ((bf16[4,512,512]{2,0,1:T(4,128)(2,1)}), bf16[4,512,512]{2,0,1:T(4,128)(2,1)}, u32[]{:S(2)}, u32[]{:S(2)}) async-start(bf16[4,512,512]{2,0,1:T(4,128)(2,1)} %copy.87), calls=%async_computation.3 | async-start | bytes 4194304 | tf_op jit(solution)/shard_map/all_to_all | solution.py:143
  219.2 10.1 slice-start.2
  222.0 4.6 copy-start.16
  222.0 7.3 slice-start.3
  228.6 12.6 slice-start.4
  229.3 11.8 copy-start.12
  229.3 11.8 slice-start.5
  283.4 13.0 copy-start.6
  296.4 17.0 %copy-start.14 = (bf16[4,256,1024]{2,1,0:T(8,128)(2,1)S(1)}, bf16[4,256,1024]{2,1,0:T(8,128)(2,1)}, u32[]{:S(2)}) copy-start(bf16[4,256,1024]{2,1,0:T(8,128)(2,1)} %param.15) | copy-start | bytes 6291460
  313.3 18.5 %copy-start.34 = (f32[1024,1]{0,1:T(1,128)S(1)}, f32[1024,1]{0,1:T(1,128)}, u32[]{:S(2)}) copy-start(f32[1024,1]{0,1:T(1,128)} %copy-done.33) | copy-start | bytes 12292
  369.7 4.8 copy-start.18
  369.7 4.8 copy-start.20
  369.7 4.8 copy-start.23
  374.7 6.0 copy-start.7
  421.1 6.7 copy-start.8
  421.1 6.7 copy-start.19
  421.1 6.7 copy-start.21
  421.1 6.7 copy-start.24
  427.7 6.0 copy-start.7
  474.0 6.6 copy-start.8
  474.0 6.6 copy-start.19
  474.0 6.6 copy-start.21
  474.0 6.7 copy-start.24
  480.7 6.0 copy-start.7
  527.0 6.6 copy-start.8
  527.0 6.6 copy-start.19
  527.0 6.6 copy-start.21
  527.0 6.6 copy-start.24
  533.7 6.0 copy-start.7
  580.0 6.7 copy-start.8
  580.0 6.7 copy-start.19
  580.0 6.7 copy-start.21
  580.0 6.7 copy-start.24
  591.3 24.6 %all-to-all-start.5 = ((bf16[4,512,512]{2,0,1:T(4,128)(2,1)}), bf16[4,512,512]{2,0,1:T(4,128)(2,1)S(1)}, u32[]{:S(2)}, u32[]{:S(2)}) async-start(bf16[4,512,512]{2,0,1:T(4,128)(2,1)} %copy.92), calls=%async_computation.5 | async-start | bytes 4194304 | tf_op jit(solution)/shard_map/all_to_all | solution.py:223
  595.1 26.0 %copy-start.35 = (f32[1024,1]{0,1:T(1,128)S(1)}, f32[1024,1]{0,1:T(1,128)}, u32[]{:S(2)}) copy-start(f32[1024,1]{0,1:T(1,128)} %copy-done.33) | copy-start | bytes 12292
  615.9 24.9 %all-to-all-start.6 = ((bf16[4,512,512]{2,0,1:T(4,128)(2,1)}), bf16[4,512,512]{2,0,1:T(4,128)(2,1)}, u32[]{:S(2)}, u32[]{:S(2)}) async-start(bf16[4,512,512]{2,0,1:T(4,128)(2,1)} %copy.95), calls=%async_computation.6 | async-start | bytes 4194304 | tf_op jit(solution)/shard_map/all_to_all | solution.py:224
  620.8 123.0 %reduce-scatter.21.cloned.1.call-start = ((), (), s32[]{:S(2)}) async-start(), calls=%async_computation.22 | async-start | bytes 4456448 | tf_op jit(solution)/shard_map/reduce_scatter | solution.py:247
  628.3 17.5 %copy-start.27 = (f32[1,2,4,128]{3,2,1,0:T(4,128)S(1)}, f32[1,2,4,128]{3,2,1,0:T(4,128)}, u32[]{:S(2)}) copy-start(f32[1,2,4,128]{3,2,1,0:T(4,128)} %get-tuple-element.380) | copy-start | bytes 12292
  628.3 17.5 %copy-start.28 = (f32[1,2,4,128]{3,2,1,0:T(4,128)S(1)}, f32[1,2,4,128]{3,2,1,0:T(4,128)}, u32[]{:S(2)}) copy-start(f32[1,2,4,128]{3,2,1,0:T(4,128)} %get-tuple-element.378) | copy-start | bytes 12292
  640.8 24.0 %all-to-all-start.7 = ((bf16[4,512,512]{2,0,1:T(4,128)(2,1)}), bf16[4,512,512]{2,0,1:T(4,128)(2,1)}, u32[]{:S(2)}, u32[]{:S(2)}) async-start(bf16[4,512,512]{2,0,1:T(4,128)(2,1)} %copy.98), calls=%async_computation.7 | async-start | bytes 4194304 | tf_op jit(solution)/shard_map/all_to_all | solution.py:225
  645.7 193.9 %reduce-scatter.17.cloned.1.call-start = ((), (), s32[]{:S(2)}) async-start(), calls=%async_computation.20 | async-start | bytes 13369344 | tf_op jit(solution)/shard_map/reduce_scatter | solution.py:246
  691.2 330.8 %reduce-scatter.25.cloned.1.call-start = ((), (), s32[]{:S(2)}) async-start(), calls=%async_computation.24 | async-start | bytes 17825792 | tf_op jit(solution)/shard_map/reduce_scatter | solution.py:248
  707.4 496.7 %reduce-scatter.29.cloned.1.call-start = ((), (), s32[]{:S(2)}) async-start(), calls=%async_computation.26 | async-start | bytes 17825792 | tf_op jit(solution)/shard_map/reduce_scatter | solution.py:249
  723.2 663.1 %reduce-scatter.33.cloned.1.call-start = ((), (), s32[]{:S(2)}) async-start(), calls=%async_computation.28 | async-start | bytes 17825792 | tf_op jit(solution)/shard_map/reduce_scatter | solution.py:250
  740.9 704.0 %reduce-scatter.39.cloned.1.call-start = ((), (), s32[]{:S(2)}) async-start(), calls=%async_computation.31 | async-start | bytes 557056
  741.5 464.7 %copy-start.40 = (u32[32]{0:T(128)S(1)}, u32[32]{0:T(128)}, u32[]{:S(2)}) copy-start(u32[32]{0:T(128)} %constant.80) | copy-start | bytes 388
  742.6 761.3 %reduce-scatter.37.cloned.1.call-start = ((), (), s32[]{:S(2)}) async-start(), calls=%async_computation.30 | async-start | bytes 557056
  743.8 772.3 %reduce-scatter.23.cloned.1.call-start = ((), (), s32[]{:S(2)}) async-start(), calls=%async_computation.23 | async-start | bytes 196608 | tf_op jit(solution)/shard_map/reduce_scatter | solution.py:258
  745.5 786.6 %reduce-scatter.19.cloned.1.call-start = ((), (), s32[]{:S(2)}) async-start(), calls=%async_computation.21 | async-start | bytes 589824 | tf_op jit(solution)/shard_map/reduce_scatter | solution.py:255
  841.6 707.8 %reduce-scatter.27.cloned.1.call-start = ((), (), s32[]{:S(2)}) async-start(), calls=%async_computation.25 | async-start | bytes 786432 | tf_op jit(solution)/shard_map/reduce_scatter | solution.py:261
  1024.1 542.8 %reduce-scatter.31.cloned.1.call-start = ((), (), s32[]{:S(2)}) async-start(), calls=%async_computation.27 | async-start | bytes 786432 | tf_op jit(solution)/shard_map/reduce_scatter | solution.py:264
  1206.2 377.3 %reduce-scatter.35.cloned.1.call-start = ((), (), s32[]{:S(2)}) async-start(), calls=%async_computation.29 | async-start | bytes 786432 | tf_op jit(solution)/shard_map/reduce_scatter | solution.py:267
  1388.4 196.9 %copy-start.1 = (bf16[1024,1024]{1,0:T(8,128)(2,1)S(1)}, bf16[1024,1024]{1,0:T(8,128)(2,1)}, u32[]{:S(2)}) copy-start(bf16[1024,1024]{1,0:T(8,128)(2,1)} %param.18) | copy-start | bytes 6291460
  (17 other events, 39.7 us)
Sparse Core Ops, SparseCore 0:
  628.4 72.7 reduce-scatter.20
  705.8 133.7 reduce-scatter.16
  844.3 177.6 reduce-scatter.24
  1026.5 177.5 reduce-scatter.28
  1208.6 177.5 reduce-scatter.32
  1390.1 54.7 reduce-scatter.38
  1449.0 54.8 reduce-scatter.36
  1506.8 9.2 reduce-scatter.22
  1518.9 13.1 reduce-scatter.18
  1534.7 14.5 reduce-scatter.26
  1552.3 14.5 reduce-scatter.30
  1569.0 14.5 reduce-scatter.34
where the time goes:
time: 1610 us; the launch traced here: 1590 us
  waiting for transfers between devices  902 us (56%)
  matrix products  415 us (26%)
  local copies, waits for them, and re-layouts  131 us (8%)
  other arithmetic  64.6 us (4%)
  starting transfers between devices  34.2 us (2%)
  blocking collectives  29.3 us (2%)
    reduce_scatter x1, waiting for transfers between devices, body(): lax.psum_scatter(gate_grad, 'dp', scatter_dimension=0, tiled=True)  180 us
    reduce_scatter x1, waiting for transfers between devices, body(): lax.psum_scatter(up_grad, 'dp', scatter_dimension=0, tiled=True)  180 us
    reduce_scatter x1, waiting for transfers between devices, body(): lax.psum_scatter(down_grad, 'dp', scatter_dimension=0, tiled=True)  179 us
    unnamed x14, waiting for transfers between devices  109 us
    reduce_scatter x1, waiting for transfers between devices, body(): lax.psum_scatter(qkv_grad, 'dp', scatter_dimension=0, tiled=True)  94.1 us
    dot_general x5, matrix products, times_transposed(): lax.dot_general(left_op, right_op, (((1,), (1,)), ((), ())), preferred_el...  73.9 us
    dot_general x4, matrix products, attend_back(): jnp.einsum('hqk,qhd->khd', product_delta, clip_queries, preferred_element...  66.3 us
    dot_general x5, matrix products, inner_rows(): lax.dot_general(left_op, right_op, (((0,), (0,)), ((), ())), preferred_el...  62.5 us
  transfers between devices with their start and end apart: 19, of which 18 were waited for; matrix products, arithmetic and copies ran while one was open for 10% of the time, Pallas kernels for 0%

commit v1 on v0

--- a/solution.py
+++ b/solution.py
@@ -1,8 +1,13 @@
+import functools
 import math
 
 import jax
 import jax.numpy as jnp
+import numpy as np
 from jax import lax
+from jax.experimental import pallas as pl
+from jax.experimental.pallas import tpu as pltpu
+from jax.sharding import Mesh
 from jax.sharding import PartitionSpec as P
 
 HEADS = 16
@@ -287,33 +292,829 @@
     )
 
 
+BF = jnp.bfloat16
+F32 = jnp.float32
+TILE = 128
+MIB = 1024 * 1024
+
+
+def mm(left, right):
+    return lax.dot_general(left, right, (((1,), (0,)), ((), ())), preferred_element_type=F32)
+
+
+def mm_t(left, right):
+    return lax.dot_general(left, right, (((1,), (1,)), ((), ())), preferred_element_type=F32)
+
+
+def t_mm(left, right):
+    return lax.dot_general(left, right, (((0,), (0,)), ((), ())), preferred_element_type=F32)
+
+
+def call_kernel(
+    kernel, info, args, *, name, grid, ins, outs, shapes, scratch=(), vmem=48, cost=None, after=()
+):
+    flops, moved = cost
+    count, unread = len(args), len(after)
+
+    def run(info, *refs):
+        kernel(info, *refs[:count], *refs[count + unread :])
+
+    args = [*args, *after]
+    ins = [*ins] + [pl.BlockSpec(memory_space=pl.ANY)] * unread
+    return pl.pallas_call(
+        run,
+        grid_spec=pltpu.PrefetchScalarGridSpec(
+            num_scalar_prefetch=1, grid=grid, in_specs=ins, out_specs=outs, scratch_shapes=scratch
+        ),
+        out_shape=shapes,
+        compiler_params=pltpu.CompilerParams(
+            dimension_semantics=("arbitrary",) * len(grid), vmem_limit_bytes=vmem * MIB
+        ),
+        cost_estimate=pl.CostEstimate(flops=int(flops), bytes_accessed=int(moved), transcendentals=0),
+        name=name,
+    )(info, *args)
+
+
+def shape_of(shape, dtype=BF):
+    return jax.ShapeDtypeStruct(shape, dtype)
+
+
+def rows_spec(rows, width, column=0):
+    return pl.BlockSpec((rows, width), lambda r, info: (r, column))
+
+
+def whole_spec(shape):
+    return pl.BlockSpec(shape, lambda r, info: (0,) * len(shape))
+
+
+LEN0 = 5
+
+
+def norm_stats(values):
+    row_mean = jnp.mean(values, axis=-1, keepdims=True)
+    centred = values - row_mean
+    inverse = lax.rsqrt(jnp.mean(centred * centred, axis=-1, keepdims=True) + NORM_EPS)
+    return centred * inverse, inverse
+
+
+def norm_back(upstream, normal, inverse, gain):
+    scaled = upstream * gain
+    return inverse * (
+        scaled
+        - jnp.mean(scaled, axis=-1, keepdims=True)
+        - normal * jnp.mean(scaled * normal, axis=-1, keepdims=True)
+    )
+
+
+def turn(values, cosine, sine_a, sine_b):
+    return (
+        values * cosine
+        + pltpu.roll(values, TILE - 32, 1) * sine_a
+        + pltpu.roll(values, 32, 1) * sine_b
+    )
+
+
+def column_sum(values):
+    return jnp.sum(values, axis=0, keepdims=True)
+
+
+def qkv_kernel(info, x_ref, w_ref, gb_ref, tab_ref, qkv_ref, n_ref):
+    r = pl.program_id(0)
+    live = info[3] < info[LEN0 + r]
+
+    @pl.when(live)
+    def _():
+        normal, _ = norm_stats(x_ref[...].astype(F32))
+        normed = (normal * gb_ref[0:1, :] + gb_ref[4:5, :]).astype(BF)
+        n_ref[...] = normed
+        width = normed.shape[1]
+        cosine, sine_a, sine_b = tab_ref[0], tab_ref[1], tab_ref[2]
+        for part in range(3):
+            mixed = mm(normed, w_ref[:, part * width : (part + 1) * width])
+            for t in range(width // TILE):
+                piece = mixed[:, t * TILE : (t + 1) * TILE]
+                if part < 2:
+                    piece = turn(piece, cosine, sine_a, sine_b)
+                at = part * width + t * TILE
+                qkv_ref[:, at : at + TILE] = piece.astype(BF)
+
+    @pl.when(jnp.logical_not(live))
+    def _():
+        qkv_ref[...] = jnp.zeros_like(qkv_ref)
+        n_ref[...] = jnp.zeros_like(n_ref)
+
+
+def halo_kernel(info, x_ref, wk_ref, wv_ref, gb_ref, tab_ref, kv_ref, n_ref):
+    r = pl.program_id(0)
+    live = jnp.logical_and(info[0] > 0, info[3] < info[LEN0 + r])
+
+    @pl.when(live)
+    def _():
+        normal, _ = norm_stats(x_ref[...].astype(F32))
+        normed = (normal * gb_ref[0:1, :] + gb_ref[4:5, :]).astype(BF)
+        n_ref[...] = normed
+        width = normed.shape[1]
+        keys = mm(normed, wk_ref[...])
+        for t in range(width // TILE):
+            piece = keys[:, t * TILE : (t + 1) * TILE]
+            kv_ref[:, t * TILE : (t + 1) * TILE] = turn(
+                piece, tab_ref[0], tab_ref[1], tab_ref[2]
+            ).astype(BF)
+        kv_ref[:, width:] = mm(normed, wv_ref[...]).astype(BF)
+
+    @pl.when(jnp.logical_not(live))
+    def _():
+        kv_ref[...] = jnp.zeros_like(kv_ref)
+        n_ref[...] = jnp.zeros_like(n_ref)
+
+
+def window_bias(info, clip, block):
+    i = lax.broadcasted_iota(jnp.int32, (2 * TILE, 2 * TILE), 0) % TILE
+    j = lax.broadcasted_iota(jnp.int32, (2 * TILE, 2 * TILE), 1)
+    key = info[3] + (block - 1) * TILE + j
+    allowed = (j > i) & (j <= i + TILE) & (key >= 0) & (key < info[LEN0 + clip])
+    return jnp.where(allowed, 0.0, MASKED)
+
+
+def two_heads(values):
+    lane = lax.broadcasted_iota(jnp.int32, values.shape, 1)
+    nought = jnp.zeros_like(values)
+    return jnp.concatenate(
+        [jnp.where(lane < 64, values, nought), jnp.where(lane < 64, nought, values)], axis=0
+    )
+
+
+def one_row(values):
+    lane = lax.broadcasted_iota(jnp.int32, (TILE, TILE), 1)
+    return jnp.where(lane < 64, values[:TILE], values[TILE:])
+
+
+def key_window(halo_ref, own_ref, block, at, own_at):
+    if block == 0:
+        return jnp.concatenate(
+            [halo_ref[:, at : at + TILE], own_ref[0:TILE, own_at : own_at + TILE]], axis=0
+        )
+    return own_ref[(block - 1) * TILE : (block + 1) * TILE, own_at : own_at + TILE]
+
+
+def attend_kernel(scale, info, qkv_ref, kvh_ref, ctx_ref, lse_ref):
+    clip = pl.program_id(0)
+    rows, width = ctx_ref.shape
+    for block in range(rows // TILE):
+        live = info[3] + block * TILE < info[LEN0 + clip]
+        at_rows = slice(block * TILE, (block + 1) * TILE)
+
+        @pl.when(live)
+        def _():
+            bias = window_bias(info, clip, block)
+            lane = lax.broadcasted_iota(jnp.int32, (TILE, TILE), 1)
+            totals = jnp.zeros((TILE, TILE), F32)
+            for pair in range(width // TILE):
+                at = pair * TILE
+                queries = two_heads(qkv_ref[at_rows, at : at + TILE])
+                keys = key_window(kvh_ref, qkv_ref, block, at, width + at)
+                values = key_window(kvh_ref, qkv_ref, block, width + at, 2 * width + at)
+                scores = mm_t(queries, keys) * scale + bias
+                top = jnp.max(scores, axis=1, keepdims=True)
+                exponent = jnp.exp(scores - top)
+                total = jnp.sum(exponent, axis=1, keepdims=True)
+                weights = (exponent * (1.0 / total)).astype(BF)
+                ctx_ref[at_rows, at : at + TILE] = one_row(mm(weights, values)).astype(BF)
+                log_total = top + jnp.log(total)
+                totals = jnp.where(lane == 2 * pair, log_total[:TILE], totals)
+                totals = jnp.where(lane == 2 * pair + 1, log_total[TILE:], totals)
+            lse_ref[at_rows, :] = totals
+
+        @pl.when(jnp.logical_not(live))
+        def _():
+            ctx_ref[at_rows, :] = jnp.zeros((TILE, width), BF)
+            lse_ref[at_rows, :] = jnp.zeros((TILE, TILE), F32)
+
+
+def attend_back_kernel(
+    scale, info, qkv_ref, kvh_ref, dctx_ref, lse_ref, tab_ref, tabh_ref, md_ref, mdh_ref, dk_acc, dv_acc
+):
+    clip = pl.program_id(0)
+    rows, width = dctx_ref.shape
+    blocks = rows // TILE
+    first_live = info[3] < info[LEN0 + clip]
+
+    @pl.when(jnp.logical_not(first_live))
+    def _():
+        md_ref[...] = jnp.zeros_like(md_ref)
+        mdh_ref[...] = jnp.zeros_like(mdh_ref)
+
+    @pl.when(first_live)
+    def _():
+        dk_acc[...] = jnp.zeros_like(dk_acc)
+        dv_acc[...] = jnp.zeros_like(dv_acc)
+        for block in range(blocks):
+            at_rows = slice(block * TILE, (block + 1) * TILE)
+            key_rows = slice(block * TILE, (block + 2) * TILE)
+            live = info[3] + block * TILE < info[LEN0 + clip]
+
+            @pl.when(live)
+            def _():
+                bias = window_bias(info, clip, block)
+                for pair in range(width // TILE):
+                    at = pair * TILE
+                    queries = two_heads(qkv_ref[at_rows, at : at + TILE])
+                    delta = two_heads(dctx_ref[at_rows, at : at + TILE])
+                    keys = key_window(kvh_ref, qkv_ref, block, at, width + at)
+                    values = key_window(kvh_ref, qkv_ref, block, width + at, 2 * width + at)
+                    log_total = jnp.concatenate(
+                        [
+                            lse_ref[at_rows, 2 * pair : 2 * pair + 1],
+                            lse_ref[at_rows, 2 * pair + 1 : 2 * pair + 2],
+                        ],
+                        axis=0,
+                    )
+                    weights = jnp.exp(mm_t(queries, keys) * scale + bias - log_total)
+                    weight_delta = mm_t(delta, values)
+                    inner = jnp.sum(weight_delta * weights, axis=1, keepdims=True)
+                    product_delta = (weights * (weight_delta - inner) * scale).astype(BF)
+                    query_delta = one_row(mm(product_delta, keys))
+                    md_ref[at_rows, at : at + TILE] = turn(
+                        query_delta, tab_ref[0, at_rows], -tab_ref[1, at_rows], -tab_ref[2, at_rows]
+                    ).astype(BF)
+                    dk_acc[key_rows, at : at + TILE] += t_mm(product_delta, queries)
+                    dv_acc[key_rows, at : at + TILE] += t_mm(weights.astype(BF), delta)
+
+            @pl.when(jnp.logical_not(live))
+            def _():
+                md_ref[at_rows, 0:width] = jnp.zeros((TILE, width), BF)
+
+        for pair in range(width // TILE):
+            at = pair * TILE
+            mdh_ref[:, at : at + TILE] = turn(
+                dk_acc[:TILE, at : at + TILE], tabh_ref[0], -tabh_ref[1], -tabh_ref[2]
+            ).astype(BF)
+            md_ref[:, width + at : width + at + TILE] = turn(
+                dk_acc[TILE:, at : at + TILE], tab_ref[0], -tab_ref[1], -tab_ref[2]
+            ).astype(BF)
+        mdh_ref[:, width:] = dv_acc[0:TILE, :].astype(BF)
+        md_ref[:, 2 * width :] = dv_acc[TILE:, :].astype(BF)
+
+
+def out_kernel(info, ctx_ref, x_ref, w_ref, gb_ref, att_ref, n_ref):
+    r = pl.program_id(0)
+    live = info[3] < info[LEN0 + r]
+
+    @pl.when(live)
+    def _():
+        attended = mm(ctx_ref[...], w_ref[...])
+        att_ref[...] = attended
+        middle = x_ref[...].astype(F32) + gb_ref[2:3, :] * attended
+        normal, _ = norm_stats(middle)
+        n_ref[...] = (normal * gb_ref[1:2, :] + gb_ref[5:6, :]).astype(BF)
+
+    @pl.when(jnp.logical_not(live))
+    def _():
+        att_ref[...] = jnp.zeros_like(att_ref)
+        n_ref[...] = jnp.zeros_like(n_ref)
+
+
+def row_valid(info, clip, rows):
+    place = info[3] + lax.broadcasted_iota(jnp.int32, (rows, 1), 0)
+    return (place < info[LEN0 + clip]).astype(F32)
+
+
+def output_kernel(info, x_ref, ct_ref, att_ref, ba_ref, bb_ref, gb_ref, out_ref, sum_ref):
+    r = pl.program_id(0)
+    valid = row_valid(info, r, x_ref.shape[0])
+    branch = ba_ref[...].astype(F32) + bb_ref[...].astype(F32)
+    middle = x_ref[...].astype(F32) + gb_ref[2:3, :] * att_ref[...]
+    out_ref[...] = ((middle + gb_ref[3:4, :] * branch) * valid).astype(BF)
+    part = column_sum(ct_ref[...].astype(F32) * valid * branch)
+
+    @pl.when(r == 0)
+    def _():
+        sum_ref[...] = jnp.zeros_like(sum_ref)
+
+    sum_ref[0:1, :] += part
+
+
+def out_back_kernel(
+    info, sa_ref, sb_ref, att_ref, x_ref, ct_ref, ctx_ref, w_ref, gb_ref,
+    delta_ref, dctx_ref, keep_ref, send_ref, sum_ref, acc,
+):
+    r = pl.program_id(0)
+    rows, width = x_ref.shape
+
+    @pl.when(r == 0)
+    def _():
+        sum_ref[...] = jnp.zeros_like(sum_ref)
+        acc[...] = jnp.zeros_like(acc)
+
+    live = info[3] < info[LEN0 + r]
+
+    @pl.when(live)
+    def _():
+        valid = row_valid(info, r, rows)
+        attended = att_ref[...]
+        middle = x_ref[...].astype(F32) + gb_ref[2:3, :] * attended
+        normal, inverse = norm_stats(middle)
+        second = sa_ref[...].astype(F32) + sb_ref[...].astype(F32)
+        back = norm_back(second, normal, inverse, gb_ref[1:2, :])
+        middle_delta = ct_ref[...].astype(F32) * valid + back
+        delta_ref[...] = middle_delta
+        attended_delta = (middle_delta * gb_ref[2:3, :]).astype(BF)
+        dctx_ref[...] = mm_t(attended_delta, w_ref[...]).astype(BF)
+        acc[...] += t_mm(ctx_ref[...], attended_delta)
+        sum_ref[0:1, :] += column_sum(second * normal)
+        sum_ref[1:2, :] += column_sum(middle_delta * attended)
+        sum_ref[2:3, :] += column_sum(second)
+
+    @pl.when(jnp.logical_not(live))
+    def _():
+        delta_ref[...] = jnp.zeros_like(delta_ref)
+        dctx_ref[...] = jnp.zeros_like(dctx_ref)
+
+    @pl.when(r == pl.num_programs(0) - 1)
+    def _():
+        half = width // 2
+        for x in range(2):
+            col = pl.multiple_of(((info[0] + x) % 2) * half, TILE)
+            for y in range(2):
+                for z in range(4):
+                    base = z * 256 + ((info[1] + y) % 2) * 128
+                    for c, ref in ((0, keep_ref), (1, send_ref)):
+                        row = pl.multiple_of(base + ((info[2] + c) % 2) * 64, 64)
+                        ref[x, y, z] = acc[pl.ds(row, 64), pl.ds(col, half)].astype(BF)
+
+
+def qkv_grad_kernel(info, n_ref, md_ref, nh_ref, mdh_ref, keep_ref, send_ref, acc):
+    t = pl.program_id(0)
+    acc[...] = t_mm(n_ref[...], md_ref[...])
+
+    @pl.when(jnp.logical_and(info[0] > 0, t >= 2))
+    def _():
+        acc[...] += t_mm(nh_ref[...], mdh_ref[...])
+
+    for y in range(2):
+        for z in range(4):
+            z_there = (info[4] // 2 + z // 2) % 2 * 2 + (info[4] + z) % 2
+            base = z_there * 256 + ((info[1] + y) % 2) * 128
+            for c, ref in ((0, keep_ref), (1, send_ref)):
+                row = pl.multiple_of(base + ((info[2] + c) % 2) * 64, 64)
+                ref[0, y, z] = acc[pl.ds(row, 64), :].astype(BF)
+
+
+def first_back_kernel(info, md_ref, w_ref, x_ref, delta_ref, gb_ref, out_ref, sum_ref):
+    r = pl.program_id(0)
+
+    @pl.when(r == 0)
+    def _():
+        sum_ref[...] = jnp.zeros_like(sum_ref)
+
+    live = info[3] < info[LEN0 + r]
+
+    @pl.when(live)
+    def _():
+        first = mm_t(md_ref[...], w_ref[...])
+        normal, inverse = norm_stats(x_ref[...].astype(F32))
+        out_ref[...] = delta_ref[...] + norm_back(first, normal, inverse, gb_ref[0:1, :])
+        sum_ref[0:1, :] += column_sum(first * normal)
+        sum_ref[1:2, :] += column_sum(first)
+
+    @pl.when(jnp.logical_not(live))
+    def _():
+        out_ref[...] = jnp.zeros_like(out_ref)
+
+
+def first_halo_kernel(info, mdh_ref, wk_ref, wv_ref, x_ref, out_ref, sum_ref):
+    r = pl.program_id(0)
+    width = x_ref.shape[1]
+
+    @pl.when(r == 0)
+    def _():
+        sum_ref[...] = jnp.zeros_like(sum_ref)
+
+    live = jnp.logical_and(info[0] > 0, info[3] < info[LEN0 + r])
+
+    @pl.when(live)
+    def _():
+        first = mm_t(mdh_ref[:, :width], wk_ref[...]) + mm_t(mdh_ref[:, width:], wv_ref[...])
+        out_ref[...] = first.astype(BF)
+        normal, _ = norm_stats(x_ref[...].astype(F32))
+        sum_ref[0:1, :] += column_sum(first * normal)
+        sum_ref[1:2, :] += column_sum(first)
+
+    @pl.when(jnp.logical_not(live))
+    def _():
+        out_ref[...] = jnp.zeros_like(out_ref)
+
+
+def input_grad_kernel(info, part_ref, halo_ref, x_ref, gb_ref, out_ref):
+    rows = part_ref.shape[0]
+    split = rows - halo_ref.shape[0]
+    out_ref[:split, :] = part_ref[:split, :].astype(BF)
+
+    @pl.when(info[0] == 0)
+    def _():
+        normal, inverse = norm_stats(x_ref[split:, :].astype(F32))
+        back = norm_back(halo_ref[...].astype(F32), normal, inverse, gb_ref[0:1, :])
+        out_ref[split:, :] = (part_ref[split:, :] + back).astype(BF)
+
+    @pl.when(info[0] > 0)
+    def _():
+        out_ref[split:, :] = part_ref[split:, :].astype(BF)
+
+
+def ffn_kernel(c, z0, first, x_leads, half, info, n_own, n_other, b_own, b_other, *rest):
+    if not first:
+        br_in, se_in, *rest = rest
+    wg_hbm, wu_hbm, wd_hbm, br_ref, se_ref, keep_ref, send_ref, wg, wu, wd, ag, au, ad, sems = rest
+    r = pl.program_id(0)
+
+    def copies():
+        for x in range(2):
+            for q in range(2):
+                k = x * 2 + q
+                d = ((info[0] + x) % 2 * 2 + z0) * 4 + (info[1] + q) % 2 * 2 + info[2]
+                src = pl.ds(pl.multiple_of(d * 256 + c * TILE, TILE), TILE)
+                dst = pl.ds(k * TILE, TILE)
+                yield pltpu.make_async_copy(wg_hbm.at[:, src], wg.at[:, dst], sems.at[0, k])
+                yield pltpu.make_async_copy(wu_hbm.at[:, src], wu.at[:, dst], sems.at[1, k])
+                yield pltpu.make_async_copy(wd_hbm.at[src, :], wd.at[dst, :], sems.at[2, k])
+
+    @pl.when(r == 0)
+    def _():
+        for copy in copies():
+            copy.start()
+        for copy in copies():
+            copy.wait()
+
+    own = r < half
+    normed = jnp.where(own, n_own[...], n_other[...])
+    delta = jnp.where(own, b_own[...], b_other[...])
+    gate = mm(normed, wg[...])
+    upward = mm(normed, wu[...])
+    hidden_delta = mm_t(delta, wd[...])
+    sigmoid = jax.nn.sigmoid(gate)
+    active = gate * sigmoid
+    hidden = (active * upward).astype(BF)
+    up_delta = (hidden_delta * active).astype(BF)
+    gate_delta = (hidden_delta * upward * (sigmoid + active * (1.0 - sigmoid))).astype(BF)
+    branch = mm(hidden, wd[...])
+    second = mm_t(gate_delta, wg[...]) + mm_t(up_delta, wu[...])
+    if not first:
+        branch = branch + br_in[...].astype(F32)
+        second = second + se_in[...].astype(F32)
+    br_ref[...] = branch.astype(BF)
+    se_ref[...] = second.astype(BF)
+    grads = (t_mm(normed, gate_delta), t_mm(normed, up_delta), t_mm(delta, hidden))
+
+    @pl.when(r == 0)
+    def _():
+        for acc, grad in zip((ag, au, ad), grads):
+            acc[...] = grad
+
+    @pl.when(r > 0)
+    def _():
+        for acc, grad in zip((ag, au, ad), grads):
+            acc[...] += grad
+
+    @pl.when(r == pl.num_programs(0) - 1)
+    def _():
+        def put(x, y, tile, value):
+            lead, other = (x, y) if x_leads else (y, x)
+            ref = send_ref if lead else keep_ref
+            ref[other, tile * TILE : (tile + 1) * TILE, :] = value.astype(BF)
+
+        def block(i, n=1):
+            return slice(i * TILE, (i + n) * TILE)
+
+        for x in range(2):
+            for y in range(2):
+                for z in range(4):
+                    here, there = block(z * 2 + y), block(z * 2 + 1 - y)
+                    for q in range(2):
+                        cols, turned = block(x * 2 + q), block(x * 2 + 1 - q)
+                        for i, acc in enumerate((ag, au)):
+                            value = jnp.where(info[1] == 0, acc[here, cols], acc[there, turned])
+                            put(x, y, 8 * i + z * 2 + q, value)
+                for z1 in range(2):
+                    for dq in range(4):
+                        value = jnp.where(
+                            info[0] == 0,
+                            ad[block(x * 4 + dq), block(z1 * 2 + y)],
+                            ad[block((1 - x) * 4 + dq), block((1 - z1) * 2 + y)],
+                        )
+                        put(x, y, 16 + z1 * 4 + dq, value)
+
+
+def ffn_call(c, z0, x_leads, info, pieces, weights, previous, after=(), block_rows=512):
+    rows, width = pieces[0].shape
+    half = rows // block_rows
+    first = previous is None
+    hidden = 4 * TILE
+
+    def spec(index):
+        return pl.BlockSpec((block_rows, width), index)
+
+    own = spec(lambda r, info: (jnp.minimum(r, half - 1), 0))
+    other = spec(lambda r, info: (jnp.maximum(r - half, 0), 0))
+    every = spec(lambda r, info: (r, 0))
+    packed = (2, 24 * TILE, TILE)
+    extra = [] if first else list(previous)
+    return call_kernel(
+        functools.partial(ffn_kernel, c, z0, first, x_leads, half),
+        info,
+        [*pieces, *extra, *weights],
+        name="feed_forward",
+        grid=(2 * half,),
+        ins=[own, other, own, other]
+        + [every] * len(extra)
+        + [pl.BlockSpec(memory_space=pl.ANY)] * 3,
+        outs=[every, every, whole_spec(packed), whole_spec(packed)],
+        shapes=[shape_of((2 * rows, width))] * 2 + [shape_of(packed)] * 2,
+        scratch=[
+            pltpu.VMEM((width, hidden), BF),
+            pltpu.VMEM((width, hidden), BF),
+            pltpu.VMEM((hidden, width), BF),
+            pltpu.VMEM((width, hidden), F32),
+            pltpu.VMEM((width, hidden), F32),
+            pltpu.VMEM((width, hidden), F32),
+            pltpu.SemaphoreType.DMA((3, 4)),
+        ],
+        vmem=56,
+        cost=(18 * 2 * rows * width * hidden, 30 * MIB),
+        after=after,
+    )
+
+
+SWAP = [(0, 1), (1, 0)]
+Z_NEAR = [(0, 1), (1, 0), (2, 3), (3, 2)]
+Z_FAR = [(0, 2), (2, 0), (1, 3), (3, 1)]
+
+
+def swap(values, axis):
+    return lax.ppermute(values, axis, SWAP)
+
+
+def plus(left, right):
+    return (left.astype(F32) + right.astype(F32)).astype(BF)
+
+
+def fold(keep, send, axis):
+    return plus(keep, swap(send, axis))
+
+
+def fold_two(keep, send, lead, other):
+    total = fold(keep, send, lead)
+    return fold(total[0], total[1], other)
+
+
+def scatter_z(values):
+    return lax.psum_scatter(values, "z", scatter_dimension=0, tiled=True)[0]
+
+
+def turn_table(first, last, head_dim):
+    pairs = head_dim // 2
+    rates = np.exp(np.arange(pairs, dtype=np.float32) * np.float32(-2.0 * math.log(10000.0) / head_dim))
+    angles = np.arange(first, last, dtype=np.float32)[:, None] * rates[None, :].astype(np.float32)
+    cosine, sine = (np.tile(t(angles), (1, TILE // pairs)) for t in (np.cos, np.sin))
+    front = (np.arange(TILE) % head_dim < pairs)[None, :]
+    return np.stack([cosine, np.where(front, -sine, 0), np.where(front, 0, sine)]).astype(np.float32)
+
+
+def fast_body(
+    frames, cotangent, lengths, qkv_weight, out_weight, gate_weight, up_weight, down_weight,
+    gain_table, bias_table,
+):
+    clips, rows, width = frames.shape
+    count = clips * rows
+    head_dim = width // HEADS
+    scale = 1.0 / math.sqrt(head_dim)
+    x_at, y_at, core_at, z_at = (lax.axis_index(a) for a in ("seq", "y", "core", "z"))
+    start = x_at * rows
+    info = jnp.concatenate(
+        [jnp.stack([x_at, y_at, core_at, start, z_at]).astype(jnp.int32), lengths.astype(jnp.int32)]
+    )
+    flat = frames.reshape(count, width)
+    tangent = cotangent.reshape(count, width)
+    halo = lax.ppermute(
+        frames[:, rows - TILE :].reshape(clips * TILE, width), "seq", [(0, 1)]
+    )
+    places = start + jnp.arange(rows)
+    valid = (places[None, :] < lengths[:, None]).astype(F32).reshape(count, 1)
+    branch_delta = (tangent.astype(F32) * valid * gain_table[:, 3]).astype(BF)
+    branch_delta_other = swap(branch_delta, "core")
+    table = jnp.concatenate([gain_table, bias_table, jnp.zeros((width, 2), F32)], axis=1).T
+    seats = lax.axis_size("seq")
+    own_turns = jnp.asarray(turn_table(0, seats * rows, head_dim))
+    halo_turns = jnp.asarray(
+        np.concatenate([turn_table(i * rows - TILE, i * rows, head_dim) for i in range(seats)], axis=1)
+    )
+    own_tab = pl.BlockSpec((3, rows, TILE), lambda r, info: (0, info[0], 0))
+    halo_tab = pl.BlockSpec((3, TILE, TILE), lambda r, info: (0, info[0], 0))
+    gb = whole_spec(table.shape)
+    own = rows_spec(rows, width)
+    halo_rows = rows_spec(TILE, width)
+    qkv_rows = rows_spec(rows, 3 * width)
+    kv_rows = rows_spec(TILE, 2 * width)
+    w_qkv = whole_spec((width, 3 * width))
+    w_key = pl.BlockSpec((width, width), lambda r, info: (0, 1))
+    w_value = pl.BlockSpec((width, width), lambda r, info: (0, 2))
+    w_out = whole_spec((width, width))
+    sums = whole_spec((8, width))
+    grid = (clips,)
+    mac = 2 * count * width * width
+
+    qkv, normed_one = call_kernel(
+        qkv_kernel, info, [flat, qkv_weight, table, own_turns], name="qkv", grid=grid,
+        ins=[own, w_qkv, gb, own_tab], outs=[qkv_rows, own],
+        shapes=[shape_of((count, 3 * width)), shape_of((count, width))], cost=(3 * mac, 16 * MIB),
+    )
+    kv_halo, normed_halo = call_kernel(
+        halo_kernel, info, [halo, qkv_weight, qkv_weight, table, halo_turns], name="halo",
+        grid=grid, ins=[halo_rows, w_key, w_value, gb, halo_tab],
+        outs=[kv_rows, halo_rows],
+        shapes=[shape_of((clips * TILE, 2 * width)), shape_of((clips * TILE, width))],
+        cost=(mac, 8 * MIB),
+    )
+    context, log_totals = call_kernel(
+        functools.partial(attend_kernel, scale), info, [qkv, kv_halo], name="attend", grid=grid,
+        ins=[qkv_rows, kv_rows], outs=[own, rows_spec(rows, TILE)],
+        shapes=[shape_of((count, width)), shape_of((count, TILE), F32)], cost=(4 * mac, 12 * MIB),
+    )
+    attended, normed_two = call_kernel(
+        out_kernel, info, [context, flat, out_weight, table], name="project", grid=grid,
+        ins=[own, own, w_out, gb], outs=[own, own],
+        shapes=[shape_of((count, width), F32), shape_of((count, width))], cost=(mac, 12 * MIB),
+    )
+    normed_two_other = swap(normed_two, "core")
+
+    pieces = (normed_two, normed_two_other, branch_delta, branch_delta_other)
+    weights = (gate_weight, up_weight, down_weight)
+    units = [(0, 0), (0, 1), (1, 0), (1, 1)]
+    axes = [("seq", "y"), ("y", "seq")] * 2
+    previous, first_sums = None, []
+
+    def run_ffn(i, after):
+        c, z0 = units[i]
+        *state, keep, send = ffn_call(
+            c, z0, axes[i][0] == "seq", info, pieces, weights, previous, after
+        )
+        return state, keep, swap(send, axes[i][0])
+
+    def last_sum(total, i):
+        return plus(total[0], swap(total[1], axes[i][1])).reshape(24, TILE, TILE)
+
+    def z_sum(parts):
+        gates = [
+            part[8 * i : 8 * i + 8].reshape(4, 2, TILE, TILE) for part in parts for i in range(2)
+        ]
+        downs = jnp.stack([part[16:].reshape(2, 4, TILE, TILE) for part in parts], axis=1)
+        return scatter_z(jnp.concatenate([*gates, downs.reshape(4, 4, TILE, TILE)], axis=1))
+
+    previous, keep_0, came_0 = run_ffn(0, ())
+    previous, keep_1, came_1 = run_ffn(1, ())
+    previous, keep_2, came_2 = run_ffn(2, (came_0,))
+    total_0 = plus(keep_0, came_0)
+    previous, keep_3, came_3 = run_ffn(3, (total_0, came_1))
+    total_1 = plus(keep_1, came_1)
+    part_0 = last_sum(total_0, 0)
+    branch, second = previous
+    second_other = swap(second[count:], "core")
+    branch_other = swap(branch[count:], "core")
+
+    packed = (2, 2, 4, 64, width // 2)
+    middle_delta, context_delta, out_keep, out_send, sums_two = call_kernel(
+        out_back_kernel, info,
+        [second, second_other, attended, flat, tangent, context, out_weight, table],
+        name="project_back", grid=grid,
+        ins=[own, own, own, own, own, own, w_out, gb],
+        outs=[own, own, whole_spec(packed), whole_spec(packed), sums],
+        shapes=[
+            shape_of((count, width), F32), shape_of((count, width)), shape_of(packed),
+            shape_of(packed), shape_of((8, width), F32),
+        ],
+        scratch=[pltpu.VMEM((width, width), F32)], cost=(2 * mac, 24 * MIB),
+        after=(total_1, came_2),
+    )
+    total_2 = plus(keep_2, came_2)
+    part_1 = last_sum(total_1, 1)
+    out_came = swap(out_send, "core")
+
+    output, sums_out = call_kernel(
+        output_kernel, info, [flat, tangent, attended, branch, branch_other, table],
+        name="output", grid=grid, ins=[own, own, own, own, own, gb], outs=[own, sums],
+        shapes=[shape_of((count, width)), shape_of((8, width), F32)], cost=(0, 14 * MIB),
+        after=(part_0, total_2, came_3),
+    )
+    total_3 = plus(keep_3, came_3)
+    z_0 = z_sum((part_0, part_1))
+    out_total = plus(out_keep, out_came)
+    out_came = swap(out_total[1], "seq")
+
+    mixed_delta, mixed_halo = call_kernel(
+        functools.partial(attend_back_kernel, scale), info,
+        [qkv, kv_halo, context_delta, log_totals, own_turns, halo_turns], name="attend_back", grid=grid,
+        ins=[qkv_rows, kv_rows, own, rows_spec(rows, TILE), own_tab, halo_tab],
+        outs=[qkv_rows, kv_rows],
+        shapes=[shape_of((count, 3 * width)), shape_of((clips * TILE, 2 * width))],
+        scratch=[pltpu.VMEM((rows + TILE, width), F32), pltpu.VMEM((rows + TILE, width), F32)],
+        cost=(10 * mac, 24 * MIB), after=(total_3, out_total, part_1, sums_out),
+    )
+    part_2, part_3 = last_sum(total_2, 2), last_sum(total_3, 3)
+    out_total = plus(out_total[0], out_came)
+    out_grad = scatter_z(plus(out_total[0], swap(out_total[1], "y"))).astype(F32)
+    first_halo, sums_halo = call_kernel(
+        first_halo_kernel, info, [mixed_halo, qkv_weight, qkv_weight, halo], name="first_halo",
+        grid=grid, ins=[kv_rows, w_key, w_value, halo_rows], outs=[halo_rows, sums],
+        shapes=[shape_of((clips * TILE, width)), shape_of((8, width), F32)], cost=(mac, 8 * MIB),
+    )
+    first_back = lax.ppermute(first_halo, "seq", [(1, 0)])
+
+    cut = 3 * width // 6
+    packed = (2, 2, 4, 64, 3 * cut)
+    out_spec = pl.BlockSpec(
+        (1, 2, 4, 64, cut), lambda t, info: ((t // 3 + info[0]) % 2, 0, 0, 0, t % 3)
+    )
+    qkv_keep, qkv_send = call_kernel(
+        qkv_grad_kernel, info, [normed_one, mixed_delta, normed_halo, mixed_halo],
+        name="qkv_grad", grid=(6,),
+        ins=[
+            whole_spec((count, width)),
+            pl.BlockSpec((count, cut), lambda t, info: (0, t)),
+            whole_spec((clips * TILE, width)),
+            pl.BlockSpec((clips * TILE, cut), lambda t, info: (0, jnp.maximum(t - 2, 0))),
+        ],
+        outs=[out_spec, out_spec], shapes=[shape_of(packed)] * 2,
+        scratch=[pltpu.VMEM((width, cut), F32)], cost=(4 * mac, 16 * MIB), after=(first_halo, part_2, part_3),
+    )
+    z_1 = z_sum((part_2, part_3))
+    qkv_total = fold(qkv_keep, qkv_send, "core")
+    half = 32
+    left, right = qkv_total[:, :, :, :half], qkv_total[:, :, :, half:]
+    left = fold_two(left[0], left[1], "seq", "y")
+    right = fold_two(right[:, 0], right[:, 1], "y", "seq")
+    qkv_total = jnp.concatenate([left, right], axis=1).reshape(2, 2, 64, -1)
+    for step, pairs in ((1, Z_NEAR), (2, Z_FAR)):
+        keep, send = (qkv_total[:, 0], qkv_total[:, 1]) if step == 1 else (qkv_total[0], qkv_total[1])
+        qkv_total = plus(keep, lax.ppermute(send, "z", pairs))
+    qkv_grad = qkv_total.astype(F32)
+
+    part_grad, sums_one = call_kernel(
+        first_back_kernel, info, [mixed_delta, qkv_weight, flat, middle_delta, table],
+        name="first_back", grid=grid, ins=[qkv_rows, w_qkv, own, own, gb], outs=[own, sums],
+        shapes=[shape_of((count, width), F32), shape_of((8, width), F32)],
+        cost=(3 * mac, 24 * MIB),
+    )
+    input_grad = call_kernel(
+        input_grad_kernel, info, [part_grad, first_back, flat, table], name="input_grad",
+        grid=grid, ins=[own, halo_rows, own, gb], outs=own, shapes=shape_of((count, width)),
+        cost=(0, 8 * MIB),
+    )
+
+    ones = sums_one + sums_halo
+    vectors = jnp.stack(
+        [ones[0], sums_two[0], sums_two[1], sums_out[0], ones[1], sums_two[2], ones[2], ones[3]]
+    )
+    for axis, pairs in (("core", SWAP), ("seq", SWAP), ("y", SWAP), ("z", Z_NEAR), ("z", Z_FAR)):
+        vectors = vectors + lax.ppermute(vectors, axis, pairs)
+    vectors = vectors.T
+    dp_at = (z_at * 2 + y_at) * 2 + core_at
+    share = width // 16
+    mine = lax.dynamic_slice_in_dim(vectors, dp_at * share, share, axis=0)
+    gain_grad = lax.dynamic_slice_in_dim(mine[:, :4], x_at * 2, 2, axis=1)
+    bias_grad = lax.dynamic_slice_in_dim(mine[:, 4:6], x_at, 1, axis=1)
+
+    tiles = jnp.stack([z_0, z_1])
+    gates = tiles[:, :8].reshape(2, 2, 2, 2, 2, share, TILE)
+    kept = lax.dynamic_index_in_dim(gates, core_at, axis=4, keepdims=False)
+    sent = lax.dynamic_index_in_dim(gates, 1 - core_at, axis=4, keepdims=False)
+    came = swap(sent, "core")
+    both = jnp.where(core_at == 0, jnp.stack([kept, came], 4), jnp.stack([came, kept], 4))
+    both = both.transpose(2, 5, 1, 3, 4, 0, 6).astype(F32)
+    gate_grad = both[0].reshape(share, -1)
+    up_grad = both[1].reshape(share, -1)
+    down_grad = tiles[:, 8:].reshape(2, width // 2, TILE).transpose(0, 2, 1).astype(F32)
+    down_grad = down_grad.reshape(2 * TILE, width // 2)
+    shape = (clips, rows, width)
+    return (
+        output.reshape(shape), input_grad.reshape(shape), qkv_grad, out_grad, gate_grad, up_grad,
+        down_grad, gain_grad, bias_grad,
+    )
+
+
 def solution(mesh):
-    placed = (
-        P("dp", "seq", None),
-        P("dp", "seq", None),
-        P("dp"),
-        P(),
-        P(),
-        P(),
-        P(),
-        P(),
-        P(),
-        P(),
-    )
+    placed = (("dp", "seq", None),) * 2 + (("dp",),) + ((),) * 7
+    given = (("dp", "seq", None),) * 2 + (("dp", "seq"),) * 7
+    fast = mesh.shape["dp"] == 16 and mesh.shape["seq"] == 2
+    dp_axes = ("z", "y", "core") if fast else "dp"
+
+    def specs(entries):
+        return tuple(P(*(dp_axes if a == "dp" else a for a in entry)) for entry in entries)
+
+    if fast:
+        mesh = Mesh(mesh.devices.reshape(4, 2, 2, 2), ("z", "y", "core", "seq"))
     return jax.shard_map(
-        body,
+        fast_body if fast else body,
         mesh=mesh,
-        in_specs=placed,
-        out_specs=(
-            P("dp", "seq", None),
-            P("dp", "seq", None),
-            P("dp", "seq"),
-            P("dp", "seq"),
-            P("dp", "seq"),
-            P("dp", "seq"),
-            P("dp", "seq"),
-            P("dp", "seq"),
-            P("dp", "seq"),
-        ),
+        in_specs=specs(placed),
+        out_specs=specs(given),
         check_vma=False,
     )

time: 1610 us -> 481 us (0.30)
  waiting for transfers between devices: 902 us -> 97.8 us
  matrix products: 415 us -> 0 us
  Pallas kernels: 0 us -> 264 us
  local copies, waits for them, and re-layouts: 131 us -> 38.3 us
  other arithmetic: 64.6 us -> 23.2 us
  blocking collectives: 29.3 us -> 0 us
    reduce_scatter x10 -> x3, waiting for transfers between devices: 699 us -> 0.02 us  [scatter_z(): return lax.psum_scatter(values, 'z', scatter_dimension=0, tiled=True)[0]]
    dot_general x43 -> x0, matrix products: 415 us -> none  [the longest x5 73.9 us: times_transposed(): lax.dot_general(left_op, right_op, (((1,), (1,)), ((), ())), preferred_el...]
    pallas_call x0 -> x15, Pallas kernels: none -> 264 us  [call_kernel(): pl.pallas_call(run, grid_spec=pltpu.PrefetchScalarGridSpec(num_scalar_pre...]
    unnamed x14 -> x3, waiting for transfers between devices: 109 us -> 0.05 us
    ppermute x0 -> x30, waiting for transfers between devices: none -> 97.8 us  [the longest x21 66.1 us: swap(): return lax.ppermute(values, axis, SWAP)]
    all_to_all x7 -> x0, waiting for transfers between devices: 94.2 us -> none  [the longest x1 20.3 us: body(): lax.all_to_all(queries, 'seq', split_axis=2, concat_axis=1, tiled=True)]
    reshape x9 -> x1, local copies, waits for them, and re-layouts: 37.5 us -> 1 us  [fast_body(): down_grad = down_grad.reshape(2 * TILE, width // 2)]
    ppermute x0 -> x30, starting transfers between devices: none -> 35.9 us  [the longest x5 14.3 us: fast_body(): vectors = vectors + lax.ppermute(vectors, axis, pairs)]
  transfers between devices with their start and end apart: 19 -> 33, of which waited for: 18 -> 15; matrix products, arithmetic and copies ran while one was open for 10% -> 9% of each run, Pallas kernels for 0% -> 42%
where the time goes in v1:
time: 481 us; the launch traced here: 474 us
  Pallas kernels  264 us (55%)
  waiting for transfers between devices  97.8 us (20%)
  local copies, waits for them, and re-layouts  38.3 us (8%)
  starting transfers between devices  36 us (7%)
  other arithmetic  23.2 us (5%)
  between operations  15 us (3%)
    pallas_call x15, Pallas kernels, call_kernel(): pl.pallas_call(run, grid_spec=pltpu.PrefetchScalarGridSpec(num_scalar_pre...  264 us
    ppermute x21, waiting for transfers between devices, swap(): return lax.ppermute(values, axis, SWAP)  66.1 us
    unnamed x94, local copies, waits for them, and re-layouts  19.1 us
    convert_element_type x16, other arithmetic, plus(): return (left.astype(F32) + right.astype(F32)).astype(BF)  15.7 us
    ppermute x5, starting transfers between devices, fast_body(): vectors = vectors + lax.ppermute(vectors, axis, pairs)  14.3 us
    ppermute x21, starting transfers between devices, swap(): return lax.ppermute(values, axis, SWAP)  13.3 us
    ppermute x5, waiting for transfers between devices, fast_body(): vectors = vectors + lax.ppermute(vectors, axis, pairs)  11.3 us
    ppermute x1, waiting for transfers between devices, fast_body(): first_back = lax.ppermute(first_halo, 'seq', [(1, 0)])  11 us
  transfers between devices with their start and end apart: 33, of which 15 were waited for; matrix products, arithmetic and copies ran while one was open for 9% of the time, Pallas kernels for 42%

profile of v1, /device:TPU:0, one launch (start us, length us, event | category | flops | bytes accessed | tf_op | source)
XLA Modules:
  0.0 474.1 jit_solution(6082276956393642093)
XLA Ops:
  7.2 2.3 slice.178
  9.5 4.9 %collective-permute-start = (bf16[512,1024]{1,0:T(8,128)(2,1)}, bf16[512,1024]{1,0:T(8,128)(2,1)S(1)}, u32[]{:S(2)}, u32[]{:S(2)}) collective-permute-start(bf16[512,1024]{1,0:T(8,128)(2,1)} %bitcast.8), channel_id=1, source_target_pairs={{0,1},{2,3},{4,5},{6,7},{8,9},{10,11},{12,13},{14,15},{16,17},{18,... | collective-permute-start | bytes 3145736 | tf_op jit(solution)/shard_map/ppermute | solution.py:897
  14.6 3.6 multiply_convert_fusion.refs_2_
  18.4 1.1 copy-done.21
  19.5 12.9 %qkv.1 = (bf16[1024,3072]{1,0:T(8,128)(2,1)}, bf16[1024,1024]{1,0:T(8,128)(2,1)S(1)}) custom-call(s32[9]{0:T(128)S(1)} %concatenate.15.info, bf16[1024,1024]{1,0:T(8,128)(2,1)S(1)} %bitcast.153, bf16[1024,3072]{1,0:T(8,128)(2,1)} %refs_2_.5, f32[8,1024]{1,0:T(8,128)S(1)} %maximum_bitcast_fusion.refs_2_.refs_3_.refs_5_.refs_7_.refs_4_, ...), custom_call_target="tpu_custom_call" | custom-call | flops 6442450944 | bytes 16777216 | tf_op jit(solution)/shard_map/qkv/pallas_call | solution.py:324
  32.4 1.4 copy-done.23
  33.8 3.2 collective-permute-done.refs_0_.refs_3_
  37.1 3.1 halo.1
  41.2 14.9 %attend.1 = (bf16[1024,1024]{1,0:T(8,128)(2,1)S(1)}, f32[1024,128]{1,0:T(8,128)S(1)}) custom-call(s32[9]{0:T(128)S(1)} %concatenate.15.info, bf16[1024,3072]{1,0:T(8,128)(2,1)} %get-tuple-element.48.refs_0_, bf16[512,2048]{1,0:T(8,128)(2,1)S(1)} %get-tuple-element.49.refs_1_), custom_call_target="tpu_custom_call" | custom-call | flops 8589934592 | bytes 12582912 | tf_op jit(solution)/shard_map/attend/pallas_call | solution.py:324
  56.9 8.0 %project.1 = (f32[1024,1024]{1,0:T(8,128)}, bf16[1024,1024]{1,0:T(8,128)(2,1)S(1)}) custom-call(s32[9]{0:T(128)S(1)} %concatenate.15.info, bf16[1024,1024]{1,0:T(8,128)(2,1)S(1)} %get-tuple-element.50.refs_0_.refs_5_, bf16[1024,1024]{1,0:T(8,128)(2,1)} %bitcast.151, bf16[1024,1024]{1,0:T(8,128)(2,1)} %refs_6_.9, ...), custom_call_target="tpu_custom_call" | custom-call | flops 2147483648 | bytes 12582912 | tf_op jit(solution)/shard_map/project/pallas_call | solution.py:324
  64.9 4.1 collective-permute-done.1.refs_1_
  69.0 1.3 copy-done.41
  70.3 31.7 %feed_forward.4 = (bf16[2048,1024]{1,0:T(8,128)(2,1)}, bf16[2048,1024]{1,0:T(8,128)(2,1)}, bf16[2,3072,128]{2,1,0:T(8,128)(2,1)}, bf16[2,3072,128]{2,1,0:T(8,128)(2,1)}) custom-call(s32[9]{0:T(128)} %copy-done.14, bf16[1024,1024]{1,0:T(8,128)(2,1)} %copy-done.17, bf16[1024,1024]{1,0:T(8,128)(2,1)} %copy-done.41, ...), custom_call_target="tpu_custom_call" | custom-call | flops 19327352832 | bytes 31457280 | tf_op jit(solution)/shard_map/feed_forward/pallas_call | solution.py:324
  102.1 33.1 %feed_forward.5 = (bf16[2048,1024]{1,0:T(8,128)(2,1)}, bf16[2048,1024]{1,0:T(8,128)(2,1)}, bf16[2,3072,128]{2,1,0:T(8,128)(2,1)}, bf16[2,3072,128]{2,1,0:T(8,128)(2,1)}) custom-call(s32[9]{0:T(128)} %copy-done.14, bf16[1024,1024]{1,0:T(8,128)(2,1)} %copy-done.17, bf16[1024,1024]{1,0:T(8,128)(2,1)} %copy-done.41, ...), custom_call_target="tpu_custom_call" | custom-call | flops 19327352832 | bytes 31457280 | tf_op jit(solution)/shard_map/feed_forward/pallas_call | solution.py:324
  135.5 3.3 collective-permute-done.3.refs_9_
  140.0 32.6 %feed_forward.6 = (bf16[2048,1024]{1,0:T(8,128)(2,1)}, bf16[2048,1024]{1,0:T(8,128)(2,1)}, bf16[2,3072,128]{2,1,0:T(8,128)(2,1)}, bf16[2,3072,128]{2,1,0:T(8,128)(2,1)}) custom-call(s32[9]{0:T(128)} %copy-done.14, bf16[1024,1024]{1,0:T(8,128)(2,1)} %copy-done.17, bf16[1024,1024]{1,0:T(8,128)(2,1)} %copy-done.41, ...), custom_call_target="tpu_custom_call" | custom-call | flops 19327352832 | bytes 31457280 | tf_op jit(solution)/shard_map/feed_forward/pallas_call | solution.py:324
  172.7 1.2 copy-done.33
  173.8 32.7 %feed_forward.7 = (bf16[2048,1024]{1,0:T(8,128)(2,1)}, bf16[2048,1024]{1,0:T(8,128)(2,1)}, bf16[2,3072,128]{2,1,0:T(8,128)(2,1)}, bf16[2,3072,128]{2,1,0:T(8,128)(2,1)}) custom-call(s32[9]{0:T(128)} %copy-done.14, bf16[1024,1024]{1,0:T(8,128)(2,1)} %copy-done.17, bf16[1024,1024]{1,0:T(8,128)(2,1)} %copy-done.41, ...), custom_call_target="tpu_custom_call" | custom-call | flops 19327352832 | bytes 31457280 | tf_op jit(solution)/shard_map/feed_forward/pallas_call | solution.py:324
  206.6 3.2 slice.180
  209.8 1.3 collective-permute-start.7
  211.1 1.7 collective-permute-start.8
  212.9 1.5 slice.183
  216.0 14.1 %collective-permute-done.6 = bf16[3072,128]{1,0:T(8,128)(2,1)S(1)} collective-permute-done((bf16[3072,128]{1,0:T(8,128)(2,1)S(1)}, bf16[3072,128]{1,0:T(8,128)(2,1)S(1)}, u32[]{:S(2)}, u32[]{:S(2)}) %collective-permute-start.6) | collective-permute-done | bytes 786464 | tf_op jit(solution)/shard_map/ppermute | solution.py:853
  230.1 1.0 collective-permute-start.11
  233.0 30.7 %collective-permute-done.11 = bf16[3072,128]{1,0:T(8,128)(2,1)S(1)} collective-permute-done((bf16[3072,128]{1,0:T(8,128)(2,1)S(1)}, bf16[3072,128]{1,0:T(8,128)(2,1)S(1)}, u32[]{:S(2)}, u32[]{:S(2)}) %collective-permute-start.11) | collective-permute-done | bytes 786464 | tf_op jit(solution)/shard_map/ppermute | solution.py:853
  266.7 2.4 add_convert_fusion.3.refs_7_
  269.1 1.8 collective-permute-start.13
  271.0 1.9 add_convert_fusion.1.refs_6_
  273.0 1.1 collective-permute-start.14
  274.3 14.9 %project_back.1 = (f32[1024,1024]{1,0:T(8,128)}, bf16[1024,1024]{1,0:T(8,128)(2,1)}, bf16[2,2,4,64,512]{4,3,2,1,0:T(8,128)(2,1)S(1)}, bf16[2,2,4,64,512]{4,3,2,1,0:T(8,128)(2,1)S(1)}, f32[8,1024]{1,0:T(8,128)S(1)}) custom-call(s32[9]{0:T(128)S(1)} %copy-done.15, bf16[2048,1024]{1,0:T(8,128)(2,1)} %get-tuple-element.67.refs_0_, ...), custom_call_target="tpu_custom_call" | custom-call | flops 4294967296 | bytes 25165824 | tf_op jit(solution)/shard_map/project_back/pallas_call | solution.py:324
  289.2 7.0 %output.1 = (bf16[1024,1024]{1,0:T(8,128)(2,1)}, f32[8,1024]{1,0:T(8,128)S(1)}) custom-call(s32[9]{0:T(128)S(1)} %copy-done.15, bf16[1024,1024]{1,0:T(8,128)(2,1)S(1)} %bitcast.154, bf16[1024,1024]{1,0:T(8,128)(2,1)} %bitcast.162, f32[1024,1024]{1,0:T(8,128)} %get-tuple-element.51.refs_2_, bf16[2048,1024]{1,0:T(8,128)(2,1)} %get-tuple-element.62.refs_3_, ...), custom_call_target="tpu_custom_call" | custom-call | bytes 14680064 | tf_op jit(solution)/shard_map/output/pallas_call | solution.py:324
  298.4 36.6 %attend_back.1 = (bf16[1024,3072]{1,0:T(8,128)(2,1)}, bf16[512,2048]{1,0:T(8,128)(2,1)}) custom-call(s32[9]{0:T(128)S(1)} %copy-done.15, bf16[1024,3072]{1,0:T(8,128)(2,1)} %get-tuple-element.48.refs_0_, bf16[512,2048]{1,0:T(8,128)(2,1)} %copy-done.16, bf16[1024,1024]{1,0:T(8,128)(2,1)} %get-tuple-element.69.refs_2_, f32[1024,128]{1,0:T(8,128)S(1)} %copy-done.26, ...), custom_call_target="tpu_custom_call" | custom-call | flops 21474836480 | bytes 25165824 | tf_op jit(solution)/shard_map/attend_back/pallas_call | solution.py:324
  335.0 1.6 copy-done.11
  336.6 3.3 first_halo.1
  340.0 12.3 %qkv_grad.1 = (bf16[2,2,4,64,1536]{4,3,2,1,0:T(8,128)(2,1)}, bf16[2,2,4,64,1536]{4,3,2,1,0:T(8,128)(2,1)}) custom-call(s32[9]{0:T(128)S(1)} %copy-done.15, bf16[1024,1024]{1,0:T(8,128)(2,1)S(1)} %copy-done.24, bf16[1024,3072]{1,0:T(8,128)(2,1)} %get-tuple-element.75.refs_0_.refs_1_, bf16[512,1024]{1,0:T(8,128)(2,1)S(1)} %copy-done.20, ...), custom_call_target="tpu_custom_call" | custom-call | flops 8589934592 | bytes 16777216 | tf_op jit(solution)/shard_map/qkv_grad/pallas_call | solution.py:324
  357.6 14.7 %first_back.1 = (f32[1024,1024]{1,0:T(8,128)}, f32[8,1024]{1,0:T(8,128)S(1)}) custom-call(s32[9]{0:T(128)S(1)} %copy-done.15, bf16[1024,3072]{1,0:T(8,128)(2,1)} %get-tuple-element.75.refs_0_.refs_1_, bf16[1024,3072]{1,0:T(8,128)(2,1)} %refs_2_.5, bf16[1024,1024]{1,0:T(8,128)(2,1)S(1)} %bitcast.155, f32[1024,1024]{1,0:T(8,128)} %get-tuple-element.76.refs_3_, ...), custom_call_target="tpu_custom_call" | custom-call | flops 6442450944 | bytes 25165824 | tf_op jit(solution)/shard_map/first_back/pallas_call | solution.py:324
  372.6 1.1 collective-permute-done.25
  373.7 2.1 collective-permute-start.26
  375.8 1.9 collective-permute-done.26
  377.7 3.9 collective-permute-done.27
  381.6 2.3 collective-permute-start.28
  383.9 3.8 collective-permute-done.28
  387.7 9.8 %collective-permute-start.29 = (f32[8,1024]{1,0:T(8,128)S(1)}, f32[8,1024]{1,0:T(8,128)S(1)}, u32[]{:S(2)}, u32[]{:S(2)}) collective-permute-start(f32[8,1024]{1,0:T(8,128)S(1)} %add.137), channel_id=1, source_target_pairs={{0,16},{16,0},{8,24},{24,8},{1,17},{17,1},{9,25},{25,9},{2,18},{18... | collective-permute-start | bytes 98312 | tf_op jit(solution)/shard_map/ppermute | solution.py:1077
  397.5 1.3 collective-permute-start.12
  399.4 1.2 fusion.6
  401.4 3.9 add_convert_fusion
  405.3 1.0 slice_bitcast_fusion.2
  406.3 1.2 slice_bitcast_fusion
  407.5 2.4 collective-permute-start.16
  409.9 2.0 collective-permute-start.18
  414.8 11.0 %collective-permute-done.12.refs_1_ = bf16[512,1024]{1,0:T(8,128)(2,1)} collective-permute-done((bf16[512,1024]{1,0:T(8,128)(2,1)}, bf16[512,1024]{1,0:T(8,128)(2,1)}, u32[]{:S(2)}, u32[]{:S(2)}) %collective-permute-start.12) | collective-permute-done | bytes 1048608 | tf_op jit(solution)/shard_map/ppermute | solution.py:1029
  425.7 5.9 %input_grad.1 = bf16[1024,1024]{1,0:T(8,128)(2,1)} custom-call(s32[9]{0:T(128)S(1)} %copy-done.15, f32[1024,1024]{1,0:T(8,128)} %get-tuple-element.77.refs_0_, bf16[512,1024]{1,0:T(8,128)(2,1)} %collective-permute-done.12.refs_1_, bf16[1024,1024]{1,0:T(8,128)(2,1)S(1)} %bitcast.156, f32[8,1024]{1,0:T(8,128)S(1)} %maximum_bitcast_fusion.refs_2_.refs_3_.refs_5_.refs_7_.refs_4_), custom_call_target="tpu_custom_call" | custom-call | bytes 8388608 | tf_op jit(solution)/shard_map/input_grad/pallas_call | solution.py:324
  431.6 1.0 constant_dynamic-update-slice_fusion.10
  432.9 6.3 %collective-permute-done.16 = bf16[2,4,32,1536]{3,2,1,0:T(8,128)(2,1)} collective-permute-done((bf16[2,4,32,1536]{3,2,1,0:T(8,128)(2,1)}, bf16[2,4,32,1536]{3,2,1,0:T(8,128)(2,1)}, u32[]{:S(2)}, u32[]{:S(2)}) %collective-permute-start.16) | collective-permute-done | bytes 786464 | tf_op jit(solution)/shard_map/ppermute | solution.py:853
  439.2 2.3 fusion.1
  442.0 7.4 %collective-permute-done.19 = bf16[4,32,1536]{2,1,0:T(8,128)(2,1)S(1)} collective-permute-done((bf16[4,32,1536]{2,1,0:T(8,128)(2,1)S(1)}, bf16[4,32,1536]{2,1,0:T(8,128)(2,1)S(1)}, u32[]{:S(2)}, u32[]{:S(2)}) %collective-permute-start.19) | collective-permute-done | bytes 393248 | tf_op jit(solution)/shard_map/ppermute | solution.py:853
  449.7 2.0 collective-permute-start.20
  451.8 1.5 bitcast_convert_fusion
  454.3 1.1 convert_bitcast_fusion
  455.5 3.0 collective-permute-done.20
  458.5 1.1 fusion.7
  460.2 1.2 reshape_squeeze.6
  461.8 1.2 reshape_squeeze.7
  463.0 3.2 collective-permute-done.21
  (193 shorter events, 26.2 us)
Async XLA Ops:
  7.2 7.2 %copy-start.37 = (f32[1024,4]{0,1:T(4,128)S(1)}, f32[1024,4]{0,1:T(4,128)}, u32[]{:S(2)}) copy-start(f32[1024,4]{0,1:T(4,128)} %param.20) | copy-start | bytes 49156
  7.2 7.3 %copy-start.40 = (s32[4]{0:T(128)S(1)}, s32[4]{0:T(128)}, u32[]{:S(2)}) copy-start(s32[4]{0:T(128)} %param.14) | copy-start | bytes 52
  7.2 406.6 %reduce-scatter.6.cloned.1.call-start = ((), (), s32[]{:S(2)}) async-start(), calls=%async_computation.4 | async-start | bytes 1966080 | tf_op jit(solution)/shard_map/reduce_scatter | solution.py:870
  9.5 27.6 %collective-permute-start = (bf16[512,1024]{1,0:T(8,128)(2,1)}, bf16[512,1024]{1,0:T(8,128)(2,1)S(1)}, u32[]{:S(2)}, u32[]{:S(2)}) collective-permute-start(bf16[512,1024]{1,0:T(8,128)(2,1)} %bitcast.8), channel_id=1, source_target_pairs={{0,1},{2,3},{4,5},{6,7},{8,9},{10,11},{12,13},{14,15},{16,17},{18,... | collective-permute-start | bytes 3145736 | tf_op jit(solution)/shard_map/ppermute | solution.py:897
  14.5 3.7 copy-start.39
  14.5 3.8 copy-start
  18.1 46.7 %collective-permute-start.2 = (bf16[1024,1024]{1,0:T(8,128)(2,1)}, bf16[1024,1024]{1,0:T(8,128)(2,1)}, u32[]{:S(2)}, u32[]{:S(2)}) collective-permute-start(bf16[1024,1024]{1,0:T(8,128)(2,1)} %multiply_convert_fusion.refs_2_), channel_id=1, source_target_pairs={{0,2},{2,0},{1,3},{3,1},{4,6},{6,4},{5,7},{7,5},{8,10},{10,8},{9,1... | collective-permute-start | bytes 6291464 | tf_op jit(solution)/shard_map/ppermute | solution.py:853
  18.3 38.6 %copy-start.14 = (s32[9]{0:T(128)}, s32[9]{0:T(128)S(1)}, u32[]{:S(2)}) copy-start(s32[9]{0:T(128)S(1)} %concatenate.15.info) | copy-start | bytes 112
  19.5 17.6 %copy-start.12 = (f32[3,256,128]{2,1,0:T(8,128)S(1)}, f32[3,256,128]{2,1,0:T(8,128)}, u32[]{:S(2)}) copy-start(f32[3,256,128]{2,1,0:T(8,128)} %constant.43.clone.refs_4_.refs_5_) | copy-start | bytes 1179652
  37.1 3.1 copy-start.6
  41.2 14.9 %copy-start.16 = (bf16[512,2048]{1,0:T(8,128)(2,1)}, bf16[512,2048]{1,0:T(8,128)(2,1)S(1)}, u32[]{:S(2)}) copy-start(bf16[512,2048]{1,0:T(8,128)(2,1)S(1)} %get-tuple-element.49.refs_1_) | copy-start | bytes 6291460
  56.9 8.0 %copy-start.10 = (bf16[1024,1024]{1,0:T(8,128)(2,1)}, bf16[1024,1024]{1,0:T(8,128)(2,1)S(1)}, u32[]{:S(2)}) copy-start(bf16[1024,1024]{1,0:T(8,128)(2,1)S(1)} %get-tuple-element.50.refs_0_.refs_5_) | copy-start | bytes 6291460
  64.9 4.2 copy-start.17
  64.9 4.2 collective-permute-start.1
  102.1 36.7 %collective-permute-start.3 = (bf16[2,3072,128]{2,1,0:T(8,128)(2,1)}, bf16[2,3072,128]{2,1,0:T(8,128)(2,1)S(1)}, u32[]{:S(2)}, u32[]{:S(2)}) collective-permute-start(bf16[2,3072,128]{2,1,0:T(8,128)(2,1)} %get-tuple-element.57), channel_id=1, source_target_pairs={{0,1},{1,0},{2,3},{3,2},{4,5},{5,4},{6,7},{7,6},{8,9},{9,8},{10,11... | collective-permute-start | bytes 4718600 | tf_op jit(solution)/shard_map/ppermute | solution.py:853
  102.1 36.6 %copy-start.36 = (bf16[2,3072,128]{2,1,0:T(8,128)(2,1)S(1)}, bf16[2,3072,128]{2,1,0:T(8,128)(2,1)}, u32[]{:S(2)}) copy-start(bf16[2,3072,128]{2,1,0:T(8,128)(2,1)} %get-tuple-element.60) | copy-start | bytes 4718596
  135.2 37.4 %collective-permute-start.4 = (bf16[2,3072,128]{2,1,0:T(8,128)(2,1)}, bf16[2,3072,128]{2,1,0:T(8,128)(2,1)S(1)}, u32[]{:S(2)}, u32[]{:S(2)}) collective-permute-start(bf16[2,3072,128]{2,1,0:T(8,128)(2,1)} %get-tuple-element.61), channel_id=1, source_target_pairs={{0,4},{4,0},{1,5},{5,1},{2,6},{6,2},{3,7},{7,3},{8,12},{12,8},{9,1... | collective-permute-start | bytes 4718600 | tf_op jit(solution)/shard_map/ppermute | solution.py:853
  139.9 32.7 %copy-start.29 = (bf16[2,3072,128]{2,1,0:T(8,128)(2,1)}, bf16[2,3072,128]{2,1,0:T(8,128)(2,1)S(1)}, u32[]{:S(2)}) copy-start(bf16[2,3072,128]{2,1,0:T(8,128)(2,1)S(1)} %add_convert_fusion.4.refs_9_) | copy-start | bytes 4718596
  206.6 6.3 %copy-start.28 = (bf16[2048,1024]{1,0:T(8,128)(2,1)S(1)}, bf16[2048,1024]{1,0:T(8,128)(2,1)}, u32[]{:S(2)}) copy-start(bf16[2048,1024]{1,0:T(8,128)(2,1)} %get-tuple-element.67.refs_0_) | copy-start | bytes 12582916
  209.8 79.4 %collective-permute-start.5 = (bf16[1024,1024]{1,0:T(8,128)(2,1)}, bf16[1024,1024]{1,0:T(8,128)(2,1)}, u32[]{:S(2)}, u32[]{:S(2)}) collective-permute-start(bf16[1024,1024]{1,0:T(8,128)(2,1)} %slice.180), channel_id=1, source_target_pairs={{0,2},{2,0},{1,3},{3,1},{4,6},{6,4},{5,7},{7,5},{8,10},{10,8},{9,1... | collective-permute-start | bytes 6291464 | tf_op jit(solution)/shard_map/ppermute | solution.py:853
  209.8 20.3 %collective-permute-start.6 = (bf16[3072,128]{1,0:T(8,128)(2,1)S(1)}, bf16[3072,128]{1,0:T(8,128)(2,1)S(1)}, u32[]{:S(2)}, u32[]{:S(2)}) collective-permute-start(bf16[3072,128]{1,0:T(8,128)(2,1)S(1)} %slice_bitcast_fusion.10), channel_id=1, source_target_pairs={{0,4},{4,0},{1,5},{5,1},{2,6},{6,2},{3,7},{7,3},{8,12},{12,8},{9,1... | collective-permute-start | bytes 2359304 | tf_op jit(solution)/shard_map/ppermute | solution.py:853
  209.8 56.8 %collective-permute-start.7 = (bf16[2,3072,128]{2,1,0:T(8,128)(2,1)}, bf16[2,3072,128]{2,1,0:T(8,128)(2,1)S(1)}, u32[]{:S(2)}, u32[]{:S(2)}) collective-permute-start(bf16[2,3072,128]{2,1,0:T(8,128)(2,1)} %get-tuple-element.64), channel_id=1, source_target_pairs={{0,1},{1,0},{2,3},{3,2},{4,5},{5,4},{6,7},{7,6},{8,9},{9,8},{10,11... | collective-permute-start | bytes 4718600 | tf_op jit(solution)/shard_map/ppermute | solution.py:853
  211.1 59.8 %collective-permute-start.8 = (bf16[2,3072,128]{2,1,0:T(8,128)(2,1)}, bf16[2,3072,128]{2,1,0:T(8,128)(2,1)}, u32[]{:S(2)}, u32[]{:S(2)}) collective-permute-start(bf16[2,3072,128]{2,1,0:T(8,128)(2,1)} %get-tuple-element.65), channel_id=1, source_target_pairs={{0,4},{4,0},{1,5},{5,1},{2,6},{6,2},{3,7},{7,3},{8,12},{12,8},{9,1... | collective-permute-start | bytes 4718600 | tf_op jit(solution)/shard_map/ppermute | solution.py:853
  212.9 2.1 copy-start.32
  212.9 2.6 copy-start.34
  214.4 59.7 %collective-permute-start.9 = (bf16[1024,1024]{1,0:T(8,128)(2,1)}, bf16[1024,1024]{1,0:T(8,128)(2,1)}, u32[]{:S(2)}, u32[]{:S(2)}) collective-permute-start(bf16[1024,1024]{1,0:T(8,128)(2,1)} %slice.183), channel_id=1, source_target_pairs={{0,2},{2,0},{1,3},{3,1},{4,6},{6,4},{5,7},{7,5},{8,10},{10,8},{9,1... | collective-permute-start | bytes 6291464 | tf_op jit(solution)/shard_map/ppermute | solution.py:853
  215.9 47.8 %copy-start.2 = (bf16[2,3072,128]{2,1,0:T(8,128)(2,1)}, bf16[2,3072,128]{2,1,0:T(8,128)(2,1)S(1)}, u32[]{:S(2)}) copy-start(bf16[2,3072,128]{2,1,0:T(8,128)(2,1)S(1)} %add_convert_fusion.2.refs_8_) | copy-start | bytes 4718596
  215.9 15.3 %copy-start.30 = (bf16[2,3072,128]{2,1,0:T(8,128)(2,1)S(1)}, bf16[2,3072,128]{2,1,0:T(8,128)(2,1)}, u32[]{:S(2)}) copy-start(bf16[2,3072,128]{2,1,0:T(8,128)(2,1)} %copy-done.29) | copy-start | bytes 4718596
  230.1 33.5 %collective-permute-start.11 = (bf16[3072,128]{1,0:T(8,128)(2,1)S(1)}, bf16[3072,128]{1,0:T(8,128)(2,1)S(1)}, u32[]{:S(2)}, u32[]{:S(2)}) collective-permute-start(bf16[3072,128]{1,0:T(8,128)(2,1)S(1)} %slice_bitcast_fusion.8), channel_id=1, source_target_pairs={{0,1},{1,0},{2,3},{3,2},{4,5},{5,4},{6,7},{7,6},{8,9},{9,8},{10,11... | collective-permute-start | bytes 2359304 | tf_op jit(solution)/shard_map/ppermute | solution.py:853
  263.9 1.8 copy-start.8
  266.6 165.0 %reduce-scatter.8.cloned.1.call-start = ((), (), s32[]{:S(2)}) async-start(), calls=%async_computation.5 | async-start | bytes 1966080 | tf_op jit(solution)/shard_map/reduce_scatter | solution.py:870
  266.7 2.4 copy-start.4
  269.1 1.9 copy-start.31
  269.1 27.1 %collective-permute-start.13 = (bf16[3072,128]{1,0:T(8,128)(2,1)S(1)}, bf16[3072,128]{1,0:T(8,128)(2,1)S(1)}, u32[]{:S(2)}, u32[]{:S(2)}) collective-permute-start(bf16[3072,128]{1,0:T(8,128)(2,1)S(1)} %slice_bitcast_fusion.6), channel_id=1, source_target_pairs={{0,4},{4,0},{1,5},{5,1},{2,6},{6,2},{3,7},{7,3},{8,12},{12,8},{9,1... | collective-permute-start | bytes 2359304 | tf_op jit(solution)/shard_map/ppermute | solution.py:853
  271.0 3.1 copy-start.5
  273.0 23.5 %collective-permute-start.14 = (bf16[3072,128]{1,0:T(8,128)(2,1)S(1)}, bf16[3072,128]{1,0:T(8,128)(2,1)S(1)}, u32[]{:S(2)}, u32[]{:S(2)}) collective-permute-start(bf16[3072,128]{1,0:T(8,128)(2,1)S(1)} %slice_bitcast_fusion.4), channel_id=1, source_target_pairs={{0,1},{1,0},{2,3},{3,2},{4,5},{5,4},{6,7},{7,6},{8,9},{9,8},{10,11... | collective-permute-start | bytes 2359304 | tf_op jit(solution)/shard_map/ppermute | solution.py:853
  274.3 14.9 %copy-start.1 = (bf16[4,256,1024]{2,1,0:T(8,128)(2,1)S(1)}, bf16[4,256,1024]{2,1,0:T(8,128)(2,1)}, u32[]{:S(2)}) copy-start(bf16[4,256,1024]{2,1,0:T(8,128)(2,1)} %param.12) | copy-start | bytes 6291460
  289.2 7.5 %collective-permute-start.10 = (bf16[2,2,4,64,512]{4,3,2,1,0:T(8,128)(2,1)S(1)}, bf16[2,2,4,64,512]{4,3,2,1,0:T(8,128)(2,1)S(1)}, u32[]{:S(2)}, u32[]{:S(2)}) collective-permute-start(bf16[2,2,4,64,512]{4,3,2,1,0:T(8,128)(2,1)S(1)} %get-tuple-element.73), channel_id=1, source_target_pairs={{0,2},{2,0},{1,3},{3,1},{4,6},{6,4},{5,7},{7,5},{8,10},{10,8},{9,1... | collective-permute-start | bytes 3145736 | tf_op jit(solution)/shard_map/ppermute | solution.py:853
  296.7 1.6 copy-start.26
  298.4 36.6 %copy-start.7 = (bf16[512,1024]{1,0:T(8,128)(2,1)S(1)}, bf16[512,1024]{1,0:T(8,128)(2,1)}, u32[]{:S(2)}) copy-start(bf16[512,1024]{1,0:T(8,128)(2,1)} %copy-done.6) | copy-start | bytes 3145732
  335.0 1.6 copy-start.11
  336.6 3.4 copy-start.20
  336.6 3.4 copy-start.24
  339.9 12.3 %copy-start.18 = (bf16[512,1024]{1,0:T(8,128)(2,1)}, bf16[512,1024]{1,0:T(8,128)(2,1)S(1)}, u32[]{:S(2)}) copy-start(bf16[512,1024]{1,0:T(8,128)(2,1)S(1)} %get-tuple-element.79.refs_4_) | copy-start | bytes 3145732
  352.2 49.1 %collective-permute-start.15 = (bf16[2,2,4,64,1536]{4,3,2,1,0:T(8,128)(2,1)}, bf16[2,2,4,64,1536]{4,3,2,1,0:T(8,128)(2,1)}, u32[]{:S(2)}, u32[]{:S(2)}) collective-permute-start(bf16[2,2,4,64,1536]{4,3,2,1,0:T(8,128)(2,1)} %get-tuple-element.83), channel_id=1, source_target_pairs={{0,2},{2,0},{1,3},{3,1},{4,6},{6,4},{5,7},{7,5},{8,10},{10,8},{9,1... | collective-permute-start | bytes 9437192 | tf_op jit(solution)/shard_map/ppermute | solution.py:853
  356.7 95.0 %reduce-scatter.4.cloned.1.call-start = ((), (), s32[]{:S(2)}) async-start(), calls=%async_computation.3 | async-start | bytes 327680 | tf_op jit(solution)/shard_map/reduce_scatter | solution.py:870
  357.6 41.8 %collective-permute-start.22 = (bf16[2,4,64,512]{3,2,1,0:T(8,128)(2,1)}, bf16[2,4,64,512]{3,2,1,0:T(8,128)(2,1)}, u32[]{:S(2)}, u32[]{:S(2)}) collective-permute-start(bf16[2,4,64,512]{3,2,1,0:T(8,128)(2,1)} %slice_bitcast_fusion.12), channel_id=1, source_target_pairs={{0,1},{1,0},{2,3},{3,2},{4,5},{5,4},{6,7},{7,6},{8,9},{9,8},{10,11... | collective-permute-start | bytes 1572872 | tf_op jit(solution)/shard_map/ppermute | solution.py:853
  372.4 1.3 collective-permute-start.25
  373.7 3.9 collective-permute-start.26
  377.6 3.9 collective-permute-start.27
  381.6 6.1 %collective-permute-start.28 = (f32[8,1024]{1,0:T(8,128)S(1)}, f32[8,1024]{1,0:T(8,128)S(1)}, u32[]{:S(2)}, u32[]{:S(2)}) collective-permute-start(f32[8,1024]{1,0:T(8,128)S(1)} %add.136), channel_id=1, source_target_pairs={{0,8},{8,0},{16,24},{24,16},{1,9},{9,1},{17,25},{25,17},{2,10},{10... | collective-permute-start | bytes 98312 | tf_op jit(solution)/shard_map/ppermute | solution.py:1077
  387.7 11.7 %collective-permute-start.29 = (f32[8,1024]{1,0:T(8,128)S(1)}, f32[8,1024]{1,0:T(8,128)S(1)}, u32[]{:S(2)}, u32[]{:S(2)}) collective-permute-start(f32[8,1024]{1,0:T(8,128)S(1)} %add.137), channel_id=1, source_target_pairs={{0,16},{16,0},{8,24},{24,8},{1,17},{17,1},{9,25},{25,9},{2,18},{18... | collective-permute-start | bytes 98312 | tf_op jit(solution)/shard_map/ppermute | solution.py:1077
  397.5 28.3 %collective-permute-start.12 = (bf16[512,1024]{1,0:T(8,128)(2,1)}, bf16[512,1024]{1,0:T(8,128)(2,1)}, u32[]{:S(2)}, u32[]{:S(2)}) collective-permute-start(bf16[512,1024]{1,0:T(8,128)(2,1)} %copy-done.18), channel_id=1, source_target_pairs={{1,0},{3,2},{5,4},{7,6},{9,8},{11,10},{13,12},{15,14},{17,16},{19,... | collective-permute-start | bytes 3145736 | tf_op jit(solution)/shard_map/ppermute | solution.py:1029
  399.4 5.9 %copy-start.38 = (f32[64,8]{0,1:T(8,128)}, f32[64,8]{0,1:T(8,128)S(1)}, u32[]{:S(2)}) copy-start(f32[64,8]{0,1:T(8,128)S(1)} %fusion.13) | copy-start | bytes 6148
  400.6 12.3 %collective-permute-start.23 = (bf16[4,64,512]{2,1,0:T(8,128)(2,1)S(1)}, bf16[4,64,512]{2,1,0:T(8,128)(2,1)S(1)}, u32[]{:S(2)}, u32[]{:S(2)}) collective-permute-start(bf16[4,64,512]{2,1,0:T(8,128)(2,1)S(1)} %slice_bitcast_fusion.20), channel_id=1, source_target_pairs={{0,4},{4,0},{1,5},{5,1},{2,6},{6,2},{3,7},{7,3},{8,12},{12,8},{9,1... | collective-permute-start | bytes 786440 | tf_op jit(solution)/shard_map/ppermute | solution.py:853
  405.3 7.1 %copy-start.27 = (bf16[2,2,4,64,1536]{4,3,2,1,0:T(8,128)(2,1)}, bf16[2,2,4,64,1536]{4,3,2,1,0:T(8,128)(2,1)S(1)}, u32[]{:S(2)}) copy-start(bf16[2,2,4,64,1536]{4,3,2,1,0:T(8,128)(2,1)S(1)} %add_convert_fusion) | copy-start | bytes 9437188
  406.3 6.0 %slice-start = ((f32[64,8]{0,1:T(8,128)}), f32[64,4]{0,1:T(4,128)S(1)}, s32[]{:S(2)}) async-start(f32[64,8]{0,1:T(8,128)} %copy-done.38), calls=%async_computation.6 | async-start | bytes 4096 | tf_op jit(solution)/shard_map/slice | solution.py:1082
  407.5 31.7 %collective-permute-start.16 = (bf16[2,4,32,1536]{3,2,1,0:T(8,128)(2,1)}, bf16[2,4,32,1536]{3,2,1,0:T(8,128)(2,1)}, u32[]{:S(2)}, u32[]{:S(2)}) collective-permute-start(bf16[2,4,32,1536]{3,2,1,0:T(8,128)(2,1)} %slice_bitcast_fusion.2), channel_id=1, source_target_pairs={{0,1},{1,0},{2,3},{3,2},{4,5},{5,4},{6,7},{7,6},{8,9},{9,8},{10,11... | collective-permute-start | bytes 2359304 | tf_op jit(solution)/shard_map/ppermute | solution.py:853
  409.9 29.4 %collective-permute-start.18 = (bf16[2,4,32,1536]{3,2,1,0:T(8,128)(2,1)}, bf16[2,4,32,1536]{3,2,1,0:T(8,128)(2,1)}, u32[]{:S(2)}, u32[]{:S(2)}) collective-permute-start(bf16[2,4,32,1536]{3,2,1,0:T(8,128)(2,1)} %slice_bitcast_fusion), channel_id=1, source_target_pairs={{0,4},{4,0},{1,5},{5,1},{2,6},{6,2},{3,7},{7,3},{8,12},{12,8},{9,1... | collective-permute-start | bytes 2359304 | tf_op jit(solution)/shard_map/ppermute | solution.py:853
  432.8 21.6 %collective-permute-start.24 = (bf16[2,2,2,2,64,128]{5,4,3,2,1,0:T(8,128)(2,1)S(1)}, bf16[2,2,2,2,64,128]{5,4,3,2,1,0:T(8,128)(2,1)}, u32[]{:S(2)}, u32[]{:S(2)}) collective-permute-start(bf16[2,2,2,2,64,128]{5,4,3,2,1,0:T(8,128)(2,1)S(1)} %get-tuple-element.104), channel_id=1, source_target_pairs={{0,2},{2,0},{1,3},{3,1},{4,6},{6,4},{5,7},{7,5},{8,10},{10,8},{9,1... | collective-permute-start | bytes 786440 | tf_op jit(solution)/shard_map/ppermute | solution.py:853
  441.6 7.8 %collective-permute-start.19 = (bf16[4,32,1536]{2,1,0:T(8,128)(2,1)S(1)}, bf16[4,32,1536]{2,1,0:T(8,128)(2,1)S(1)}, u32[]{:S(2)}, u32[]{:S(2)}) collective-permute-start(bf16[4,32,1536]{2,1,0:T(8,128)(2,1)S(1)} %slice_bitcast_fusion.16), channel_id=1, source_target_pairs={{0,1},{1,0},{2,3},{3,2},{4,5},{5,4},{6,7},{7,6},{8,9},{9,8},{10,11... | collective-permute-start | bytes 1179656 | tf_op jit(solution)/shard_map/ppermute | solution.py:853
  441.7 7.8 %collective-permute-start.17 = (bf16[4,32,1536]{2,1,0:T(8,128)(2,1)S(1)}, bf16[4,32,1536]{2,1,0:T(8,128)(2,1)S(1)}, u32[]{:S(2)}, u32[]{:S(2)}) collective-permute-start(bf16[4,32,1536]{2,1,0:T(8,128)(2,1)S(1)} %slice_bitcast_fusion.18), channel_id=1, source_target_pairs={{0,4},{4,0},{1,5},{5,1},{2,6},{6,2},{3,7},{7,3},{8,12},{12,8},{9,1... | collective-permute-start | bytes 1179656 | tf_op jit(solution)/shard_map/ppermute | solution.py:853
  449.7 8.8 %collective-permute-start.20 = (bf16[2,64,1536]{2,1,0:T(8,128)(2,1)S(1)}, bf16[2,64,1536]{2,1,0:T(8,128)(2,1)}, u32[]{:S(2)}, u32[]{:S(2)}) collective-permute-start(bf16[2,64,1536]{2,1,0:T(8,128)(2,1)S(1)} %slice_bitcast_fusion.14), channel_id=1, source_target_pairs={{0,8},{8,0},{16,24},{24,16},{1,9},{9,1},{17,25},{25,17},{2,10},{10... | collective-permute-start | bytes 1179656 | tf_op jit(solution)/shard_map/ppermute | solution.py:1057
  459.6 6.6 %collective-permute-start.21 = (bf16[64,1536]{1,0:T(8,128)(2,1)S(1)}, bf16[64,1536]{1,0:T(8,128)(2,1)S(1)}, u32[]{:S(2)}, u32[]{:S(2)}) collective-permute-start(bf16[64,1536]{1,0:T(8,128)(2,1)S(1)} %slice_bitcast_fusion.22), channel_id=1, source_target_pairs={{0,16},{16,0},{8,24},{24,8},{1,17},{17,1},{9,25},{25,9},{2,18},{18... | collective-permute-start | bytes 589832 | tf_op jit(solution)/shard_map/ppermute | solution.py:1057
  (12 other events, 14.6 us)
Sparse Core Ops, SparseCore 0:
  266.7 37.2 reduce-scatter.5
  356.9 42.3 reduce-scatter.7
  413.9 17.1 reduce-scatter.3

commit v2 on v1

--- a/solution.py
+++ b/solution.py
@@ -296,6 +296,7 @@
 F32 = jnp.float32
 TILE = 128
 MIB = 1024 * 1024
+HINT = 0.25
 
 
 def mm(left, right):
@@ -311,9 +312,12 @@
 
 
 def call_kernel(
-    kernel, info, args, *, name, grid, ins, outs, shapes, scratch=(), vmem=48, cost=None, after=()
+    kernel, info, args, *, name, grid, ins, outs, shapes, scratch=(), vmem=60, cost=None, after=(),
+    onto=(),
 ):
     flops, moved = cost
+    aliases = {1 + len(args) + len(after) + k: k for k in range(len(onto))}
+    after = (*after, *onto)
     count, unread = len(args), len(after)
 
     def run(info, *refs):
@@ -327,10 +331,13 @@
             num_scalar_prefetch=1, grid=grid, in_specs=ins, out_specs=outs, scratch_shapes=scratch
         ),
         out_shape=shapes,
+        input_output_aliases=aliases,
         compiler_params=pltpu.CompilerParams(
             dimension_semantics=("arbitrary",) * len(grid), vmem_limit_bytes=vmem * MIB
         ),
-        cost_estimate=pl.CostEstimate(flops=int(flops), bytes_accessed=int(moved), transcendentals=0),
+        cost_estimate=pl.CostEstimate(
+            flops=int(flops * HINT), bytes_accessed=int(moved * HINT), transcendentals=0
+        ),
         name=name,
     )(info, *args)
 
@@ -457,44 +464,47 @@
     return own_ref[(block - 1) * TILE : (block + 1) * TILE, own_at : own_at + TILE]
 
 
-def attend_kernel(scale, info, qkv_ref, kvh_ref, ctx_ref, lse_ref):
+def attend_kernel(scale, block, info, qkv_ref, kvh_ref, ctx_ref, lse_ref):
     clip = pl.program_id(0)
-    rows, width = ctx_ref.shape
-    for block in range(rows // TILE):
-        live = info[3] + block * TILE < info[LEN0 + clip]
-        at_rows = slice(block * TILE, (block + 1) * TILE)
-
-        @pl.when(live)
-        def _():
-            bias = window_bias(info, clip, block)
-            lane = lax.broadcasted_iota(jnp.int32, (TILE, TILE), 1)
-            totals = jnp.zeros((TILE, TILE), F32)
-            for pair in range(width // TILE):
-                at = pair * TILE
-                queries = two_heads(qkv_ref[at_rows, at : at + TILE])
-                keys = key_window(kvh_ref, qkv_ref, block, at, width + at)
-                values = key_window(kvh_ref, qkv_ref, block, width + at, 2 * width + at)
-                scores = mm_t(queries, keys) * scale + bias
-                top = jnp.max(scores, axis=1, keepdims=True)
-                exponent = jnp.exp(scores - top)
-                total = jnp.sum(exponent, axis=1, keepdims=True)
-                weights = (exponent * (1.0 / total)).astype(BF)
-                ctx_ref[at_rows, at : at + TILE] = one_row(mm(weights, values)).astype(BF)
-                log_total = top + jnp.log(total)
-                totals = jnp.where(lane == 2 * pair, log_total[:TILE], totals)
-                totals = jnp.where(lane == 2 * pair + 1, log_total[TILE:], totals)
-            lse_ref[at_rows, :] = totals
-
-        @pl.when(jnp.logical_not(live))
-        def _():
-            ctx_ref[at_rows, :] = jnp.zeros((TILE, width), BF)
-            lse_ref[at_rows, :] = jnp.zeros((TILE, TILE), F32)
+    width = ctx_ref.shape[1]
+    at_rows = slice(block * TILE, (block + 1) * TILE)
+    live = info[3] + block * TILE < info[LEN0 + clip]
+
+    @pl.when(live)
+    def _():
+        bias = window_bias(info, clip, block)
+        lane = lax.broadcasted_iota(jnp.int32, (TILE, TILE), 1)
+        totals = jnp.zeros((TILE, TILE), F32)
+        for pair in range(width // TILE):
+            at = pair * TILE
+            queries = two_heads(qkv_ref[at_rows, at : at + TILE])
+            keys = key_window(kvh_ref, qkv_ref, block, at, width + at)
+            values = key_window(kvh_ref, qkv_ref, block, width + at, 2 * width + at)
+            scores = mm_t(queries, keys) * scale + bias
+            top = jnp.max(scores, axis=1, keepdims=True)
+            exponent = jnp.exp(scores - top)
+            total = jnp.sum(exponent, axis=1, keepdims=True)
+            weights = (exponent * (1.0 / total)).astype(BF)
+            ctx_ref[:, at : at + TILE] = one_row(mm(weights, values)).astype(BF)
+            log_total = top + jnp.log(total)
+            totals = jnp.where(lane == 2 * pair, log_total[:TILE], totals)
+            totals = jnp.where(lane == 2 * pair + 1, log_total[TILE:], totals)
+        lse_ref[...] = totals
+
+    @pl.when(jnp.logical_not(live))
+    def _():
+        ctx_ref[...] = jnp.zeros_like(ctx_ref)
+        lse_ref[...] = jnp.zeros_like(lse_ref)
+
+
+def attend_late_kernel(scale, info, qkv_ref, ctx_ref, lse_ref):
+    attend_kernel(scale, 1, info, qkv_ref, None, ctx_ref, lse_ref)
 
 
 def attend_back_kernel(
-    scale, info, qkv_ref, kvh_ref, dctx_ref, lse_ref, tab_ref, tabh_ref, md_ref, mdh_ref, dk_acc, dv_acc
+    scale, first_clip, info, qkv_ref, kvh_ref, dctx_ref, lse_ref, tab_ref, tabh_ref, md_ref, mdh_ref, dk_acc, dv_acc
 ):
-    clip = pl.program_id(0)
+    clip = pl.program_id(0) + first_clip
     rows, width = dctx_ref.shape
     blocks = rows // TILE
     first_live = info[3] < info[LEN0 + clip]
@@ -579,24 +589,17 @@
     return (place < info[LEN0 + clip]).astype(F32)
 
 
-def output_kernel(info, x_ref, ct_ref, att_ref, ba_ref, bb_ref, gb_ref, out_ref, sum_ref):
+def output_kernel(info, x_ref, att_ref, ba_ref, bb_ref, gb_ref, out_ref):
     r = pl.program_id(0)
     valid = row_valid(info, r, x_ref.shape[0])
-    branch = ba_ref[...].astype(F32) + bb_ref[...].astype(F32)
+    branch = ba_ref[...].astype(F32) + bb_ref[0].astype(F32)
     middle = x_ref[...].astype(F32) + gb_ref[2:3, :] * att_ref[...]
     out_ref[...] = ((middle + gb_ref[3:4, :] * branch) * valid).astype(BF)
-    part = column_sum(ct_ref[...].astype(F32) * valid * branch)
-
-    @pl.when(r == 0)
-    def _():
-        sum_ref[...] = jnp.zeros_like(sum_ref)
-
-    sum_ref[0:1, :] += part
 
 
 def out_back_kernel(
-    info, sa_ref, sb_ref, att_ref, x_ref, ct_ref, ctx_ref, w_ref, gb_ref,
-    delta_ref, dctx_ref, keep_ref, send_ref, sum_ref, acc,
+    info, sa_ref, sb_ref, ba_ref, bb_ref, att_ref, x_ref, ct_ref, ctx_ref, w_ref, gb_ref,
+    delta_ref, dctx_ref, out_ref, sum_ref, acc,
 ):
     r = pl.program_id(0)
     rows, width = x_ref.shape
@@ -614,9 +617,12 @@
         attended = att_ref[...]
         middle = x_ref[...].astype(F32) + gb_ref[2:3, :] * attended
         normal, inverse = norm_stats(middle)
-        second = sa_ref[...].astype(F32) + sb_ref[...].astype(F32)
+        second = sa_ref[...].astype(F32) + sb_ref[0].astype(F32)
         back = norm_back(second, normal, inverse, gb_ref[1:2, :])
-        middle_delta = ct_ref[...].astype(F32) * valid + back
+        output_delta = ct_ref[...].astype(F32) * valid
+        branch = ba_ref[...].astype(F32) + bb_ref[0].astype(F32)
+        sum_ref[3:4, :] += column_sum(output_delta * branch)
+        middle_delta = output_delta + back
         delta_ref[...] = middle_delta
         attended_delta = (middle_delta * gb_ref[2:3, :]).astype(BF)
         dctx_ref[...] = mm_t(attended_delta, w_ref[...]).astype(BF)
@@ -632,32 +638,33 @@
 
     @pl.when(r == pl.num_programs(0) - 1)
     def _():
-        half = width // 2
-        for x in range(2):
-            col = pl.multiple_of(((info[0] + x) % 2) * half, TILE)
-            for y in range(2):
-                for z in range(4):
-                    base = z * 256 + ((info[1] + y) % 2) * 128
-                    for c, ref in ((0, keep_ref), (1, send_ref)):
-                        row = pl.multiple_of(base + ((info[2] + c) % 2) * 64, 64)
-                        ref[x, y, z] = acc[pl.ds(row, 64), pl.ds(col, half)].astype(BF)
-
-
-def qkv_grad_kernel(info, n_ref, md_ref, nh_ref, mdh_ref, keep_ref, send_ref, acc):
+        out_ref[...] = acc[...].astype(BF)
+
+
+def qkv_grad_kernel(info, n_ref, md_ref, nh_ref, mdh_ref, *refs):
     t = pl.program_id(0)
+    acc = refs[4]
     acc[...] = t_mm(n_ref[...], md_ref[...])
 
     @pl.when(jnp.logical_and(info[0] > 0, t >= 2))
     def _():
         acc[...] += t_mm(nh_ref[...], mdh_ref[...])
 
-    for y in range(2):
-        for z in range(4):
-            z_there = (info[4] // 2 + z // 2) % 2 * 2 + (info[4] + z) % 2
-            base = z_there * 256 + ((info[1] + y) % 2) * 128
-            for c, ref in ((0, keep_ref), (1, send_ref)):
-                row = pl.multiple_of(base + ((info[2] + c) % 2) * 64, 64)
-                ref[0, y, z] = acc[pl.ds(row, 64), :].astype(BF)
+    def put(left):
+        for y in range(2):
+            for z in range(4):
+                z_there = (info[4] // 2 + z // 2) % 2 * 2 + (info[4] + z) % 2
+                base = z_there * 256 + ((info[1] + y) % 2) * 128
+                for c in range(2):
+                    row = pl.multiple_of(base + ((info[2] + c) % 2) * 64, 64)
+                    value = acc[pl.ds(row, 64), :].astype(BF)
+                    if left:
+                        refs[2 * c][0, y, z] = value
+                    else:
+                        refs[2 * c + 1][y, 0, 0, z] = value
+
+    pl.when(t % 3 == 0)(functools.partial(put, True))
+    pl.when(t % 3 > 0)(functools.partial(put, False))
 
 
 def first_back_kernel(info, md_ref, w_ref, x_ref, delta_ref, gb_ref, out_ref, sum_ref):
@@ -682,7 +689,7 @@
         out_ref[...] = jnp.zeros_like(out_ref)
 
 
-def first_halo_kernel(info, mdh_ref, wk_ref, wv_ref, x_ref, out_ref, sum_ref):
+def first_halo_kernel(first_clip, info, mdh_ref, wk_ref, wv_ref, x_ref, out_ref, sum_ref):
     r = pl.program_id(0)
     width = x_ref.shape[1]
 
@@ -690,7 +697,7 @@
     def _():
         sum_ref[...] = jnp.zeros_like(sum_ref)
 
-    live = jnp.logical_and(info[0] > 0, info[3] < info[LEN0 + r])
+    live = jnp.logical_and(info[0] > 0, info[3] < info[LEN0 + first_clip + r])
 
     @pl.when(live)
     def _():
@@ -705,15 +712,17 @@
         out_ref[...] = jnp.zeros_like(out_ref)
 
 
-def input_grad_kernel(info, part_ref, halo_ref, x_ref, gb_ref, out_ref):
+def input_grad_kernel(first_clips, info, part_ref, halo_a, halo_b, x_ref, gb_ref, out_ref):
+    r = pl.program_id(0)
     rows = part_ref.shape[0]
-    split = rows - halo_ref.shape[0]
+    split = rows - halo_a.shape[0]
     out_ref[:split, :] = part_ref[:split, :].astype(BF)
 
     @pl.when(info[0] == 0)
     def _():
         normal, inverse = norm_stats(x_ref[split:, :].astype(F32))
-        back = norm_back(halo_ref[...].astype(F32), normal, inverse, gb_ref[0:1, :])
+        halo = jnp.where(r < first_clips, halo_a[...], halo_b[...])
+        back = norm_back(halo.astype(F32), normal, inverse, gb_ref[0:1, :])
         out_ref[split:, :] = (part_ref[split:, :] + back).astype(BF)
 
     @pl.when(info[0] > 0)
@@ -721,36 +730,73 @@
         out_ref[split:, :] = part_ref[split:, :].astype(BF)
 
 
-def ffn_kernel(c, z0, first, x_leads, half, info, n_own, n_other, b_own, b_other, *rest):
+def ffn_kernel(c, first, half, info, n_own, n_other, b_own, b_other, *rest):
     if not first:
-        br_in, se_in, *rest = rest
-    wg_hbm, wu_hbm, wd_hbm, br_ref, se_ref, keep_ref, send_ref, wg, wu, wd, ag, au, ad, sems = rest
+        earlier, rest = rest[:3], rest[3:]
+    wg_hbm, wu_hbm, wd_hbm, *rest = rest
+    sums, rest = rest[:3], rest[3:]
+    packs, rest = (rest[0:2], rest[2:4]), rest[4:]
+    wg, wu, wd, ag, au, ad, n_buf, b_buf, sems, row_sems = rest
     r = pl.program_id(0)
-
-    def copies():
-        for x in range(2):
-            for q in range(2):
-                k = x * 2 + q
-                d = ((info[0] + x) % 2 * 2 + z0) * 4 + (info[1] + q) % 2 * 2 + info[2]
-                src = pl.ds(pl.multiple_of(d * 256 + c * TILE, TILE), TILE)
-                dst = pl.ds(k * TILE, TILE)
-                yield pltpu.make_async_copy(wg_hbm.at[:, src], wg.at[:, dst], sems.at[0, k])
-                yield pltpu.make_async_copy(wu_hbm.at[:, src], wu.at[:, dst], sems.at[1, k])
-                yield pltpu.make_async_copy(wd_hbm.at[src, :], wd.at[dst, :], sems.at[2, k])
+    steps = pl.num_programs(0)
+    block_rows = n_buf.shape[1]
+
+    def weight_copies(kind):
+        hbm, vmem = ((wg_hbm, wg), (wu_hbm, wu), (wd_hbm, wd))[kind]
+        for k in range(8):
+            z0, x, q = k // 4, k // 2 % 2, k % 2
+            d = ((info[0] + x) % 2 * 2 + z0) * 4 + (info[1] + q) % 2 * 2 + info[2]
+            src = pl.ds(pl.multiple_of(d * 256 + c * TILE, TILE), TILE)
+            dst = pl.ds(k * TILE, TILE)
+            if kind < 2:
+                yield pltpu.make_async_copy(hbm.at[:, src], vmem.at[:, dst], sems.at[kind, k])
+            else:
+                yield pltpu.make_async_copy(hbm.at[src, :], vmem.at[dst, :], sems.at[kind, k])
+
+    def row_copies(step, sources):
+        src = pl.ds(pl.multiple_of(step % half * block_rows, block_rows), block_rows)
+        for i, (hbm, vmem) in enumerate(zip(sources, (n_buf, b_buf))):
+            yield pltpu.make_async_copy(
+                hbm.at[src, :], vmem.at[step % 2], row_sems.at[i, step % 2]
+            )
+
+    def start_rows(step):
+        @pl.when(step < half)
+        def _():
+            for copy in row_copies(step, (n_own, b_own)):
+                copy.start()
+
+        @pl.when(step >= half)
+        def _():
+            for copy in row_copies(step, (n_other, b_other)):
+                copy.start()
 
     @pl.when(r == 0)
     def _():
-        for copy in copies():
-            copy.start()
-        for copy in copies():
-            copy.wait()
-
-    own = r < half
-    normed = jnp.where(own, n_own[...], n_other[...])
-    delta = jnp.where(own, b_own[...], b_other[...])
-    gate = mm(normed, wg[...])
-    upward = mm(normed, wu[...])
-    hidden_delta = mm_t(delta, wd[...])
+        start_rows(r)
+        for kind in range(3):
+            for copy in weight_copies(kind):
+                copy.start()
+        for acc in (ag, au, ad):
+            acc[...] = jnp.zeros_like(acc)
+
+    @pl.when(r + 1 < steps)
+    def _():
+        start_rows(r + 1)
+
+    for copy in row_copies(r, (n_own, b_own)):
+        copy.wait()
+
+    @pl.when(r == 0)
+    def _():
+        for kind in range(3):
+            for copy in weight_copies(kind):
+                copy.wait()
+
+    normed, delta = n_buf.at[r % 2], b_buf.at[r % 2]
+    gate = mm(normed[...], wg[...])
+    upward = mm(normed[...], wu[...])
+    hidden_delta = mm_t(delta[...], wd[...])
     sigmoid = jax.nn.sigmoid(gate)
     active = gate * sigmoid
     hidden = (active * upward).astype(BF)
@@ -759,76 +805,70 @@
     branch = mm(hidden, wd[...])
     second = mm_t(gate_delta, wg[...]) + mm_t(up_delta, wu[...])
     if not first:
-        branch = branch + br_in[...].astype(F32)
-        second = second + se_in[...].astype(F32)
-    br_ref[...] = branch.astype(BF)
-    se_ref[...] = second.astype(BF)
-    grads = (t_mm(normed, gate_delta), t_mm(normed, up_delta), t_mm(delta, hidden))
-
-    @pl.when(r == 0)
-    def _():
-        for acc, grad in zip((ag, au, ad), grads):
-            acc[...] = grad
-
-    @pl.when(r > 0)
-    def _():
-        for acc, grad in zip((ag, au, ad), grads):
-            acc[...] += grad
+        branch = branch + jnp.where(r < half, earlier[0][...], earlier[2][0]).astype(F32)
+        second = second + jnp.where(r < half, earlier[1][...], earlier[2][1]).astype(F32)
+    branch, second = branch.astype(BF), second.astype(BF)
+    sums[0][...] = branch
+    sums[1][...] = second
+    sums[2][0] = branch
+    sums[2][1] = second
+    ag[...] += t_mm(normed[...], gate_delta)
+    au[...] += t_mm(normed[...], up_delta)
+    ad[...] += t_mm(delta[...], hidden)
 
     @pl.when(r == pl.num_programs(0) - 1)
     def _():
-        def put(x, y, tile, value):
-            lead, other = (x, y) if x_leads else (y, x)
-            ref = send_ref if lead else keep_ref
-            ref[other, tile * TILE : (tile + 1) * TILE, :] = value.astype(BF)
-
-        def block(i, n=1):
-            return slice(i * TILE, (i + n) * TILE)
-
-        for x in range(2):
-            for y in range(2):
-                for z in range(4):
-                    here, there = block(z * 2 + y), block(z * 2 + 1 - y)
-                    for q in range(2):
-                        cols, turned = block(x * 2 + q), block(x * 2 + 1 - q)
-                        for i, acc in enumerate((ag, au)):
-                            value = jnp.where(info[1] == 0, acc[here, cols], acc[there, turned])
-                            put(x, y, 8 * i + z * 2 + q, value)
-                for z1 in range(2):
-                    for dq in range(4):
-                        value = jnp.where(
-                            info[0] == 0,
-                            ad[block(x * 4 + dq), block(z1 * 2 + y)],
-                            ad[block((1 - x) * 4 + dq), block((1 - z1) * 2 + y)],
-                        )
-                        put(x, y, 16 + z1 * 4 + dq, value)
-
-
-def ffn_call(c, z0, x_leads, info, pieces, weights, previous, after=(), block_rows=512):
+        def flip(bit, own):
+            return (bit + own) % 2
+
+        def tile(acc, row, col):
+            row = pl.multiple_of(row * TILE, TILE)
+            col = pl.multiple_of(col * TILE, TILE)
+            return acc[pl.ds(row, TILE), pl.ds(col, TILE)].astype(BF)
+
+        x_own, y_own, z1_own, z0_own = info[0], info[1], info[4] // 2, info[4] % 2
+        for u in range(2):
+            for x in range(2):
+                for y in range(2):
+                    lead, other = (x, y) if u == 0 else (y, x)
+                    ref = packs[u][lead]
+
+                    def put(at, value):
+                        ref[other, at * TILE : (at + 1) * TILE, :] = value
+
+                    for z1 in range(2):
+                        for z0 in range(2):
+                            z = flip(z1, z1_own) * 2 + flip(z0, z0_own)
+                            at = 4 * z1 if z0 == 0 else 16 + 4 * z1
+                            for i, acc in enumerate((ag, au)):
+                                for q in range(2):
+                                    col = u * 4 + x * 2 + flip(q, y_own)
+                                    put(at + 2 * i + q, tile(acc, z * 2 + flip(y, y_own), col))
+                        col = flip(u, z0_own) * 4 + flip(flip(z1, z1_own), x_own) * 2 + y
+                        for dq in range(4):
+                            put(8 + 4 * z1 + dq, tile(ad, flip(x, x_own) * 4 + dq, col))
+
+
+def ffn_call(c, info, pieces, weights, previous, after=(), block_rows=256):
     rows, width = pieces[0].shape
     half = rows // block_rows
     first = previous is None
-    hidden = 4 * TILE
-
-    def spec(index):
-        return pl.BlockSpec((block_rows, width), index)
-
-    own = spec(lambda r, info: (jnp.minimum(r, half - 1), 0))
-    other = spec(lambda r, info: (jnp.maximum(r - half, 0), 0))
-    every = spec(lambda r, info: (r, 0))
+    hidden = 8 * TILE
+    own = pl.BlockSpec((block_rows, width), lambda r, info: (jnp.minimum(r, half), 0))
+    other = pl.BlockSpec((2, block_rows, width), lambda r, info: (0, jnp.maximum(r - half, 0), 0))
     packed = (2, 24 * TILE, TILE)
+    pack = pl.BlockSpec(packed, lambda r, info: (0, 0, 0), pipeline_mode=pl.Buffered(1))
     extra = [] if first else list(previous)
+    anywhere = pl.BlockSpec(memory_space=pl.ANY)
     return call_kernel(
-        functools.partial(ffn_kernel, c, z0, first, x_leads, half),
+        functools.partial(ffn_kernel, c, first, half),
         info,
         [*pieces, *extra, *weights],
         name="feed_forward",
         grid=(2 * half,),
-        ins=[own, other, own, other]
-        + [every] * len(extra)
-        + [pl.BlockSpec(memory_space=pl.ANY)] * 3,
-        outs=[every, every, whole_spec(packed), whole_spec(packed)],
-        shapes=[shape_of((2 * rows, width))] * 2 + [shape_of(packed)] * 2,
+        ins=[anywhere] * 4 + [own, own, other] * (len(extra) // 3) + [anywhere] * 3,
+        outs=[own, own, other] + [pack] * 4,
+        shapes=[shape_of((rows + block_rows, width))] * 2 + [shape_of((2, rows, width))] + [shape_of(packed)] * 4,
         scratch=[
             pltpu.VMEM((width, hidden), BF),
             pltpu.VMEM((width, hidden), BF),
@@ -836,9 +876,12 @@
             pltpu.VMEM((width, hidden), F32),
             pltpu.VMEM((width, hidden), F32),
             pltpu.VMEM((width, hidden), F32),
-            pltpu.SemaphoreType.DMA((3, 4)),
+            pltpu.VMEM((2, block_rows, width), BF),
+            pltpu.VMEM((2, block_rows, width), BF),
+            pltpu.SemaphoreType.DMA((3, 8)),
+            pltpu.SemaphoreType.DMA((2, 2)),
         ],
-        vmem=56,
+        vmem=60,
         cost=(18 * 2 * rows * width * hidden, 30 * MIB),
         after=after,
     )
@@ -847,6 +890,14 @@
 SWAP = [(0, 1), (1, 0)]
 Z_NEAR = [(0, 1), (1, 0), (2, 3), (3, 2)]
 Z_FAR = [(0, 2), (2, 0), (1, 3), (3, 1)]
+
+
+def meet(*values):
+    return lax.optimization_barrier(values)
+
+
+def later(values, *needed):
+    return lax.optimization_barrier((values, needed))[0]
 
 
 def swap(values, axis):
@@ -900,7 +951,6 @@
     places = start + jnp.arange(rows)
     valid = (places[None, :] < lengths[:, None]).astype(F32).reshape(count, 1)
     branch_delta = (tangent.astype(F32) * valid * gain_table[:, 3]).astype(BF)
-    branch_delta_other = swap(branch_delta, "core")
     table = jnp.concatenate([gain_table, bias_table, jnp.zeros((width, 2), F32)], axis=1).T
     seats = lax.axis_size("seq")
     own_turns = jnp.asarray(turn_table(0, seats * rows, head_dim))
@@ -919,6 +969,10 @@
     w_value = pl.BlockSpec((width, width), lambda r, info: (0, 2))
     w_out = whole_spec((width, width))
     sums = whole_spec((8, width))
+
+    def half_sums(part):
+        return pl.BlockSpec((1, rows, width), lambda r, info: (part, r, 0))
+
     grid = (clips,)
     mac = 2 * count * width * width
 
@@ -927,17 +981,29 @@
         ins=[own, w_qkv, gb, own_tab], outs=[qkv_rows, own],
         shapes=[shape_of((count, 3 * width)), shape_of((count, width))], cost=(3 * mac, 16 * MIB),
     )
+    def half_rows(width, part):
+        return pl.BlockSpec((TILE, width), lambda r, info: (2 * r + part, 0))
+
+    seen = [shape_of((count, width)), shape_of((count, TILE), F32)]
+    late = call_kernel(
+        functools.partial(attend_late_kernel, scale), info, [qkv], name="attend_late", grid=grid,
+        ins=[qkv_rows], outs=[half_rows(width, 1), half_rows(TILE, 1)], shapes=seen,
+        cost=(2 * mac, 8 * MIB),
+    )
+    halo, branch_delta = lax.optimization_barrier((halo, branch_delta))
+    branch_delta_other = swap(branch_delta, "core")
     kv_halo, normed_halo = call_kernel(
         halo_kernel, info, [halo, qkv_weight, qkv_weight, table, halo_turns], name="halo",
         grid=grid, ins=[halo_rows, w_key, w_value, gb, halo_tab],
         outs=[kv_rows, halo_rows],
         shapes=[shape_of((clips * TILE, 2 * width)), shape_of((clips * TILE, width))],
-        cost=(mac, 8 * MIB),
+        cost=(mac, 8 * MIB), after=late,
     )
     context, log_totals = call_kernel(
-        functools.partial(attend_kernel, scale), info, [qkv, kv_halo], name="attend", grid=grid,
-        ins=[qkv_rows, kv_rows], outs=[own, rows_spec(rows, TILE)],
-        shapes=[shape_of((count, width)), shape_of((count, TILE), F32)], cost=(4 * mac, 12 * MIB),
+        functools.partial(attend_kernel, scale, 0), info, [qkv, kv_halo], name="attend_early",
+        grid=grid, ins=[half_rows(3 * width, 0), kv_rows],
+        outs=[half_rows(width, 0), half_rows(TILE, 0)], shapes=seen,
+        cost=(2 * mac, 12 * MIB), onto=late,
     )
     attended, normed_two = call_kernel(
         out_kernel, info, [context, flat, out_weight, table], name="project", grid=grid,
@@ -948,92 +1014,113 @@
 
     pieces = (normed_two, normed_two_other, branch_delta, branch_delta_other)
     weights = (gate_weight, up_weight, down_weight)
-    units = [(0, 0), (0, 1), (1, 0), (1, 1)]
-    axes = [("seq", "y"), ("y", "seq")] * 2
-    previous, first_sums = None, []
-
-    def run_ffn(i, after):
-        c, z0 = units[i]
-        *state, keep, send = ffn_call(
-            c, z0, axes[i][0] == "seq", info, pieces, weights, previous, after
+    def start_pair(keeps):
+        (keep_a, send_a), (keep_b, send_b) = keeps
+        return (keep_a, swap(send_a, "seq")), (keep_b, swap(send_b, "y"))
+
+    def second_pair(totals):
+        (stay_a, go_a), (stay_b, go_b) = totals
+        return (stay_a, swap(go_a, "y")), (stay_b, swap(go_b, "seq"))
+
+    def halves(pairs):
+        return [tuple(plus(keep[k], came[k]) for k in range(2)) for keep, came in pairs]
+
+    def near_pair(pairs):
+        a, b = (plus(stay, came).reshape(24, TILE, TILE) for stay, came in pairs)
+        keep, send = jnp.concatenate([a[:16], b[:8]]), jnp.concatenate([a[16:], b[8:]])
+        return keep, lax.ppermute(send, "z", Z_NEAR)
+
+    def far_pair(pair):
+        total = plus(*pair).reshape(3, 2, 4, TILE, TILE)
+        return total[:, 0], lax.ppermute(total[:, 1], "z", Z_FAR)
+
+    def run_ffn(c, previous, after):
+        *state, keep_a, send_a, keep_b, send_b = ffn_call(
+            c, info, pieces, weights, previous, after
         )
-        return state, keep, swap(send, axes[i][0])
-
-    def last_sum(total, i):
-        return plus(total[0], swap(total[1], axes[i][1])).reshape(24, TILE, TILE)
-
-    def z_sum(parts):
-        gates = [
-            part[8 * i : 8 * i + 8].reshape(4, 2, TILE, TILE) for part in parts for i in range(2)
-        ]
-        downs = jnp.stack([part[16:].reshape(2, 4, TILE, TILE) for part in parts], axis=1)
-        return scatter_z(jnp.concatenate([*gates, downs.reshape(4, 4, TILE, TILE)], axis=1))
-
-    previous, keep_0, came_0 = run_ffn(0, ())
-    previous, keep_1, came_1 = run_ffn(1, ())
-    previous, keep_2, came_2 = run_ffn(2, (came_0,))
-    total_0 = plus(keep_0, came_0)
-    previous, keep_3, came_3 = run_ffn(3, (total_0, came_1))
-    total_1 = plus(keep_1, came_1)
-    part_0 = last_sum(total_0, 0)
-    branch, second = previous
-    second_other = swap(second[count:], "core")
-    branch_other = swap(branch[count:], "core")
-
-    packed = (2, 2, 4, 64, width // 2)
-    middle_delta, context_delta, out_keep, out_send, sums_two = call_kernel(
+        return state, ((keep_a, send_a), (keep_b, send_b))
+
+    previous, grads_0 = run_ffn(0, None, ())
+    moved_0 = start_pair(grads_0)
+    (branch, second, sums_sent), grads_1 = run_ffn(1, previous, ())
+    branch, second, sums_sent, grads_1, moved_0 = meet(branch, second, sums_sent, grads_1, moved_0)
+    sums_other = swap(sums_sent, "core")
+    grads_1, sums_other = meet(grads_1, sums_other)
+    totals_0 = halves(moved_0)
+    moved_0 = second_pair(totals_0)
+    moved_1 = start_pair(grads_1)
+
+    middle_delta, context_delta, out_grad, sums_two = call_kernel(
         out_back_kernel, info,
-        [second, second_other, attended, flat, tangent, context, out_weight, table],
+        [second, sums_other, branch, sums_other, attended, flat, tangent, context, out_weight, table],
         name="project_back", grid=grid,
-        ins=[own, own, own, own, own, own, w_out, gb],
-        outs=[own, own, whole_spec(packed), whole_spec(packed), sums],
+        ins=[own, half_sums(1), own, half_sums(0), own, own, own, own, w_out, gb],
+        outs=[own, own, w_out, sums],
         shapes=[
-            shape_of((count, width), F32), shape_of((count, width)), shape_of(packed),
-            shape_of(packed), shape_of((8, width), F32),
+            shape_of((count, width), F32), shape_of((count, width)), shape_of((width, width)),
+            shape_of((8, width), F32),
         ],
-        scratch=[pltpu.VMEM((width, width), F32)], cost=(2 * mac, 24 * MIB),
-        after=(total_1, came_2),
-    )
-    total_2 = plus(keep_2, came_2)
-    part_1 = last_sum(total_1, 1)
-    out_came = swap(out_send, "core")
-
-    output, sums_out = call_kernel(
-        output_kernel, info, [flat, tangent, attended, branch, branch_other, table],
-        name="output", grid=grid, ins=[own, own, own, own, own, gb], outs=[own, sums],
-        shapes=[shape_of((count, width)), shape_of((8, width), F32)], cost=(0, 14 * MIB),
-        after=(part_0, total_2, came_3),
-    )
-    total_3 = plus(keep_3, came_3)
-    z_0 = z_sum((part_0, part_1))
-    out_total = plus(out_keep, out_came)
-    out_came = swap(out_total[1], "seq")
-
-    mixed_delta, mixed_halo = call_kernel(
-        functools.partial(attend_back_kernel, scale), info,
-        [qkv, kv_halo, context_delta, log_totals, own_turns, halo_turns], name="attend_back", grid=grid,
-        ins=[qkv_rows, kv_rows, own, rows_spec(rows, TILE), own_tab, halo_tab],
-        outs=[qkv_rows, kv_rows],
-        shapes=[shape_of((count, 3 * width)), shape_of((clips * TILE, 2 * width))],
-        scratch=[pltpu.VMEM((rows + TILE, width), F32), pltpu.VMEM((rows + TILE, width), F32)],
-        cost=(10 * mac, 24 * MIB), after=(total_3, out_total, part_1, sums_out),
-    )
-    part_2, part_3 = last_sum(total_2, 2), last_sum(total_3, 3)
-    out_total = plus(out_total[0], out_came)
-    out_grad = scatter_z(plus(out_total[0], swap(out_total[1], "y"))).astype(F32)
-    first_halo, sums_halo = call_kernel(
-        first_halo_kernel, info, [mixed_halo, qkv_weight, qkv_weight, halo], name="first_halo",
-        grid=grid, ins=[kv_rows, w_key, w_value, halo_rows], outs=[halo_rows, sums],
-        shapes=[shape_of((clips * TILE, width)), shape_of((8, width), F32)], cost=(mac, 8 * MIB),
-    )
-    first_back = lax.ppermute(first_halo, "seq", [(1, 0)])
+        scratch=[pltpu.VMEM((width, width), F32)], cost=(2 * mac, 24 * MIB), after=tuple(t for pair in totals_0 for t in pair),
+    )
+    out_grad = lax.psum_scatter(out_grad, ("z", "y", "core"), scatter_dimension=0, tiled=True)
+
+    def attend_back(first_clip, onto, after, taken):
+        def at(rows, width):
+            return pl.BlockSpec((rows, width), lambda r, info: (r + first_clip, 0))
+
+        return call_kernel(
+            functools.partial(attend_back_kernel, scale, first_clip), info,
+            [qkv, kv_halo, context_delta, log_totals, own_turns, halo_turns],
+            name="attend_back", grid=(taken,),
+            ins=[
+                at(rows, 3 * width), at(TILE, 2 * width), at(rows, width), at(rows, TILE),
+                own_tab, halo_tab,
+            ],
+            outs=[at(rows, 3 * width), at(TILE, 2 * width)],
+            shapes=[shape_of((count, 3 * width)), shape_of((clips * TILE, 2 * width))],
+            scratch=[pltpu.VMEM((rows + TILE, width), F32), pltpu.VMEM((rows + TILE, width), F32)],
+            cost=(2.5 * mac * taken, 6 * MIB * taken), after=after, onto=onto,
+        )
+
+    some = clips - 1
+
+    def first_halo(first_clip, mixed_halo, after, taken):
+        def at(width):
+            return pl.BlockSpec((TILE, width), lambda r, info: (r + first_clip, 0))
+
+        return call_kernel(
+            functools.partial(first_halo_kernel, first_clip), info,
+            [mixed_halo, qkv_weight, qkv_weight, halo], name="first_halo", grid=(taken,),
+            ins=[at(2 * width), w_key, w_value, at(width)], outs=[halo_rows, sums],
+            shapes=[shape_of((taken * TILE, width)), shape_of((8, width), F32)],
+            cost=(mac // 4 * taken, 6 * MIB), after=after,
+        )
+
+    mixed = attend_back(0, (), (), some)
+    mixed, moved_0, moved_1 = meet(mixed, moved_0, moved_1)
+    totals_1 = halves(moved_1)
+    moved_1 = second_pair(totals_1)
+    near_0 = near_pair(moved_0)
+    ready = (*(t for pair in totals_1 for t in pair), near_0[0])
+    back_a, sums_a = first_halo(0, mixed[1], ready, some)
+    mixed_delta, mixed_halo = attend_back(some, mixed, (back_a,), clips - some)
+    mixed_delta, mixed_halo, back_a, moved_1, near_0 = meet(
+        mixed_delta, mixed_halo, back_a, moved_1, near_0
+    )
+    came_a = lax.ppermute(back_a, "seq", [(1, 0)])
+    far_0 = far_pair(near_0)
 
     cut = 3 * width // 6
-    packed = (2, 2, 4, 64, 3 * cut)
-    out_spec = pl.BlockSpec(
-        (1, 2, 4, 64, cut), lambda t, info: ((t // 3 + info[0]) % 2, 0, 0, 0, t % 3)
-    )
-    qkv_keep, qkv_send = call_kernel(
+    def x_seat(t, info):
+        return (t // 3 + info[0]) % 2
+
+    left_spec = pl.BlockSpec((1, 2, 4, 64, cut), lambda t, info: (x_seat(t, info), 0, 0, 0, 0))
+    right_spec = pl.BlockSpec(
+        (2, 1, 1, 4, 64, cut),
+        lambda t, info: (0, x_seat(t, info), jnp.maximum(t % 3 - 1, 0), 0, 0, 0),
+    )
+    packed = [shape_of((2, 2, 4, 64, cut)), shape_of((2, 2, 2, 4, 64, cut))]
+    keep_l, keep_r, send_l, send_r = call_kernel(
         qkv_grad_kernel, info, [normed_one, mixed_delta, normed_halo, mixed_halo],
         name="qkv_grad", grid=(6,),
         ins=[
@@ -1042,48 +1129,80 @@
             whole_spec((clips * TILE, width)),
             pl.BlockSpec((clips * TILE, cut), lambda t, info: (0, jnp.maximum(t - 2, 0))),
         ],
-        outs=[out_spec, out_spec], shapes=[shape_of(packed)] * 2,
-        scratch=[pltpu.VMEM((width, cut), F32)], cost=(4 * mac, 16 * MIB), after=(first_halo, part_2, part_3),
-    )
-    z_1 = z_sum((part_2, part_3))
-    qkv_total = fold(qkv_keep, qkv_send, "core")
-    half = 32
-    left, right = qkv_total[:, :, :, :half], qkv_total[:, :, :, half:]
-    left = fold_two(left[0], left[1], "seq", "y")
-    right = fold_two(right[:, 0], right[:, 1], "y", "seq")
-    qkv_total = jnp.concatenate([left, right], axis=1).reshape(2, 2, 64, -1)
-    for step, pairs in ((1, Z_NEAR), (2, Z_FAR)):
-        keep, send = (qkv_total[:, 0], qkv_total[:, 1]) if step == 1 else (qkv_total[0], qkv_total[1])
-        qkv_total = plus(keep, lax.ppermute(send, "z", pairs))
-    qkv_grad = qkv_total.astype(F32)
-
+        outs=[left_spec, right_spec] * 2, shapes=packed * 2,
+        scratch=[pltpu.VMEM((width, cut), F32)], cost=(4 * mac, 16 * MIB),
+        after=(far_0[0],),
+    )
+    came_a, far_0, keep_l, keep_r, send_l, send_r = meet(
+        came_a, far_0, keep_l, keep_r, send_l, send_r
+    )
+    qkv_came = swap(send_l, "core"), swap(send_r, "core")
+    back_b, sums_b = first_halo(some, mixed_halo, (keep_l,), clips - some)
+    qkv_came, back_b = meet(qkv_came, back_b)
+    came_b = lax.ppermute(back_b, "seq", [(1, 0)])
+    came_l, came_r = qkv_came
+    stay_l, go_l = (plus(keep_l[k], came_l[k]) for k in range(2))
+    stay_r, go_r = (plus(keep_r[k], came_r[k]) for k in range(2))
+    go_l, go_r = swap(go_l, "seq"), swap(go_r, "y")
+    near_1 = near_pair(later(moved_1, stay_l, stay_r, back_b))
     part_grad, sums_one = call_kernel(
         first_back_kernel, info, [mixed_delta, qkv_weight, flat, middle_delta, table],
         name="first_back", grid=grid, ins=[qkv_rows, w_qkv, own, own, gb], outs=[own, sums],
         shapes=[shape_of((count, width), F32), shape_of((8, width), F32)],
-        cost=(3 * mac, 24 * MIB),
-    )
+        cost=(3 * mac, 24 * MIB), after=(stay_l, stay_r, near_1[0]),
+    )
+    go_l, go_r, near_1, came_b, part_grad, sums_one = meet(
+        go_l, go_r, near_1, came_b, part_grad, sums_one
+    )
+    share = width // 16
+    ones = sums_one + sums_a + sums_b
+    nought = jnp.zeros((width,), F32)
+    vectors = jnp.stack(
+        [ones[0], sums_two[0], ones[1], nought, sums_two[1], sums_two[3], sums_two[2], nought]
+    )
+    vectors = vectors.reshape(2, 4, 16, share).transpose(2, 0, 1, 3).reshape(32, 4, share)
+    vectors = lax.all_to_all(vectors, ("z", "y", "core", "seq"), 0, 0, tiled=True)
+    left, right = plus(stay_l, go_l), plus(stay_r, go_r)
+    vectors, left, right, near_1 = meet(vectors, left, right, near_1)
+    go_l, go_r = swap(left[1], "y"), swap(right[1], "seq")
+    far_1 = far_pair(near_1)
+    output = call_kernel(
+        output_kernel, info, [flat, attended, branch, sums_other, table],
+        name="output", grid=grid, ins=[own, own, own, half_sums(0), gb], outs=own,
+        shapes=shape_of((count, width)), cost=(0, 14 * MIB),
+        after=(left, right, far_1[0], came_b),
+    )
+    go_l, go_r, output = meet(go_l, go_r, output)
+    left, right = plus(left[0], go_l), plus(right[0], go_r)
+    qkv_total = jnp.concatenate([left[None], right]).reshape(3, 2, 2, 64, cut)
+    qkv_near = qkv_total[:, :, 1]
+    go = lax.ppermute(qkv_near, "z", Z_NEAR)
     input_grad = call_kernel(
-        input_grad_kernel, info, [part_grad, first_back, flat, table], name="input_grad",
-        grid=grid, ins=[own, halo_rows, own, gb], outs=own, shapes=shape_of((count, width)),
-        cost=(0, 8 * MIB),
-    )
-
-    ones = sums_one + sums_halo
-    vectors = jnp.stack(
-        [ones[0], sums_two[0], sums_two[1], sums_out[0], ones[1], sums_two[2], ones[2], ones[3]]
-    )
-    for axis, pairs in (("core", SWAP), ("seq", SWAP), ("y", SWAP), ("z", Z_NEAR), ("z", Z_FAR)):
-        vectors = vectors + lax.ppermute(vectors, axis, pairs)
-    vectors = vectors.T
-    dp_at = (z_at * 2 + y_at) * 2 + core_at
-    share = width // 16
-    mine = lax.dynamic_slice_in_dim(vectors, dp_at * share, share, axis=0)
-    gain_grad = lax.dynamic_slice_in_dim(mine[:, :4], x_at * 2, 2, axis=1)
-    bias_grad = lax.dynamic_slice_in_dim(mine[:, 4:6], x_at, 1, axis=1)
-
-    tiles = jnp.stack([z_0, z_1])
-    gates = tiles[:, :8].reshape(2, 2, 2, 2, 2, share, TILE)
+        functools.partial(input_grad_kernel, some), info, [part_grad, came_a, came_b, flat, table],
+        name="input_grad", grid=grid,
+        ins=[
+            own,
+            pl.BlockSpec((TILE, width), lambda r, info: (jnp.minimum(r, some - 1), 0)),
+            pl.BlockSpec((TILE, width), lambda r, info: (jnp.maximum(r - some, 0), 0)),
+            own, gb,
+        ],
+        outs=own, shapes=shape_of((count, width)), cost=(0, 8 * MIB),
+        after=(left, right, output, qkv_total),
+    )
+    go, far_1, input_grad = meet(go, far_1, input_grad)
+    qkv_total = plus(qkv_total[:, :, 0], go)
+    qkv_total = plus(qkv_total[:, 0], lax.ppermute(qkv_total[:, 1], "z", Z_FAR))
+    qkv_grad = qkv_total.transpose(1, 0, 2).reshape(-1, 3 * cut).astype(F32)
+    out_halves = later(out_grad, input_grad).reshape(-1, 2, width // 2)
+    out_kept = lax.dynamic_index_in_dim(out_halves, x_at, axis=1, keepdims=False)
+    out_sent = lax.dynamic_index_in_dim(out_halves, 1 - x_at, axis=1, keepdims=False)
+    out_grad = out_kept.astype(F32) + swap(out_sent, "seq").astype(F32)
+
+    vectors = jnp.sum(vectors, axis=0).T
+    gain_grad, bias_grad = vectors[:, :2], vectors[:, 2:3]
+
+    tiles = jnp.stack([plus(*far_0), plus(*far_1)])
+    gates = tiles[:, ::2].reshape(2, 2, 2, 2, 2, share, TILE)
     kept = lax.dynamic_index_in_dim(gates, core_at, axis=4, keepdims=False)
     sent = lax.dynamic_index_in_dim(gates, 1 - core_at, axis=4, keepdims=False)
     came = swap(sent, "core")
@@ -1091,7 +1210,7 @@
     both = both.transpose(2, 5, 1, 3, 4, 0, 6).astype(F32)
     gate_grad = both[0].reshape(share, -1)
     up_grad = both[1].reshape(share, -1)
-    down_grad = tiles[:, 8:].reshape(2, width // 2, TILE).transpose(0, 2, 1).astype(F32)
+    down_grad = tiles[:, 1].reshape(2, width // 2, TILE).transpose(0, 2, 1).astype(F32)
     down_grad = down_grad.reshape(2 * TILE, width // 2)
     shape = (clips, rows, width)
     return (

time: 481 us -> 427 us (0.89)
  waiting for transfers between devices: 97.8 us -> 52.9 us
  local copies, waits for them, and re-layouts: 38.3 us -> 18.9 us
  other arithmetic: 23.2 us -> 33.9 us
    ppermute x21 -> x19, waiting for transfers between devices: 66.1 us -> 26.4 us  [swap(): return lax.ppermute(values, axis, SWAP)]
    unnamed x94 -> x91, local copies, waits for them, and re-layouts: 19.1 us -> 4.58 us
    ppermute x8, starting transfers between devices: 17.7 us -> 7.03 us  [the longest x2 2.86 us: far_pair(): return (total[:, 0], lax.ppermute(total[:, 1], 'z', Z_FAR))]
    convert_element_type x16, other arithmetic: 15.7 us -> 24.3 us  [plus(): return (left.astype(F32) + right.astype(F32)).astype(BF)]
    ppermute x8, waiting for transfers between devices: 28.5 us -> 20 us  [the longest x1 7.9 us: fast_body(): go = lax.ppermute(qkv_near, 'z', Z_NEAR)]
    all_to_all x0 -> x1, waiting for transfers between devices: none -> 6.47 us  [fast_body(): lax.all_to_all(vectors, ('z', 'y', 'core', 'seq'), 0, 0, tiled=True)]
    all_to_all x0 -> x1, starting transfers between devices: none -> 5.58 us  [fast_body(): lax.all_to_all(vectors, ('z', 'y', 'core', 'seq'), 0, 0, tiled=True)]
    ppermute x21 -> x19, starting transfers between devices: 13.3 us -> 16.9 us  [swap(): return lax.ppermute(values, axis, SWAP)]
  transfers between devices with their start and end apart: 33 -> 30, of which waited for: 15 -> 14; matrix products, arithmetic and copies ran while one was open for 9% -> 9% of each run, Pallas kernels for 42% -> 45%
where the time goes in v2:
time: 427 us; the launch traced here: 419 us
  Pallas kernels  264 us (62%)
  waiting for transfers between devices  52.9 us (12%)
  starting transfers between devices  34.4 us (8%)
  other arithmetic  33.9 us (8%)
  local copies, waits for them, and re-layouts  18.9 us (4%)
  between operations  15.4 us (4%)
    pallas_call x16, Pallas kernels, call_kernel(): pl.pallas_call(run, grid_spec=pltpu.PrefetchScalarGridSpec(num_scalar_pre...  264 us
    ppermute x19, waiting for transfers between devices, swap(): return lax.ppermute(values, axis, SWAP)  26.4 us
    convert_element_type x16, other arithmetic, plus(): return (left.astype(F32) + right.astype(F32)).astype(BF)  24.3 us
    ppermute x19, starting transfers between devices, swap(): return lax.ppermute(values, axis, SWAP)  16.9 us
  transfers between devices with their start and end apart: 30, of which 14 were waited for; matrix products, arithmetic and copies ran while one was open for 9% of the time, Pallas kernels for 45%

profile of v2, /device:TPU:0, one launch (start us, length us, event | category | flops | bytes accessed | tf_op | source)
XLA Modules:
  0.0 419.4 jit_solution(11537414432242346632)
XLA Ops:
  7.3 2.4 slice.198
  9.6 4.9 %collective-permute-start = (bf16[512,1024]{1,0:T(8,128)(2,1)}, bf16[512,1024]{1,0:T(8,128)(2,1)S(1)}, u32[]{:S(2)}, u32[]{:S(2)}) collective-permute-start(bf16[512,1024]{1,0:T(8,128)(2,1)} %bitcast.7), channel_id=1, source_target_pairs={{0,1},{2,3},{4,5},{6,7},{8,9},{10,11},{12,13},{14,15},{16,17},{18,... | collective-permute-start | bytes 3145736 | tf_op jit(solution)/shard_map/ppermute | solution.py:948
  16.1 13.4 %qkv.1 = (bf16[1024,3072]{1,0:T(8,128)(2,1)}, bf16[1024,1024]{1,0:T(8,128)(2,1)}) custom-call(s32[9]{0:T(128)} %concatenate.26.info, bf16[1024,1024]{1,0:T(8,128)(2,1)} %bitcast.129, bf16[1024,3072]{1,0:T(8,128)(2,1)} %refs_1_.9, f32[8,1024]{1,0:T(8,128)} %maximum_bitcast_fusion.refs_2_.refs_3_.refs_9_.refs_4_, f32[3,512,128]{2,1,0:T(8,128)} %constant.44.clone.refs_3_.refs_4_), custom_call_target="tpu_custom_call" | custom-call | flops 1610612736 | bytes 4194304 | tf_op jit(solution)/shard_map/qkv/pallas_call | solution.py:328
  29.5 9.4 %attend_late.1 = (bf16[1024,1024]{1,0:T(8,128)(2,1)}, f32[1024,128]{1,0:T(8,128)}) custom-call(s32[9]{0:T(128)} %concatenate.26.info, bf16[1024,3072]{1,0:T(8,128)(2,1)} %get-tuple-element.122.refs_0_), custom_call_target="tpu_custom_call" | custom-call | flops 1073741824 | bytes 2097152 | tf_op jit(solution)/shard_map/attend_late/pallas_call | solution.py:328
  38.9 2.0 multiply_convert_fusion.refs_2_
  40.8 0.9 copy-done.2
  41.8 5.8 %halo.1 = (bf16[512,2048]{1,0:T(8,128)(2,1)}, bf16[512,1024]{1,0:T(8,128)(2,1)}) custom-call(s32[9]{0:T(128)} %concatenate.26.info, bf16[512,1024]{1,0:T(8,128)(2,1)} %copy-done.2, bf16[1024,3072]{1,0:T(8,128)(2,1)} %refs_1_.9, bf16[1024,3072]{1,0:T(8,128)(2,1)} %refs_1_.9, f32[8,1024]{1,0:T(8,128)} %maximum_bitcast_fusion.refs_2_.refs_3_.refs_9_.refs_4_, ...), custom_call_target="tpu_custom_call" | custom-call | flops 536870912 | bytes 2097152 | tf_op jit(solution)/shard_map/halo/pallas_call | solution.py:328
  47.6 9.1 %attend_early.1 = (bf16[1024,1024]{1,0:T(8,128)(2,1)}, f32[1024,128]{1,0:T(8,128)}) custom-call(s32[9]{0:T(128)} %concatenate.26.info, bf16[1024,3072]{1,0:T(8,128)(2,1)} %get-tuple-element.122.refs_0_, bf16[512,2048]{1,0:T(8,128)(2,1)} %get-tuple-element.126.refs_1_, ...), custom_call_target="tpu_custom_call", output_to_operand_aliasing={{0}: (3, {}), {1}: (4, {})} | custom-call | flops 1073741824 | bytes 3145728 | tf_op jit(solution)/shard_map/attend_early/pallas_call | solution.py:328
  56.7 8.8 %project.1 = (f32[1024,1024]{1,0:T(8,128)}, bf16[1024,1024]{1,0:T(8,128)(2,1)}) custom-call(s32[9]{0:T(128)} %concatenate.26.info, bf16[1024,1024]{1,0:T(8,128)(2,1)} %get-tuple-element.127.refs_0_.refs_7_, bf16[1024,1024]{1,0:T(8,128)(2,1)} %bitcast.130, bf16[1024,1024]{1,0:T(8,128)(2,1)} %refs_8_.3, ...), custom_call_target="tpu_custom_call" | custom-call | flops 536870912 | bytes 3145728 | tf_op jit(solution)/shard_map/project/pallas_call | solution.py:328
  66.1 6.3 %collective-permute-done.1.refs_1_ = bf16[1024,1024]{1,0:T(8,128)(2,1)} collective-permute-done((bf16[1024,1024]{1,0:T(8,128)(2,1)}, bf16[1024,1024]{1,0:T(8,128)(2,1)}, u32[]{:S(2)}, u32[]{:S(2)}) %collective-permute-start.1) | collective-permute-done | bytes 2097184 | tf_op jit(solution)/shard_map/ppermute | solution.py:904
  72.9 52.3 %feed_forward.2 = (bf16[1280,1024]{1,0:T(8,128)(2,1)}, bf16[1280,1024]{1,0:T(8,128)(2,1)}, bf16[2,1024,1024]{2,1,0:T(8,128)(2,1)}, bf16[2,3072,128]{2,1,0:T(8,12...) custom-call(s32[9]{0:T(128)} %concatenate.26.info, ...), custom_call_target="tpu_custom_call" | custom-call | flops 9663676416 | bytes 7864320 | tf_op jit(solution)/shard_map/feed_forward/pallas_call | solution.py:328
  125.3 2.2 collective-permute-start.4
  127.5 54.7 %feed_forward.3 = (bf16[1280,1024]{1,0:T(8,128)(2,1)}, bf16[1280,1024]{1,0:T(8,128)(2,1)}, bf16[2,1024,1024]{2,1,0:T(8,128)(2,1)}, bf16[2,3072,128]{2,1,0:T(8,12...) custom-call(s32[9]{0:T(128)} %concatenate.26.info, ...), custom_call_target="tpu_custom_call" | custom-call | flops 9663676416 | bytes 7864320 | tf_op jit(solution)/shard_map/feed_forward/pallas_call | solution.py:328
  182.3 7.5 %collective-permute-done.5.refs_1_.refs_3_ = bf16[2,1024,1024]{2,1,0:T(8,128)(2,1)} collective-permute-done((bf16[2,1024,1024]{2,1,0:T(8,128)(2,1)}, bf16[2,1024,1024]{2,1,0:T(8,128)(2,1)}, u32[]{:S(2)}, u32[]{:S(2)}) %collective-permute-start.5) | collective-permute-done | bytes 4194336 | tf_op jit(solution)/shard_map/ppermute | solution.py:904
  189.8 1.3 collective-permute-start.8
  191.6 2.7 fusion.6
  194.5 1.3 fusion.4
  195.9 2.0 collective-permute-start.6
  197.9 16.7 %project_back.1 = (f32[1024,1024]{1,0:T(8,128)}, bf16[1024,1024]{1,0:T(8,128)(2,1)}, bf16[1024,1024]{1,0:T(8,128)(2,1)}, f32[8,1024]{1,0:T(8,128)}) custom-call(s32[9]{0:T(128)} %concatenate.26.info, bf16[1280,1024]{1,0:T(8,128)(2,1)} %get-tuple-element.144.refs_0_, bf16[2,1024,1024]{2,1,0:T(8,128)(2,1)} %collective-permute-done.5.refs_1_.refs_3_, ...), custom_call_target="tpu_custom_call" | custom-call | flops 1073741824 | bytes 6291456 | tf_op jit(solution)/shard_map/project_back/pallas_call | solution.py:328
  214.7 25.4 %attend_back.2 = (bf16[1024,3072]{1,0:T(8,128)(2,1)}, bf16[512,2048]{1,0:T(8,128)(2,1)}) custom-call(s32[9]{0:T(128)} %concatenate.26.info, bf16[1024,3072]{1,0:T(8,128)(2,1)} %get-tuple-element.122.refs_0_, bf16[512,2048]{1,0:T(8,128)(2,1)} %get-tuple-element.126.refs_1_, bf16[1024,1024]{1,0:T(8,128)(2,1)} %get-tuple-element.157.refs_2_, ...), custom_call_target="tpu_custom_call" | custom-call | flops 4026531840 | bytes 4718592 | tf_op jit(solution)/shard_map/attend_back/pallas_call | solution.py:328
  240.1 3.2 collective-permute-done.7
  243.3 1.1 collective-permute-done.6
  244.5 1.5 add_convert_fusion.7
  247.4 2.7 fusion.10
  250.8 2.7 fusion.8
  254.5 1.0 pad_maximum_fusion.2.refs_8_
  255.5 5.3 %first_halo.2 = (bf16[384,1024]{1,0:T(8,128)(2,1)}, f32[8,1024]{1,0:T(8,128)}) custom-call(s32[9]{0:T(128)} %concatenate.26.info, bf16[512,2048]{1,0:T(8,128)(2,1)} %get-tuple-element.165.refs_0_.refs_8_, bf16[1024,3072]{1,0:T(8,128)(2,1)} %refs_1_.9, bf16[1024,3072]{1,0:T(8,128)(2,1)} %refs_1_.9, bf16[512,1024]{1,0:T(8,128)(2,1)} %copy-done.2, ...), custom_call_target="tpu_custom_call" | custom-call | flops 402653184 | bytes 1572864 | tf_op jit(solution)/shard_map/first_halo/pallas_call | solution.py:328
  260.8 14.9 %attend_back.3 = (bf16[1024,3072]{1,0:T(8,128)(2,1)}, bf16[512,2048]{1,0:T(8,128)(2,1)}) custom-call(s32[9]{0:T(128)} %concatenate.26.info, bf16[1024,3072]{1,0:T(8,128)(2,1)} %get-tuple-element.122.refs_0_, bf16[512,2048]{1,0:T(8,128)(2,1)} %get-tuple-element.126.refs_1_, ...), custom_call_target="tpu_custom_call", output_to_operand_aliasing={{0}: (8, {}), {1}: (9, {})} | custom-call | flops 1342177280 | bytes 1572864 | tf_op jit(solution)/shard_map/attend_back/pallas_call | solution.py:328
  275.7 1.3 collective-permute-start.13
  277.0 1.4 add_convert_fusion.6
  279.3 2.6 collective-permute-start.14
  281.8 14.1 %qkv_grad.1 = (bf16[2,2,4,64,512]{4,3,2,1,0:T(8,128)(2,1)}, bf16[2,2,2,4,64,512]{5,4,3,2,1,0:T(8,128)(2,1)}, bf16[2,2,4,64,512]{4,3,2,1,0:T(8,128)(2,1)}, bf16[2,2,2,4,64,512]{5,4,3,2,1,0:T(8,128)(2,1)}) custom-call(s32[9]{0:T(128)} %concatenate.26.info, bf16[1024,1024]{1,0:T(8,128)(2,1)} %get-tuple-element.181.refs_0_, ...), custom_call_target="tpu_custom_call" | custom-call | flops 2147483648 | bytes 4194304 | tf_op jit(solution)/shard_map/qkv_grad/pallas_call | solution.py:328
  295.9 1.8 collective-permute-done.14
  299.3 3.8 first_halo.3
  303.0 1.3 collective-permute-done.15
  304.6 2.6 fusion.13
  307.3 2.1 fusion.1
  309.4 1.4 collective-permute-start.18
  310.7 1.3 add_convert_fusion.5
  312.1 1.3 add_convert_fusion.4
  313.5 0.9 pad_maximum_fusion.5
  314.5 4.4 %collective-permute-start.17 = (bf16[2,4,64,512]{3,2,1,0:T(8,128)(2,1)}, bf16[2,4,64,512]{3,2,1,0:T(8,128)(2,1)}, u32[]{:S(2)}, u32[]{:S(2)}) collective-permute-start(bf16[2,4,64,512]{3,2,1,0:T(8,128)(2,1)} %get-tuple-element.246), channel_id=1, source_target_pairs={{0,1},{1,0},{2,3},{3,2},{4,5},{5,4},{6,7},{7,6},{8,9},{9,8},{10,11... | collective-permute-start | bytes 1572872 | tf_op jit(solution)/shard_map/ppermute | solution.py:904
  319.8 1.3 collective-permute-start.20
  321.1 0.9 pad_maximum_fusion.4.refs_7_
  322.1 16.0 %first_back.1 = (f32[1024,1024]{1,0:T(8,128)}, f32[8,1024]{1,0:T(8,128)}) custom-call(s32[9]{0:T(128)} %concatenate.26.info, bf16[1024,3072]{1,0:T(8,128)(2,1)} %get-tuple-element.182.refs_1_.refs_0_, bf16[1024,3072]{1,0:T(8,128)(2,1)} %refs_1_.9, bf16[1024,1024]{1,0:T(8,128)(2,1)} %bitcast.132, f32[1024,1024]{1,0:T(8,128)} %get-tuple-element.205.refs_3_, ...), custom_call_target="tpu_custom_call" | custom-call | flops 1610612736 | bytes 6291456 | tf_op jit(solution)/shard_map/first_back/pallas_call | solution.py:328
  338.2 1.6 add_convert_fusion.refs_6_
  340.9 5.6 %all-to-all-start = ((f32[32,1,256]{2,1,0:T(1,128)}), f32[32,1,256]{2,1,0:T(1,128)S(1)}, u32[]{:S(2)}, u32[]{:S(2)}) async-start(f32[32,1,256]{2,1,0:T(1,128)} %reshape.185), calls=%async_computation | async-start | bytes 65536 | tf_op jit(solution)/shard_map/all_to_all | solution.py:1164
  346.5 1.3 add_convert_fusion.17.refs_5_
  347.8 6.5 %all-to-all-done = f32[32,1,256]{2,1,0:T(1,128)S(1)} async-done(((f32[32,1,256]{2,1,0:T(1,128)}), f32[32,1,256]{2,1,0:T(1,128)S(1)}, u32[]{:S(2)}, u32[]{:S(2)}) %all-to-all-start) | async-done | bytes 32800 | tf_op jit(solution)/shard_map/all_to_all | solution.py:1164
  357.6 1.4 add_convert_fusion.3
  359.0 0.9 slice_bitcast_fusion.1
  360.2 7.3 %output.1.refs_7_ = bf16[1024,1024]{1,0:T(8,128)(2,1)} custom-call(s32[9]{0:T(128)} %concatenate.26.info, bf16[1024,1024]{1,0:T(8,128)(2,1)} %bitcast.133, f32[1024,1024]{1,0:T(8,128)} %get-tuple-element.152.refs_4_.refs_1_, bf16[1280,1024]{1,0:T(8,128)(2,1)} %get-tuple-element.151.refs_2_, bf16[2,1024,1024]{2,1,0:T(8,128)(2,1)} %collective-permute-done.5.refs_1_.refs_3_, ...), custom_call_target="tpu_custom_call" | custom-call | bytes 3670016 | tf_op jit(solution)/shard_map/output/pallas_call | solution.py:328
  367.5 2.6 collective-permute-done.22
  372.9 1.0 pad_maximum_fusion.refs_8_
  373.9 6.7 %input_grad.1 = bf16[1024,1024]{1,0:T(8,128)(2,1)} custom-call(s32[9]{0:T(128)} %concatenate.26.info, f32[1024,1024]{1,0:T(8,128)} %get-tuple-element.224.refs_0_, bf16[384,1024]{1,0:T(8,128)(2,1)} %copy-done.33, bf16[128,1024]{1,0:T(8,128)(2,1)} %copy-done.31, bf16[1024,1024]{1,0:T(8,128)(2,1)} %bitcast.134, ...), custom_call_target="tpu_custom_call" | custom-call | bytes 2097152 | tf_op jit(solution)/shard_map/input_grad/pallas_call | solution.py:328
  380.5 3.4 collective-permute-done.24
  384.0 7.9 %collective-permute-done.23 = bf16[3,2,64,512]{3,2,1,0:T(8,128)(2,1)S(1)} collective-permute-done((bf16[3,2,64,512]{3,2,1,0:T(8,128)(2,1)S(1)}, bf16[3,2,64,512]{3,2,1,0:T(8,128)(2,1)S(1)}, u32[]{:S(2)}, u32[]{:S(2)}) %collective-permute-start.23) | collective-permute-done | bytes 393248 | tf_op jit(solution)/shard_map/ppermute | solution.py:1179
  391.9 1.1 fusion.16
  393.1 1.0 copy.57
  394.4 1.0 reshape.169
  396.7 3.5 collective-permute-done.26
  400.9 6.9 %collective-permute-done.25 = bf16[3,64,512]{2,1,0:T(8,128)(2,1)S(1)} collective-permute-done((bf16[3,64,512]{2,1,0:T(8,128)(2,1)S(1)}, bf16[3,64,512]{2,1,0:T(8,128)(2,1)S(1)}, u32[]{:S(2)}, u32[]{:S(2)}) %collective-permute-start.25) | collective-permute-done | bytes 196640 | tf_op jit(solution)/shard_map/ppermute | solution.py:1194
  409.2 1.2 reshape_squeeze.7
  410.8 1.2 reshape_squeeze.8
  (181 shorter events, 21.5 us)
Async XLA Ops:
  7.2 7.4 %copy-start.42 = (s32[4]{0:T(128)S(1)}, s32[4]{0:T(128)}, u32[]{:S(2)}) copy-start(s32[4]{0:T(128)} %param.14) | copy-start | bytes 52
  7.2 7.5 %copy-start.39 = (f32[1024,4]{0,1:T(4,128)S(1)}, f32[1024,4]{0,1:T(4,128)}, u32[]{:S(2)}) copy-start(f32[1024,4]{0,1:T(4,128)} %param.20) | copy-start | bytes 49156
  7.2 8.2 %copy-start.40 = (f32[1024,2]{0,1:T(2,128)S(1)}, f32[1024,2]{0,1:T(2,128)}, u32[]{:S(2)}) copy-start(f32[1024,2]{0,1:T(2,128)} %param.21) | copy-start | bytes 24580
  7.2 387.2 %reduce-scatter.2.cloned.1.call-start = ((), (), s32[]{:S(2)}) async-start(), calls=%async_computation.2 | async-start | bytes 2228224 | tf_op jit(solution)/shard_map/reduce_scatter | solution.py:1065
  9.6 31.2 %collective-permute-start = (bf16[512,1024]{1,0:T(8,128)(2,1)}, bf16[512,1024]{1,0:T(8,128)(2,1)S(1)}, u32[]{:S(2)}, u32[]{:S(2)}) collective-permute-start(bf16[512,1024]{1,0:T(8,128)(2,1)} %bitcast.7), channel_id=1, source_target_pairs={{0,1},{2,3},{4,5},{6,7},{8,9},{10,11},{12,13},{14,15},{16,17},{18,... | collective-permute-start | bytes 3145736 | tf_op jit(solution)/shard_map/ppermute | solution.py:948
  29.5 9.4 %copy-start.6 = (bf16[4,256,1024]{2,1,0:T(8,128)(2,1)S(1)}, bf16[4,256,1024]{2,1,0:T(8,128)(2,1)}, u32[]{:S(2)}) copy-start(bf16[4,256,1024]{2,1,0:T(8,128)(2,1)} %param.13) | copy-start | bytes 6291460
  56.7 8.8 %copy-start.7 = (bf16[1024,1024]{1,0:T(8,128)(2,1)S(1)}, bf16[1024,1024]{1,0:T(8,128)(2,1)}, u32[]{:S(2)}) copy-start(bf16[1024,1024]{1,0:T(8,128)(2,1)} %multiply_convert_fusion.refs_2_) | copy-start | bytes 6291460
  65.6 6.8 %collective-permute-start.1 = (bf16[1024,1024]{1,0:T(8,128)(2,1)}, bf16[1024,1024]{1,0:T(8,128)(2,1)}, u32[]{:S(2)}, u32[]{:S(2)}) collective-permute-start(bf16[1024,1024]{1,0:T(8,128)(2,1)} %get-tuple-element.128.refs_0_), channel_id=1, source_target_pairs={{0,2},{2,0},{1,3},{3,1},{4,6},{6,4},{5,7},{7,5},{8,10},{10,8},{9,1... | collective-permute-start | bytes 6291464 | tf_op jit(solution)/shard_map/ppermute | solution.py:904
  65.6 7.3 %collective-permute-start.2 = (bf16[1024,1024]{1,0:T(8,128)(2,1)S(1)}, bf16[1024,1024]{1,0:T(8,128)(2,1)}, u32[]{:S(2)}, u32[]{:S(2)}) collective-permute-start(bf16[1024,1024]{1,0:T(8,128)(2,1)S(1)} %copy-done.7), channel_id=1, source_target_pairs={{0,2},{2,0},{1,3},{3,1},{4,6},{6,4},{5,7},{7,5},{8,10},{10,8},{9,1... | collective-permute-start | bytes 6291464 | tf_op jit(solution)/shard_map/ppermute | solution.py:904
  125.2 57.0 %collective-permute-start.3 = (bf16[2,3072,128]{2,1,0:T(8,128)(2,1)}, bf16[2,3072,128]{2,1,0:T(8,128)(2,1)S(1)}, u32[]{:S(2)}, u32[]{:S(2)}) collective-permute-start(bf16[2,3072,128]{2,1,0:T(8,128)(2,1)} %get-tuple-element.141), channel_id=1, source_target_pairs={{0,1},{1,0},{2,3},{3,2},{4,5},{5,4},{6,7},{7,6},{8,9},{9,8},{10,11... | collective-permute-start | bytes 4718600 | tf_op jit(solution)/shard_map/ppermute | solution.py:904
  125.3 56.9 %collective-permute-start.4 = (bf16[2,3072,128]{2,1,0:T(8,128)(2,1)}, bf16[2,3072,128]{2,1,0:T(8,128)(2,1)}, u32[]{:S(2)}, u32[]{:S(2)}) collective-permute-start(bf16[2,3072,128]{2,1,0:T(8,128)(2,1)} %get-tuple-element.143), channel_id=1, source_target_pairs={{0,4},{4,0},{1,5},{5,1},{2,6},{6,2},{3,7},{7,3},{8,12},{12,8},{9,1... | collective-permute-start | bytes 4718600 | tf_op jit(solution)/shard_map/ppermute | solution.py:904
  127.5 64.2 %copy-start.30 = (bf16[2,3072,128]{2,1,0:T(8,128)(2,1)S(1)}, bf16[2,3072,128]{2,1,0:T(8,128)(2,1)}, u32[]{:S(2)}) copy-start(bf16[2,3072,128]{2,1,0:T(8,128)(2,1)} %get-tuple-element.155) | copy-start | bytes 4718596
  182.2 12.3 %copy-start.29 = (bf16[2,3072,128]{2,1,0:T(8,128)(2,1)S(1)}, bf16[2,3072,128]{2,1,0:T(8,128)(2,1)}, u32[]{:S(2)}) copy-start(bf16[2,3072,128]{2,1,0:T(8,128)(2,1)} %get-tuple-element.153) | copy-start | bytes 4718596
  182.2 7.6 %collective-permute-start.5 = (bf16[2,1024,1024]{2,1,0:T(8,128)(2,1)}, bf16[2,1024,1024]{2,1,0:T(8,128)(2,1)}, u32[]{:S(2)}, u32[]{:S(2)}) collective-permute-start(bf16[2,1024,1024]{2,1,0:T(8,128)(2,1)} %get-tuple-element.149), channel_id=1, source_target_pairs={{0,2},{2,0},{1,3},{3,1},{4,6},{6,4},{5,7},{7,5},{8,10},{10,8},{9,1... | collective-permute-start | bytes 12582920 | tf_op jit(solution)/shard_map/ppermute | solution.py:904
  189.8 54.6 %collective-permute-start.8 = (bf16[2,3072,128]{2,1,0:T(8,128)(2,1)}, bf16[2,3072,128]{2,1,0:T(8,128)(2,1)}, u32[]{:S(2)}, u32[]{:S(2)}) collective-permute-start(bf16[2,3072,128]{2,1,0:T(8,128)(2,1)} %get-tuple-element.162), channel_id=1, source_target_pairs={{0,1},{1,0},{2,3},{3,2},{4,5},{5,4},{6,7},{7,6},{8,9},{9,8},{10,11... | collective-permute-start | bytes 4718600 | tf_op jit(solution)/shard_map/ppermute | solution.py:904
  191.1 53.3 %collective-permute-start.9 = (bf16[2,3072,128]{2,1,0:T(8,128)(2,1)}, bf16[2,3072,128]{2,1,0:T(8,128)(2,1)}, u32[]{:S(2)}, u32[]{:S(2)}) collective-permute-start(bf16[2,3072,128]{2,1,0:T(8,128)(2,1)} %get-tuple-element.164), channel_id=1, source_target_pairs={{0,4},{4,0},{1,5},{5,1},{2,6},{6,2},{3,7},{7,3},{8,12},{12,8},{9,1... | collective-permute-start | bytes 4718600 | tf_op jit(solution)/shard_map/ppermute | solution.py:904
  194.3 49.0 %collective-permute-start.7 = (bf16[3072,128]{1,0:T(8,128)(2,1)S(1)}, bf16[3072,128]{1,0:T(8,128)(2,1)S(1)}, u32[]{:S(2)}, u32[]{:S(2)}) collective-permute-start(bf16[3072,128]{1,0:T(8,128)(2,1)S(1)} %get-tuple-element.241.refs_13_), channel_id=1, source_target_pairs={{0,1},{1,0},{2,3},{3,2},{4,5},{5,4},{6,7},{7,6},{8,9},{9,8},{10,11... | collective-permute-start | bytes 2359304 | tf_op jit(solution)/shard_map/ppermute | solution.py:904
  195.9 2.0 copy-start.25
  195.9 48.6 %collective-permute-start.6 = (bf16[3072,128]{1,0:T(8,128)(2,1)S(1)}, bf16[3072,128]{1,0:T(8,128)(2,1)}, u32[]{:S(2)}, u32[]{:S(2)}) collective-permute-start(bf16[3072,128]{1,0:T(8,128)(2,1)S(1)} %get-tuple-element.243.refs_11_), channel_id=1, source_target_pairs={{0,4},{4,0},{1,5},{5,1},{2,6},{6,2},{3,7},{7,3},{8,12},{12,8},{9,1... | collective-permute-start | bytes 2359304 | tf_op jit(solution)/shard_map/ppermute | solution.py:904
  214.6 29.8 %copy-start.12 = (bf16[3072,128]{1,0:T(8,128)(2,1)S(1)}, bf16[3072,128]{1,0:T(8,128)(2,1)}, u32[]{:S(2)}) copy-start(bf16[3072,128]{1,0:T(8,128)(2,1)} %get-tuple-element.172.refs_12_) | copy-start | bytes 2359300
  214.6 29.8 %copy-start.13 = (bf16[3072,128]{1,0:T(8,128)(2,1)S(1)}, bf16[3072,128]{1,0:T(8,128)(2,1)}, u32[]{:S(2)}) copy-start(bf16[3072,128]{1,0:T(8,128)(2,1)} %get-tuple-element.170.refs_10_) | copy-start | bytes 2359300
  246.2 4.6 %copy-start.27 = (bf16[2,3072,128]{2,1,0:T(8,128)(2,1)S(1)}, bf16[2,3072,128]{2,1,0:T(8,128)(2,1)}, u32[]{:S(2)}) copy-start(bf16[2,3072,128]{2,1,0:T(8,128)(2,1)} %get-tuple-element.166) | copy-start | bytes 4718596
  246.2 29.5 %collective-permute-start.12 = (bf16[24,128,128]{2,1,0:T(8,128)(2,1)S(1)}, bf16[24,128,128]{2,1,0:T(8,128)(2,1)}, u32[]{:S(2)}, u32[]{:S(2)}) collective-permute-start(bf16[24,128,128]{2,1,0:T(8,128)(2,1)S(1)} %pad_maximum_fusion.3), channel_id=1, source_target_pairs={{0,8},{8,0},{16,24},{24,16},{1,9},{9,1},{17,25},{25,17},{2,10},{10... | collective-permute-start | bytes 2359304 | tf_op jit(solution)/shard_map/ppermute | solution.py:1031
  250.1 3.4 copy-start.22
  250.1 25.6 %collective-permute-start.11 = (bf16[3072,128]{1,0:T(8,128)(2,1)S(1)}, bf16[3072,128]{1,0:T(8,128)(2,1)}, u32[]{:S(2)}, u32[]{:S(2)}) collective-permute-start(bf16[3072,128]{1,0:T(8,128)(2,1)S(1)} %get-tuple-element.237.refs_7_), channel_id=1, source_target_pairs={{0,1},{1,0},{2,3},{3,2},{4,5},{5,4},{6,7},{7,6},{8,9},{9,8},{10,11... | collective-permute-start | bytes 2359304 | tf_op jit(solution)/shard_map/ppermute | solution.py:904
  253.5 2.0 copy-start.23
  253.5 22.2 %collective-permute-start.10 = (bf16[3072,128]{1,0:T(8,128)(2,1)S(1)}, bf16[3072,128]{1,0:T(8,128)(2,1)}, u32[]{:S(2)}, u32[]{:S(2)}) collective-permute-start(bf16[3072,128]{1,0:T(8,128)(2,1)S(1)} %get-tuple-element.239.refs_5_), channel_id=1, source_target_pairs={{0,4},{4,0},{1,5},{5,1},{2,6},{6,2},{3,7},{7,3},{8,12},{12,8},{9,1... | collective-permute-start | bytes 2359304 | tf_op jit(solution)/shard_map/ppermute | solution.py:904
  260.7 14.9 %copy-start.32 = (bf16[384,1024]{1,0:T(8,128)(2,1)S(1)}, bf16[384,1024]{1,0:T(8,128)(2,1)}, u32[]{:S(2)}) copy-start(bf16[384,1024]{1,0:T(8,128)(2,1)} %get-tuple-element.178.refs_6_) | copy-start | bytes 2359300
  260.8 16.2 %copy-start.11 = (bf16[24,128,128]{2,1,0:T(8,128)(2,1)S(1)}, bf16[24,128,128]{2,1,0:T(8,128)(2,1)}, u32[]{:S(2)}) copy-start(bf16[24,128,128]{2,1,0:T(8,128)(2,1)} %pad_maximum_fusion.2.refs_8_) | copy-start | bytes 2359300
  275.7 22.1 %collective-permute-start.13 = (bf16[384,1024]{1,0:T(8,128)(2,1)S(1)}, bf16[384,1024]{1,0:T(8,128)(2,1)S(1)}, u32[]{:S(2)}, u32[]{:S(2)}) collective-permute-start(bf16[384,1024]{1,0:T(8,128)(2,1)S(1)} %copy-done.32), channel_id=1, source_target_pairs={{1,0},{3,2},{5,4},{7,6},{9,8},{11,10},{13,12},{15,14},{17,16},{19,... | collective-permute-start | bytes 2359304 | tf_op jit(solution)/shard_map/ppermute | solution.py:1110
  279.3 18.5 %collective-permute-start.14 = (bf16[3,4,128,128]{3,2,1,0:T(8,128)(2,1)S(1)}, bf16[3,4,128,128]{3,2,1,0:T(8,128)(2,1)S(1)}, u32[]{:S(2)}, u32[]{:S(2)}) collective-permute-start(bf16[3,4,128,128]{3,2,1,0:T(8,128)(2,1)S(1)} %get-tuple-element.251), channel_id=1, source_target_pairs={{0,16},{16,0},{8,24},{24,8},{1,17},{17,1},{9,25},{25,9},{2,18},{18... | collective-permute-start | bytes 1179656 | tf_op jit(solution)/shard_map/ppermute | solution.py:1035
  298.7 5.9 %copy-start.19 = (bf16[2,2,4,64,512]{4,3,2,1,0:T(8,128)(2,1)S(1)}, bf16[2,2,4,64,512]{4,3,2,1,0:T(8,128)(2,1)}, u32[]{:S(2)}) copy-start(bf16[2,2,4,64,512]{4,3,2,1,0:T(8,128)(2,1)} %get-tuple-element.189.refs_4_) | copy-start | bytes 3145732
  298.7 5.9 %collective-permute-start.16 = (bf16[2,2,2,4,64,512]{5,4,3,2,1,0:T(8,128)(2,1)}, bf16[2,2,2,4,64,512]{5,4,3,2,1,0:T(8,128)(2,1)S(1)}, u32[]{:S(2)}, u32[]{:S(2)}) collective-permute-start(bf16[2,2,2,4,64,512]{5,4,3,2,1,0:T(8,128)(2,1)} %get-tuple-element.191), channel_id=1, source_target_pairs={{0,2},{2,0},{1,3},{3,1},{4,6},{6,4},{5,7},{7,5},{8,10},{10,8},{9,1... | collective-permute-start | bytes 6291464 | tf_op jit(solution)/shard_map/ppermute | solution.py:904
  298.8 5.6 %collective-permute-start.15 = (bf16[2,2,4,64,512]{4,3,2,1,0:T(8,128)(2,1)}, bf16[2,2,4,64,512]{4,3,2,1,0:T(8,128)(2,1)}, u32[]{:S(2)}, u32[]{:S(2)}) collective-permute-start(bf16[2,2,4,64,512]{4,3,2,1,0:T(8,128)(2,1)} %get-tuple-element.190), channel_id=1, source_target_pairs={{0,2},{2,0},{1,3},{3,1},{4,6},{6,4},{5,7},{7,5},{8,10},{10,8},{9,1... | collective-permute-start | bytes 3145736 | tf_op jit(solution)/shard_map/ppermute | solution.py:904
  304.6 2.7 copy-start.26
  307.3 3.5 copy-start.9
  309.4 2.7 copy-start.8
  309.4 28.8 %collective-permute-start.18 = (bf16[2,2,4,64,512]{4,3,2,1,0:T(8,128)(2,1)}, bf16[2,2,4,64,512]{4,3,2,1,0:T(8,128)(2,1)}, u32[]{:S(2)}, u32[]{:S(2)}) collective-permute-start(bf16[2,2,4,64,512]{4,3,2,1,0:T(8,128)(2,1)} %get-tuple-element.236), channel_id=1, source_target_pairs={{0,4},{4,0},{1,5},{5,1},{2,6},{6,2},{3,7},{7,3},{8,12},{12,8},{9,1... | collective-permute-start | bytes 3145736 | tf_op jit(solution)/shard_map/ppermute | solution.py:904
  313.5 5.4 %copy-start.41 = (f32[8,1024]{1,0:T(8,128)S(1)}, f32[8,1024]{1,0:T(8,128)}, u32[]{:S(2)}) copy-start(f32[8,1024]{1,0:T(8,128)} %get-tuple-element.211) | copy-start | bytes 98308
  314.5 23.7 %collective-permute-start.19 = (bf16[24,128,128]{2,1,0:T(8,128)(2,1)}, bf16[24,128,128]{2,1,0:T(8,128)(2,1)}, u32[]{:S(2)}, u32[]{:S(2)}) collective-permute-start(bf16[24,128,128]{2,1,0:T(8,128)(2,1)} %pad_maximum_fusion.5), channel_id=1, source_target_pairs={{0,8},{8,0},{16,24},{24,16},{1,9},{9,1},{17,25},{25,17},{2,10},{10... | collective-permute-start | bytes 2359304 | tf_op jit(solution)/shard_map/ppermute | solution.py:1031
  314.5 23.6 %collective-permute-start.17 = (bf16[2,4,64,512]{3,2,1,0:T(8,128)(2,1)}, bf16[2,4,64,512]{3,2,1,0:T(8,128)(2,1)}, u32[]{:S(2)}, u32[]{:S(2)}) collective-permute-start(bf16[2,4,64,512]{3,2,1,0:T(8,128)(2,1)} %get-tuple-element.246), channel_id=1, source_target_pairs={{0,1},{1,0},{2,3},{3,2},{4,5},{5,4},{6,7},{7,6},{8,9},{9,8},{10,11... | collective-permute-start | bytes 1572872 | tf_op jit(solution)/shard_map/ppermute | solution.py:904
  319.8 18.3 %collective-permute-start.20 = (bf16[128,1024]{1,0:T(8,128)(2,1)S(1)}, bf16[128,1024]{1,0:T(8,128)(2,1)S(1)}, u32[]{:S(2)}, u32[]{:S(2)}) collective-permute-start(bf16[128,1024]{1,0:T(8,128)(2,1)S(1)} %copy-done.43), channel_id=1, source_target_pairs={{1,0},{3,2},{5,4},{7,6},{9,8},{11,10},{13,12},{15,14},{17,16},{19,... | collective-permute-start | bytes 786440 | tf_op jit(solution)/shard_map/ppermute | solution.py:1142
  322.1 16.1 %copy-start.5 = (bf16[2,2,4,64,512]{4,3,2,1,0:T(8,128)(2,1)S(1)}, bf16[2,2,4,64,512]{4,3,2,1,0:T(8,128)(2,1)}, u32[]{:S(2)}) copy-start(bf16[2,2,4,64,512]{4,3,2,1,0:T(8,128)(2,1)} %get-tuple-element.235.refs_6_) | copy-start | bytes 3145732
  338.1 1.7 copy-start.31
  338.1 1.7 copy-start.36
  338.2 8.3 %copy-start.18 = (bf16[2,4,64,512]{3,2,1,0:T(8,128)(2,1)S(1)}, bf16[2,4,64,512]{3,2,1,0:T(8,128)(2,1)}, u32[]{:S(2)}) copy-start(bf16[2,4,64,512]{3,2,1,0:T(8,128)(2,1)} %get-tuple-element.245.refs_5_) | copy-start | bytes 1572868
  339.8 16.6 %copy-start.3 = (bf16[2,2,4,64,512]{4,3,2,1,0:T(8,128)(2,1)}, bf16[2,2,4,64,512]{4,3,2,1,0:T(8,128)(2,1)S(1)}, u32[]{:S(2)}) copy-start(bf16[2,2,4,64,512]{4,3,2,1,0:T(8,128)(2,1)S(1)} %add_convert_fusion.refs_6_) | copy-start | bytes 3145732
  340.9 13.3 %all-to-all-start = ((f32[32,1,256]{2,1,0:T(1,128)}), f32[32,1,256]{2,1,0:T(1,128)S(1)}, u32[]{:S(2)}, u32[]{:S(2)}) async-start(f32[32,1,256]{2,1,0:T(1,128)} %reshape.185), calls=%async_computation | async-start | bytes 65536 | tf_op jit(solution)/shard_map/all_to_all | solution.py:1164
  346.5 11.1 %copy-start.10 = (bf16[24,128,128]{2,1,0:T(8,128)(2,1)S(1)}, bf16[24,128,128]{2,1,0:T(8,128)(2,1)}, u32[]{:S(2)}) copy-start(bf16[24,128,128]{2,1,0:T(8,128)(2,1)} %pad_maximum_fusion.4.refs_7_) | copy-start | bytes 2359300
  347.8 11.2 %copy-start.16 = (bf16[2,4,64,512]{3,2,1,0:T(8,128)(2,1)}, bf16[2,4,64,512]{3,2,1,0:T(8,128)(2,1)S(1)}, u32[]{:S(2)}) copy-start(bf16[2,4,64,512]{3,2,1,0:T(8,128)(2,1)S(1)} %add_convert_fusion.17.refs_5_) | copy-start | bytes 1572868
  356.4 13.7 %collective-permute-start.22 = (bf16[2,4,64,512]{3,2,1,0:T(8,128)(2,1)}, bf16[2,4,64,512]{3,2,1,0:T(8,128)(2,1)S(1)}, u32[]{:S(2)}, u32[]{:S(2)}) collective-permute-start(bf16[2,4,64,512]{3,2,1,0:T(8,128)(2,1)} %slice_bitcast_fusion), channel_id=1, source_target_pairs={{0,1},{1,0},{2,3},{3,2},{4,5},{5,4},{6,7},{7,6},{8,9},{9,8},{10,11... | collective-permute-start | bytes 1572872 | tf_op jit(solution)/shard_map/ppermute | solution.py:904
  356.9 10.6 %collective-permute-start.21 = (bf16[4,64,512]{2,1,0:T(8,128)(2,1)S(1)}, bf16[4,64,512]{2,1,0:T(8,128)(2,1)S(1)}, u32[]{:S(2)}, u32[]{:S(2)}) collective-permute-start(bf16[4,64,512]{2,1,0:T(8,128)(2,1)S(1)} %slice_bitcast_fusion.5), channel_id=1, source_target_pairs={{0,4},{4,0},{1,5},{5,1},{2,6},{6,2},{3,7},{7,3},{8,12},{12,8},{9,1... | collective-permute-start | bytes 786440 | tf_op jit(solution)/shard_map/ppermute | solution.py:904
  359.9 24.0 %collective-permute-start.24 = (bf16[3,4,128,128]{3,2,1,0:T(8,128)(2,1)}, bf16[3,4,128,128]{3,2,1,0:T(8,128)(2,1)}, u32[]{:S(2)}, u32[]{:S(2)}) collective-permute-start(bf16[3,4,128,128]{3,2,1,0:T(8,128)(2,1)} %get-tuple-element.249), channel_id=1, source_target_pairs={{0,16},{16,0},{8,24},{24,8},{1,17},{17,1},{9,25},{25,9},{2,18},{18... | collective-permute-start | bytes 1179656 | tf_op jit(solution)/shard_map/ppermute | solution.py:1035
  360.2 9.9 %copy-start.17 = (bf16[2,4,64,512]{3,2,1,0:T(8,128)(2,1)S(1)}, bf16[2,4,64,512]{3,2,1,0:T(8,128)(2,1)}, u32[]{:S(2)}) copy-start(bf16[2,4,64,512]{3,2,1,0:T(8,128)(2,1)} %copy-done.16) | copy-start | bytes 1572868
  360.2 10.0 %copy-start.4 = (bf16[2,2,4,64,512]{4,3,2,1,0:T(8,128)(2,1)S(1)}, bf16[2,2,4,64,512]{4,3,2,1,0:T(8,128)(2,1)}, u32[]{:S(2)}) copy-start(bf16[2,2,4,64,512]{4,3,2,1,0:T(8,128)(2,1)} %copy-done.3) | copy-start | bytes 3145732
  370.2 2.7 copy-start.14
  370.4 3.4 copy-start
  370.5 21.4 %collective-permute-start.23 = (bf16[3,2,64,512]{3,2,1,0:T(8,128)(2,1)S(1)}, bf16[3,2,64,512]{3,2,1,0:T(8,128)(2,1)S(1)}, u32[]{:S(2)}, u32[]{:S(2)}) collective-permute-start(bf16[3,2,64,512]{3,2,1,0:T(8,128)(2,1)S(1)} %fusion.18), channel_id=1, source_target_pairs={{0,8},{8,0},{16,24},{24,16},{1,9},{9,1},{17,25},{25,17},{2,10},{10... | collective-permute-start | bytes 1179656 | tf_op jit(solution)/shard_map/ppermute | solution.py:1179
  373.9 18.0 %copy-start.21 = (bf16[3,4,128,128]{3,2,1,0:T(8,128)(2,1)S(1)}, bf16[3,4,128,128]{3,2,1,0:T(8,128)(2,1)}, u32[]{:S(2)}) copy-start(bf16[3,4,128,128]{3,2,1,0:T(8,128)(2,1)} %get-tuple-element.232.refs_7_) | copy-start | bytes 1179652
  394.2 2.4 copy-start.1
  394.2 2.3 copy-start.15
  394.3 14.3 %collective-permute-start.27 = (bf16[2,2,2,2,64,128]{5,4,3,2,1,0:T(8,128)(2,1)S(1)}, bf16[2,2,2,2,64,128]{5,4,3,2,1,0:T(8,128)(2,1)S(1)}, u32[]{:S(2)}, u32[]{:S(2)}) collective-permute-start(bf16[2,2,2,2,64,128]{5,4,3,2,1,0:T(8,128)(2,1)S(1)} %get-tuple-element.254), channel_id=1, source_target_pairs={{0,2},{2,0},{1,3},{3,1},{4,6},{6,4},{5,7},{7,5},{8,10},{10,8},{9,1... | collective-permute-start | bytes 786440 | tf_op jit(solution)/shard_map/ppermute | solution.py:904
  395.7 4.5 %collective-permute-start.26 = (bf16[64,512]{1,0:T(8,128)(2,1)S(1)}, bf16[64,512]{1,0:T(8,128)(2,1)S(1)}, u32[]{:S(2)}, u32[]{:S(2)}) collective-permute-start(bf16[64,512]{1,0:T(8,128)(2,1)S(1)} %bitcast.159), channel_id=1, source_target_pairs={{0,1},{1,0},{2,3},{3,2},{4,5},{5,4},{6,7},{7,6},{8,9},{9,8},{10,11... | collective-permute-start | bytes 196616 | tf_op jit(solution)/shard_map/ppermute | solution.py:904
  396.6 11.1 %collective-permute-start.25 = (bf16[3,64,512]{2,1,0:T(8,128)(2,1)S(1)}, bf16[3,64,512]{2,1,0:T(8,128)(2,1)S(1)}, u32[]{:S(2)}, u32[]{:S(2)}) collective-permute-start(bf16[3,64,512]{2,1,0:T(8,128)(2,1)S(1)} %slice_bitcast_fusion.6), channel_id=1, source_target_pairs={{0,16},{16,0},{8,24},{24,8},{1,17},{17,1},{9,25},{25,9},{2,18},{18... | collective-permute-start | bytes 589832 | tf_op jit(solution)/shard_map/ppermute | solution.py:1194
  (10 other events, 12.5 us)
Sparse Core Ops, SparseCore 0:
  319.0 67.7 reduce-scatter.1

commit v3 on v2

--- a/solution.py
+++ b/solution.py
@@ -435,9 +435,18 @@
         n_ref[...] = jnp.zeros_like(n_ref)
 
 
+def staged(count, *stages):
+    kept = [{} for _ in stages]
+    for step in range(count + len(stages) - 1):
+        for k, stage in enumerate(stages):
+            i = step - k
+            if 0 <= i < count:
+                kept[k][i] = stage(i, kept[k - 1].pop(i)) if k else stage(i)
+
+
 def window_bias(info, clip, block):
-    i = lax.broadcasted_iota(jnp.int32, (2 * TILE, 2 * TILE), 0) % TILE
-    j = lax.broadcasted_iota(jnp.int32, (2 * TILE, 2 * TILE), 1)
+    j = lax.broadcasted_iota(jnp.int32, (2 * TILE, 2 * TILE), 0)
+    i = lax.broadcasted_iota(jnp.int32, (2 * TILE, 2 * TILE), 1) % TILE
     key = info[3] + (block - 1) * TILE + j
     allowed = (j > i) & (j <= i + TILE) & (key >= 0) & (key < info[LEN0 + clip])
     return jnp.where(allowed, 0.0, MASKED)
@@ -451,9 +460,8 @@
     )
 
 
-def one_row(values):
-    lane = lax.broadcasted_iota(jnp.int32, (TILE, TILE), 1)
-    return jnp.where(lane < 64, values[:TILE], values[TILE:])
+def one_row(turned):
+    return jnp.concatenate([turned[:64, :TILE], turned[64:, TILE:]], axis=0).T
 
 
 def key_window(halo_ref, own_ref, block, at, own_at):
@@ -468,28 +476,34 @@
     clip = pl.program_id(0)
     width = ctx_ref.shape[1]
     at_rows = slice(block * TILE, (block + 1) * TILE)
-    live = info[3] + block * TILE < info[LEN0 + clip]
+    live = info[3] < info[LEN0 + clip]
 
     @pl.when(live)
     def _():
         bias = window_bias(info, clip, block)
-        lane = lax.broadcasted_iota(jnp.int32, (TILE, TILE), 1)
-        totals = jnp.zeros((TILE, TILE), F32)
-        for pair in range(width // TILE):
+
+        def score(pair):
             at = pair * TILE
-            queries = two_heads(qkv_ref[at_rows, at : at + TILE])
-            keys = key_window(kvh_ref, qkv_ref, block, at, width + at)
+            queries = two_heads(qkv_ref[at_rows, at : at + TILE] * BF(scale))
+            return mm_t(key_window(kvh_ref, qkv_ref, block, at, width + at), queries)
+
+        def weigh(pair, scores):
+            scores = scores + bias
+            top = jnp.max(scores, axis=0, keepdims=True)
+            exponent = jnp.exp(scores - top)
+            total = jnp.sum(exponent, axis=0, keepdims=True)
+            lse_ref[0, pair : pair + 1, :] = top + jnp.log(total)
+            return (exponent * (1.0 / total)).astype(BF)
+
+        def gather(pair, weights):
+            at = pair * TILE
             values = key_window(kvh_ref, qkv_ref, block, width + at, 2 * width + at)
-            scores = mm_t(queries, keys) * scale + bias
-            top = jnp.max(scores, axis=1, keepdims=True)
-            exponent = jnp.exp(scores - top)
-            total = jnp.sum(exponent, axis=1, keepdims=True)
-            weights = (exponent * (1.0 / total)).astype(BF)
-            ctx_ref[:, at : at + TILE] = one_row(mm(weights, values)).astype(BF)
-            log_total = top + jnp.log(total)
-            totals = jnp.where(lane == 2 * pair, log_total[:TILE], totals)
-            totals = jnp.where(lane == 2 * pair + 1, log_total[TILE:], totals)
-        lse_ref[...] = totals
+            return t_mm(values, weights)
+
+        def put(pair, turned):
+            ctx_ref[:, pair * TILE : (pair + 1) * TILE] = one_row(turned).astype(BF)
+
+        staged(width // TILE, score, weigh, gather, put)
 
     @pl.when(jnp.logical_not(live))
     def _():
@@ -502,68 +516,78 @@
 
 
 def attend_back_kernel(
-    scale, first_clip, info, qkv_ref, kvh_ref, dctx_ref, lse_ref, tab_ref, tabh_ref, md_ref, mdh_ref, dk_acc, dv_acc
+    scale, first_clip, info, qkv_ref, kvh_ref, dctx_ref, lse_ref, tab_ref, tabh_ref, md_ref, mdh_ref
 ):
     clip = pl.program_id(0) + first_clip
     rows, width = dctx_ref.shape
-    blocks = rows // TILE
-    first_live = info[3] < info[LEN0 + clip]
-
-    @pl.when(jnp.logical_not(first_live))
+    live = info[3] < info[LEN0 + clip]
+
+    @pl.when(jnp.logical_not(live))
     def _():
         md_ref[...] = jnp.zeros_like(md_ref)
         mdh_ref[...] = jnp.zeros_like(mdh_ref)
 
-    @pl.when(first_live)
-    def _():
-        dk_acc[...] = jnp.zeros_like(dk_acc)
-        dv_acc[...] = jnp.zeros_like(dv_acc)
-        for block in range(blocks):
-            at_rows = slice(block * TILE, (block + 1) * TILE)
-            key_rows = slice(block * TILE, (block + 2) * TILE)
-            live = info[3] + block * TILE < info[LEN0 + clip]
-
-            @pl.when(live)
-            def _():
-                bias = window_bias(info, clip, block)
-                for pair in range(width // TILE):
-                    at = pair * TILE
-                    queries = two_heads(qkv_ref[at_rows, at : at + TILE])
-                    delta = two_heads(dctx_ref[at_rows, at : at + TILE])
-                    keys = key_window(kvh_ref, qkv_ref, block, at, width + at)
-                    values = key_window(kvh_ref, qkv_ref, block, width + at, 2 * width + at)
-                    log_total = jnp.concatenate(
-                        [
-                            lse_ref[at_rows, 2 * pair : 2 * pair + 1],
-                            lse_ref[at_rows, 2 * pair + 1 : 2 * pair + 2],
-                        ],
-                        axis=0,
-                    )
-                    weights = jnp.exp(mm_t(queries, keys) * scale + bias - log_total)
-                    weight_delta = mm_t(delta, values)
-                    inner = jnp.sum(weight_delta * weights, axis=1, keepdims=True)
-                    product_delta = (weights * (weight_delta - inner) * scale).astype(BF)
-                    query_delta = one_row(mm(product_delta, keys))
-                    md_ref[at_rows, at : at + TILE] = turn(
-                        query_delta, tab_ref[0, at_rows], -tab_ref[1, at_rows], -tab_ref[2, at_rows]
-                    ).astype(BF)
-                    dk_acc[key_rows, at : at + TILE] += t_mm(product_delta, queries)
-                    dv_acc[key_rows, at : at + TILE] += t_mm(weights.astype(BF), delta)
-
-            @pl.when(jnp.logical_not(live))
-            def _():
-                md_ref[at_rows, 0:width] = jnp.zeros((TILE, width), BF)
-
-        for pair in range(width // TILE):
-            at = pair * TILE
-            mdh_ref[:, at : at + TILE] = turn(
-                dk_acc[:TILE, at : at + TILE], tabh_ref[0], -tabh_ref[1], -tabh_ref[2]
+    @pl.when(live)
+    def _():
+        biases = [window_bias(info, clip, block) for block in range(2)]
+
+        def place(item):
+            pair, block = divmod(item, 2)
+            return pair, block, pair * TILE, slice(block * TILE, (block + 1) * TILE)
+
+        def score(item):
+            pair, block, at, at_rows = place(item)
+            queries = two_heads(qkv_ref[at_rows, at : at + TILE] * BF(scale))
+            delta = two_heads(dctx_ref[at_rows, at : at + TILE])
+            keys = key_window(kvh_ref, qkv_ref, block, at, width + at)
+            values = key_window(kvh_ref, qkv_ref, block, width + at, 2 * width + at)
+            return mm_t(keys, queries), mm_t(values, delta)
+
+        def weigh(item, scores):
+            pair, block, at, at_rows = place(item)
+            products, weight_delta = scores
+            weights = jnp.exp(products + biases[block] - lse_ref[block, pair : pair + 1, :])
+            inner = jnp.sum(weight_delta * weights, axis=0, keepdims=True)
+            return weights.astype(BF), (weights * (weight_delta - inner)).astype(BF)
+
+        def gather(item, weighed):
+            pair, block, at, at_rows = place(item)
+            weights, score_delta = weighed
+            queries = two_heads(qkv_ref[at_rows, at : at + TILE] * BF(scale))
+            delta = two_heads(dctx_ref[at_rows, at : at + TILE])
+            keys = key_window(kvh_ref, qkv_ref, block, at, width + at)
+            return t_mm(keys, score_delta), mm(score_delta, queries), mm(weights, delta)
+
+        before = {}
+        early, late = slice(0, TILE), slice(TILE, 2 * TILE)
+
+        def put_key(where, at, delta):
+            md_ref[where, width + at : width + at + TILE] = turn(
+                delta, tab_ref[0, where], -tab_ref[1, where], -tab_ref[2, where]
             ).astype(BF)
-            md_ref[:, width + at : width + at + TILE] = turn(
-                dk_acc[TILE:, at : at + TILE], tab_ref[0], -tab_ref[1], -tab_ref[2]
+
+        def put(item, deltas):
+            pair, block, at, at_rows = place(item)
+            turned, key_delta, value_delta = deltas
+            md_ref[at_rows, at : at + TILE] = turn(
+                one_row(turned) * scale,
+                tab_ref[0, at_rows], -tab_ref[1, at_rows], -tab_ref[2, at_rows],
             ).astype(BF)
-        mdh_ref[:, width:] = dv_acc[0:TILE, :].astype(BF)
-        md_ref[:, 2 * width :] = dv_acc[TILE:, :].astype(BF)
+            value_at = slice(2 * width + at, 2 * width + at + TILE)
+            if block == 0:
+                mdh_ref[:, at : at + TILE] = turn(
+                    key_delta[early], tabh_ref[0], -tabh_ref[1], -tabh_ref[2]
+                ).astype(BF)
+                mdh_ref[:, width + at : width + at + TILE] = value_delta[early].astype(BF)
+                before[pair] = key_delta[late], value_delta[late]
+            else:
+                key_before, value_before = before.pop(pair)
+                put_key(early, at, key_before + key_delta[early])
+                put_key(late, at, key_delta[late])
+                md_ref[early, value_at] = (value_before + value_delta[early]).astype(BF)
+                md_ref[late, value_at] = value_delta[late].astype(BF)
+
+        staged(2 * (width // TILE), score, weigh, gather, put)
 
 
 def out_kernel(info, ctx_ref, x_ref, w_ref, gb_ref, att_ref, n_ref):
@@ -592,13 +616,13 @@
 def output_kernel(info, x_ref, att_ref, ba_ref, bb_ref, gb_ref, out_ref):
     r = pl.program_id(0)
     valid = row_valid(info, r, x_ref.shape[0])
-    branch = ba_ref[...].astype(F32) + bb_ref[0].astype(F32)
+    branch = ba_ref[...].astype(F32) + bb_ref[...].astype(F32)
     middle = x_ref[...].astype(F32) + gb_ref[2:3, :] * att_ref[...]
     out_ref[...] = ((middle + gb_ref[3:4, :] * branch) * valid).astype(BF)
 
 
 def out_back_kernel(
-    info, sa_ref, sb_ref, ba_ref, bb_ref, att_ref, x_ref, ct_ref, ctx_ref, w_ref, gb_ref,
+    info, sa_ref, sb_ref, att_ref, x_ref, ct_ref, ctx_ref, w_ref, gb_ref,
     delta_ref, dctx_ref, out_ref, sum_ref, acc,
 ):
     r = pl.program_id(0)
@@ -617,11 +641,9 @@
         attended = att_ref[...]
         middle = x_ref[...].astype(F32) + gb_ref[2:3, :] * attended
         normal, inverse = norm_stats(middle)
-        second = sa_ref[...].astype(F32) + sb_ref[0].astype(F32)
+        second = sa_ref[...].astype(F32) + sb_ref[...].astype(F32)
         back = norm_back(second, normal, inverse, gb_ref[1:2, :])
         output_delta = ct_ref[...].astype(F32) * valid
-        branch = ba_ref[...].astype(F32) + bb_ref[0].astype(F32)
-        sum_ref[3:4, :] += column_sum(output_delta * branch)
         middle_delta = output_delta + back
         delta_ref[...] = middle_delta
         attended_delta = (middle_delta * gb_ref[2:3, :]).astype(BF)
@@ -730,11 +752,17 @@
         out_ref[split:, :] = part_ref[split:, :].astype(BF)
 
 
+def hidden_block(info, c, k):
+    z0, x, q = k // 4, k // 2 % 2, k % 2
+    d = ((info[0] + x) % 2 * 2 + z0) * 4 + (info[1] + q) % 2 * 2 + info[2]
+    return pl.ds(pl.multiple_of(d * 256 + c * TILE, TILE), TILE)
+
+
 def ffn_kernel(c, first, half, info, n_own, n_other, b_own, b_other, *rest):
     if not first:
-        earlier, rest = rest[:3], rest[3:]
-    wg_hbm, wu_hbm, wd_hbm, *rest = rest
-    sums, rest = rest[:3], rest[3:]
+        earlier, rest = rest[:2], rest[2:]
+    wg_hbm, wu_hbm, wd_hbm, hidden_ref, *rest = rest
+    sums, rest = rest[:2], rest[2:]
     packs, rest = (rest[0:2], rest[2:4]), rest[4:]
     wg, wu, wd, ag, au, ad, n_buf, b_buf, sems, row_sems = rest
     r = pl.program_id(0)
@@ -744,10 +772,7 @@
     def weight_copies(kind):
         hbm, vmem = ((wg_hbm, wg), (wu_hbm, wu), (wd_hbm, wd))[kind]
         for k in range(8):
-            z0, x, q = k // 4, k // 2 % 2, k % 2
-            d = ((info[0] + x) % 2 * 2 + z0) * 4 + (info[1] + q) % 2 * 2 + info[2]
-            src = pl.ds(pl.multiple_of(d * 256 + c * TILE, TILE), TILE)
-            dst = pl.ds(k * TILE, TILE)
+            src, dst = hidden_block(info, c, k), pl.ds(k * TILE, TILE)
             if kind < 2:
                 yield pltpu.make_async_copy(hbm.at[:, src], vmem.at[:, dst], sems.at[kind, k])
             else:
@@ -802,16 +827,13 @@
     hidden = (active * upward).astype(BF)
     up_delta = (hidden_delta * active).astype(BF)
     gate_delta = (hidden_delta * upward * (sigmoid + active * (1.0 - sigmoid))).astype(BF)
-    branch = mm(hidden, wd[...])
+    hidden_ref[...] = hidden
     second = mm_t(gate_delta, wg[...]) + mm_t(up_delta, wu[...])
     if not first:
-        branch = branch + jnp.where(r < half, earlier[0][...], earlier[2][0]).astype(F32)
-        second = second + jnp.where(r < half, earlier[1][...], earlier[2][1]).astype(F32)
-    branch, second = branch.astype(BF), second.astype(BF)
-    sums[0][...] = branch
+        second = second + jnp.where(r < half, earlier[0][...], earlier[1][...]).astype(F32)
+    second = second.astype(BF)
+    sums[0][...] = second
     sums[1][...] = second
-    sums[2][0] = branch
-    sums[2][1] = second
     ag[...] += t_mm(normed[...], gate_delta)
     au[...] += t_mm(normed[...], up_delta)
     ad[...] += t_mm(delta[...], hidden)
@@ -855,7 +877,8 @@
     first = previous is None
     hidden = 8 * TILE
     own = pl.BlockSpec((block_rows, width), lambda r, info: (jnp.minimum(r, half), 0))
-    other = pl.BlockSpec((2, block_rows, width), lambda r, info: (0, jnp.maximum(r - half, 0), 0))
+    other = pl.BlockSpec((block_rows, width), lambda r, info: (jnp.maximum(r - half, 0), 0))
+    every = pl.BlockSpec((block_rows, hidden), lambda r, info: (r, 0))
     packed = (2, 24 * TILE, TILE)
     pack = pl.BlockSpec(packed, lambda r, info: (0, 0, 0), pipeline_mode=pl.Buffered(1))
     extra = [] if first else list(previous)
@@ -866,9 +889,11 @@
         [*pieces, *extra, *weights],
         name="feed_forward",
         grid=(2 * half,),
-        ins=[anywhere] * 4 + [own, own, other] * (len(extra) // 3) + [anywhere] * 3,
-        outs=[own, own, other] + [pack] * 4,
-        shapes=[shape_of((rows + block_rows, width))] * 2 + [shape_of((2, rows, width))] + [shape_of(packed)] * 4,
+        ins=[anywhere] * 4 + [own, other] * (len(extra) // 2) + [anywhere] * 3,
+        outs=[every, own, other] + [pack] * 4,
+        shapes=[
+            shape_of((2 * rows, hidden)), shape_of((rows + block_rows, width)), shape_of((rows, width))
+        ] + [shape_of(packed)] * 4,
         scratch=[
             pltpu.VMEM((width, hidden), BF),
             pltpu.VMEM((width, hidden), BF),
@@ -887,6 +912,52 @@
     )
 
 
+def branch_kernel(half, info, ha, hb, b_own, b_other, wd_hbm, own_ref, other_ref, sum_ref, wd, sems):
+    r = pl.program_id(0)
+
+    def copies():
+        for c in range(2):
+            for k in range(8):
+                dst = wd.at[c, pl.ds(k * TILE, TILE), :]
+                yield pltpu.make_async_copy(wd_hbm.at[hidden_block(info, c, k), :], dst, sems.at[c, k])
+
+    @pl.when(r == 0)
+    def _():
+        for copy in copies():
+            copy.start()
+        sum_ref[...] = jnp.zeros_like(sum_ref)
+        for copy in copies():
+            copy.wait()
+
+    branch = mm(ha[...], wd[0]) + mm(hb[...], wd[1])
+    delta = jnp.where(r < half, b_own[...], b_other[...]).astype(F32)
+    sum_ref[0:1, :] += column_sum(delta * branch)
+    branch = branch.astype(BF)
+    own_ref[...] = branch
+    other_ref[...] = branch
+
+
+def branch_call(info, hiddens, deltas, down_weight, after, block_rows=512):
+    rows, width = deltas[0].shape
+    half = rows // block_rows
+    hidden = hiddens[0].shape[1]
+    every = pl.BlockSpec((block_rows, hidden), lambda r, info: (r, 0))
+    own = pl.BlockSpec((block_rows, width), lambda r, info: (jnp.minimum(r, half), 0))
+    own_in = pl.BlockSpec((block_rows, width), lambda r, info: (jnp.minimum(r, half - 1), 0))
+    other = pl.BlockSpec((block_rows, width), lambda r, info: (jnp.maximum(r - half, 0), 0))
+    return call_kernel(
+        functools.partial(branch_kernel, half), info, [*hiddens, *deltas, down_weight],
+        name="branch", grid=(2 * half,),
+        ins=[every, every, own_in, other, pl.BlockSpec(memory_space=pl.ANY)],
+        outs=[own, other, whole_spec((8, width))],
+        shapes=[
+            shape_of((rows + block_rows, width)), shape_of((rows, width)), shape_of((8, width), F32)
+        ],
+        scratch=[pltpu.VMEM((2, hidden, width), BF), pltpu.SemaphoreType.DMA((2, 8))],
+        cost=(4 * 2 * rows * width * hidden, 16 * MIB), after=after,
+    )
+
+
 SWAP = [(0, 1), (1, 0)]
 Z_NEAR = [(0, 1), (1, 0), (2, 3), (3, 2)]
 Z_FAR = [(0, 2), (2, 0), (1, 3), (3, 1)]
@@ -970,9 +1041,6 @@
     w_out = whole_spec((width, width))
     sums = whole_spec((8, width))
 
-    def half_sums(part):
-        return pl.BlockSpec((1, rows, width), lambda r, info: (part, r, 0))
-
     grid = (clips,)
     mac = 2 * count * width * width
 
@@ -984,10 +1052,15 @@
     def half_rows(width, part):
         return pl.BlockSpec((TILE, width), lambda r, info: (2 * r + part, 0))
 
-    seen = [shape_of((count, width)), shape_of((count, TILE), F32)]
+    totals_of = (2 * clips, width // TILE, 2 * TILE)
+    seen = [shape_of((count, width)), shape_of(totals_of, F32)]
+
+    def half_totals(part):
+        return pl.BlockSpec((1, *totals_of[1:]), lambda r, info: (2 * r + part, 0, 0))
+
     late = call_kernel(
         functools.partial(attend_late_kernel, scale), info, [qkv], name="attend_late", grid=grid,
-        ins=[qkv_rows], outs=[half_rows(width, 1), half_rows(TILE, 1)], shapes=seen,
+        ins=[qkv_rows], outs=[half_rows(width, 1), half_totals(1)], shapes=seen,
         cost=(2 * mac, 8 * MIB),
     )
     halo, branch_delta = lax.optimization_barrier((halo, branch_delta))
@@ -1002,7 +1075,7 @@
     context, log_totals = call_kernel(
         functools.partial(attend_kernel, scale, 0), info, [qkv, kv_halo], name="attend_early",
         grid=grid, ins=[half_rows(3 * width, 0), kv_rows],
-        outs=[half_rows(width, 0), half_rows(TILE, 0)], shapes=seen,
+        outs=[half_rows(width, 0), half_totals(0)], shapes=seen,
         cost=(2 * mac, 12 * MIB), onto=late,
     )
     attended, normed_two = call_kernel(
@@ -1040,21 +1113,21 @@
         )
         return state, ((keep_a, send_a), (keep_b, send_b))
 
-    previous, grads_0 = run_ffn(0, None, ())
+    (hidden_0, *previous), grads_0 = run_ffn(0, None, ())
     moved_0 = start_pair(grads_0)
-    (branch, second, sums_sent), grads_1 = run_ffn(1, previous, ())
-    branch, second, sums_sent, grads_1, moved_0 = meet(branch, second, sums_sent, grads_1, moved_0)
-    sums_other = swap(sums_sent, "core")
-    grads_1, sums_other = meet(grads_1, sums_other)
+    (hidden_1, second, second_sent), grads_1 = run_ffn(1, previous, ())
+    second, second_sent, grads_1, moved_0 = meet(second, second_sent, grads_1, moved_0)
+    second_other = swap(second_sent, "core")
     totals_0 = halves(moved_0)
+    grads_1, second_other, totals_0 = meet(grads_1, second_other, totals_0)
     moved_0 = second_pair(totals_0)
     moved_1 = start_pair(grads_1)
 
     middle_delta, context_delta, out_grad, sums_two = call_kernel(
         out_back_kernel, info,
-        [second, sums_other, branch, sums_other, attended, flat, tangent, context, out_weight, table],
+        [second, second_other, attended, flat, tangent, context, out_weight, table],
         name="project_back", grid=grid,
-        ins=[own, half_sums(1), own, half_sums(0), own, own, own, own, w_out, gb],
+        ins=[own, own, own, own, own, own, w_out, gb],
         outs=[own, own, w_out, sums],
         shapes=[
             shape_of((count, width), F32), shape_of((count, width)), shape_of((width, width)),
@@ -1073,12 +1146,12 @@
             [qkv, kv_halo, context_delta, log_totals, own_turns, halo_turns],
             name="attend_back", grid=(taken,),
             ins=[
-                at(rows, 3 * width), at(TILE, 2 * width), at(rows, width), at(rows, TILE),
+                at(rows, 3 * width), at(TILE, 2 * width), at(rows, width),
+                pl.BlockSpec((2, *totals_of[1:]), lambda r, info: (r + first_clip, 0, 0)),
                 own_tab, halo_tab,
             ],
             outs=[at(rows, 3 * width), at(TILE, 2 * width)],
             shapes=[shape_of((count, 3 * width)), shape_of((clips * TILE, 2 * width))],
-            scratch=[pltpu.VMEM((rows + TILE, width), F32), pltpu.VMEM((rows + TILE, width), F32)],
             cost=(2.5 * mac * taken, 6 * MIB * taken), after=after, onto=onto,
         )
 
@@ -1097,15 +1170,19 @@
         )
 
     mixed = attend_back(0, (), (), some)
-    mixed, moved_0, moved_1 = meet(mixed, moved_0, moved_1)
+    branch, branch_sent, sums_branch = branch_call(
+        info, (hidden_0, hidden_1), (branch_delta, branch_delta_other), down_weight, (mixed[1],)
+    )
+    mixed, moved_0, moved_1, branch_sent = meet(mixed, moved_0, moved_1, branch_sent)
     totals_1 = halves(moved_1)
     moved_1 = second_pair(totals_1)
     near_0 = near_pair(moved_0)
+    branch_other = swap(branch_sent, "core")
     ready = (*(t for pair in totals_1 for t in pair), near_0[0])
     back_a, sums_a = first_halo(0, mixed[1], ready, some)
     mixed_delta, mixed_halo = attend_back(some, mixed, (back_a,), clips - some)
-    mixed_delta, mixed_halo, back_a, moved_1, near_0 = meet(
-        mixed_delta, mixed_halo, back_a, moved_1, near_0
+    mixed_delta, mixed_halo, back_a, moved_1, near_0, branch_other = meet(
+        mixed_delta, mixed_halo, back_a, moved_1, near_0, branch_other
     )
     came_a = lax.ppermute(back_a, "seq", [(1, 0)])
     far_0 = far_pair(near_0)
@@ -1157,22 +1234,23 @@
     share = width // 16
     ones = sums_one + sums_a + sums_b
     nought = jnp.zeros((width,), F32)
+    scale_mlp = sums_branch[0] / gain_table[:, 3]
     vectors = jnp.stack(
-        [ones[0], sums_two[0], ones[1], nought, sums_two[1], sums_two[3], sums_two[2], nought]
-    )
-    vectors = vectors.reshape(2, 4, 16, share).transpose(2, 0, 1, 3).reshape(32, 4, share)
-    vectors = lax.all_to_all(vectors, ("z", "y", "core", "seq"), 0, 0, tiled=True)
+        [ones[0], sums_two[0], ones[1], nought, sums_two[1], scale_mlp, sums_two[2], nought]
+    )
     left, right = plus(stay_l, go_l), plus(stay_r, go_r)
-    vectors, left, right, near_1 = meet(vectors, left, right, near_1)
     go_l, go_r = swap(left[1], "y"), swap(right[1], "seq")
+    vectors_core = swap(vectors, "core")
     far_1 = far_pair(near_1)
     output = call_kernel(
-        output_kernel, info, [flat, attended, branch, sums_other, table],
-        name="output", grid=grid, ins=[own, own, own, half_sums(0), gb], outs=own,
+        output_kernel, info, [flat, attended, branch, branch_other, table],
+        name="output", grid=grid, ins=[own, own, own, own, gb], outs=own,
         shapes=shape_of((count, width)), cost=(0, 14 * MIB),
-        after=(left, right, far_1[0], came_b),
-    )
-    go_l, go_r, output = meet(go_l, go_r, output)
+        after=(left, right, far_1[0], came_b, vectors),
+    )
+    go_l, go_r, vectors_core, output = meet(go_l, go_r, vectors_core, output)
+    vectors = vectors + vectors_core
+    vectors_x = swap(vectors, "seq")
     left, right = plus(left[0], go_l), plus(right[0], go_r)
     qkv_total = jnp.concatenate([left[None], right]).reshape(3, 2, 2, 64, cut)
     qkv_near = qkv_total[:, :, 1]
@@ -1187,18 +1265,24 @@
             own, gb,
         ],
         outs=own, shapes=shape_of((count, width)), cost=(0, 8 * MIB),
-        after=(left, right, output, qkv_total),
-    )
-    go, far_1, input_grad = meet(go, far_1, input_grad)
+        after=(left, right, output, qkv_total, vectors),
+    )
+    go, far_1, vectors_x, input_grad = meet(go, far_1, vectors_x, input_grad)
+    vectors = vectors + vectors_x
+    vectors = vectors + swap(vectors, "y")
+    vectors = vectors + lax.ppermute(vectors, "z", Z_NEAR)
+    vectors = vectors + lax.ppermute(vectors, "z", Z_FAR)
     qkv_total = plus(qkv_total[:, :, 0], go)
     qkv_total = plus(qkv_total[:, 0], lax.ppermute(qkv_total[:, 1], "z", Z_FAR))
     qkv_grad = qkv_total.transpose(1, 0, 2).reshape(-1, 3 * cut).astype(F32)
-    out_halves = later(out_grad, input_grad).reshape(-1, 2, width // 2)
+    out_halves = later(out_grad, qkv_total).reshape(-1, 2, width // 2)
     out_kept = lax.dynamic_index_in_dim(out_halves, x_at, axis=1, keepdims=False)
     out_sent = lax.dynamic_index_in_dim(out_halves, 1 - x_at, axis=1, keepdims=False)
     out_grad = out_kept.astype(F32) + swap(out_sent, "seq").astype(F32)
 
-    vectors = jnp.sum(vectors, axis=0).T
+    vectors = vectors.reshape(2, 4, 16, share).transpose(2, 0, 1, 3).reshape(32, 4, share)
+    seat = ((z_at * 2 + y_at) * 2 + core_at) * 2 + x_at
+    vectors = lax.dynamic_index_in_dim(vectors, seat, keepdims=False).T
     gain_grad, bias_grad = vectors[:, :2], vectors[:, 2:3]
 
     tiles = jnp.stack([plus(*far_0), plus(*far_1)])

time: 427 us -> 407 us (0.953)
  waiting for transfers between devices: 52.9 us -> 35 us
  Pallas kernels: 264 us -> 254 us
  starting transfers between devices: 34.4 us -> 41.7 us
    pallas_call x16 -> x17, Pallas kernels: 264 us -> 254 us  [call_kernel(): pl.pallas_call(run, grid_spec=pltpu.PrefetchScalarGridSpec(num_scalar_pre...]
    ppermute x19 -> x23, waiting for transfers between devices: 26.4 us -> 18.6 us  [swap(): return lax.ppermute(values, axis, SWAP)]
    ppermute x1, waiting for transfers between devices: 6.88 us -> 0.01 us  [fast_body(): qkv_total = plus(qkv_total[:, 0], lax.ppermute(qkv_total[:, 1], 'z', Z_FAR))]
    all_to_all x1 -> x0, waiting for transfers between devices: 6.47 us -> none  [fast_body(): lax.all_to_all(vectors, ('z', 'y', 'core', 'seq'), 0, 0, tiled=True)]
    ppermute x0 -> x2, starting transfers between devices: none -> 6.2 us  [the longest x1 3.6 us: fast_body(): vectors = vectors + lax.ppermute(vectors, 'z', Z_FAR)]
    ppermute x0 -> x2, waiting for transfers between devices: none -> 5.85 us  [the longest x1 3.11 us: fast_body(): vectors = vectors + lax.ppermute(vectors, 'z', Z_NEAR)]
    all_to_all x1 -> x0, starting transfers between devices: 5.58 us -> none  [fast_body(): lax.all_to_all(vectors, ('z', 'y', 'core', 'seq'), 0, 0, tiled=True)]
    ppermute x19 -> x23, starting transfers between devices: 16.9 us -> 19.3 us  [swap(): return lax.ppermute(values, axis, SWAP)]
  transfers between devices with their start and end apart: 30 -> 35, of which waited for: 14 -> 16; matrix products, arithmetic and copies ran while one was open for 9% -> 9% of each run, Pallas kernels for 45% -> 52%
where the time goes in v3:
time: 407 us; the launch traced here: 400 us
  Pallas kernels  254 us (62%)
  starting transfers between devices  41.7 us (10%)
  waiting for transfers between devices  35 us (9%)
  other arithmetic  34.7 us (9%)
  local copies, waits for them, and re-layouts  19 us (5%)
  between operations  15.3 us (4%)
    pallas_call x17, Pallas kernels, call_kernel(): pl.pallas_call(run, grid_spec=pltpu.PrefetchScalarGridSpec(num_scalar_pre...  254 us
    convert_element_type x16, other arithmetic, plus(): return (left.astype(F32) + right.astype(F32)).astype(BF)  24.1 us
    ppermute x23, starting transfers between devices, swap(): return lax.ppermute(values, axis, SWAP)  19.3 us
    ppermute x23, waiting for transfers between devices, swap(): return lax.ppermute(values, axis, SWAP)  18.6 us
  transfers between devices with their start and end apart: 35, of which 16 were waited for; matrix products, arithmetic and copies ran while one was open for 9% of the time, Pallas kernels for 52%

profile of v3, /device:TPU:0, one launch (start us, length us, event | category | flops | bytes accessed | tf_op | source)
XLA Modules:
  0.0 399.9 jit_solution(16692448521250007500)
XLA Ops:
  7.3 2.4 slice.199
  9.6 4.9 %collective-permute-start = (bf16[512,1024]{1,0:T(8,128)(2,1)}, bf16[512,1024]{1,0:T(8,128)(2,1)S(1)}, u32[]{:S(2)}, u32[]{:S(2)}) collective-permute-start(bf16[512,1024]{1,0:T(8,128)(2,1)} %bitcast.7), channel_id=1, source_target_pairs={{0,1},{2,3},{4,5},{6,7},{8,9},{10,11},{12,13},{14,15},{16,17},{18,... | collective-permute-start | bytes 3145736 | tf_op jit(solution)/shard_map/ppermute | solution.py:1019
  16.0 13.4 %qkv.1 = (bf16[1024,3072]{1,0:T(8,128)(2,1)}, bf16[1024,1024]{1,0:T(8,128)(2,1)}) custom-call(s32[9]{0:T(128)} %concatenate.26.info, bf16[1024,1024]{1,0:T(8,128)(2,1)} %bitcast.138, bf16[1024,3072]{1,0:T(8,128)(2,1)} %refs_1_.9, f32[8,1024]{1,0:T(8,128)} %maximum_bitcast_fusion.refs_2_.refs_3_.refs_7_.refs_4_, f32[3,512,128]{2,1,0:T(8,128)} %constant.49.clone.refs_3_.refs_4_), custom_call_target="tpu_custom_call" | custom-call | flops 1610612736 | bytes 4194304 | tf_op jit(solution)/shard_map/qkv/pallas_call | solution.py:328
  29.5 9.4 %attend_late.1 = (bf16[1024,1024]{1,0:T(8,128)(2,1)}, f32[8,8,256]{2,1,0:T(8,128)}) custom-call(s32[9]{0:T(128)} %concatenate.26.info, bf16[1024,3072]{1,0:T(8,128)(2,1)} %get-tuple-element.127.refs_0_), custom_call_target="tpu_custom_call" | custom-call | flops 1073741824 | bytes 2097152 | tf_op jit(solution)/shard_map/attend_late/pallas_call | solution.py:328
  38.9 2.1 multiply_convert_fusion.refs_2_
  42.1 5.9 %halo.1 = (bf16[512,2048]{1,0:T(8,128)(2,1)}, bf16[512,1024]{1,0:T(8,128)(2,1)}) custom-call(s32[9]{0:T(128)} %concatenate.26.info, bf16[512,1024]{1,0:T(8,128)(2,1)} %copy-done.2, bf16[1024,3072]{1,0:T(8,128)(2,1)} %refs_1_.9, bf16[1024,3072]{1,0:T(8,128)(2,1)} %refs_1_.9, f32[8,1024]{1,0:T(8,128)} %maximum_bitcast_fusion.refs_2_.refs_3_.refs_7_.refs_4_, ...), custom_call_target="tpu_custom_call" | custom-call | flops 536870912 | bytes 2097152 | tf_op jit(solution)/shard_map/halo/pallas_call | solution.py:328
  48.0 9.3 %attend_early.1 = (bf16[1024,1024]{1,0:T(8,128)(2,1)}, f32[8,8,256]{2,1,0:T(8,128)}) custom-call(s32[9]{0:T(128)} %concatenate.26.info, bf16[1024,3072]{1,0:T(8,128)(2,1)} %get-tuple-element.127.refs_0_, bf16[512,2048]{1,0:T(8,128)(2,1)} %get-tuple-element.131.refs_1_, ...), custom_call_target="tpu_custom_call", output_to_operand_aliasing={{0}: (3, {}), {1}: (4, {})} | custom-call | flops 1073741824 | bytes 3145728 | tf_op jit(solution)/shard_map/attend_early/pallas_call | solution.py:328
  57.3 8.7 %project.1 = (f32[1024,1024]{1,0:T(8,128)}, bf16[1024,1024]{1,0:T(8,128)(2,1)}) custom-call(s32[9]{0:T(128)} %concatenate.26.info, bf16[1024,1024]{1,0:T(8,128)(2,1)} %get-tuple-element.132.refs_0_.refs_5_, bf16[1024,1024]{1,0:T(8,128)(2,1)} %bitcast.139, bf16[1024,1024]{1,0:T(8,128)(2,1)} %refs_6_.5, ...), custom_call_target="tpu_custom_call" | custom-call | flops 536870912 | bytes 3145728 | tf_op jit(solution)/shard_map/project/pallas_call | solution.py:328
  66.0 4.5 %collective-permute-done.1.refs_1_ = bf16[1024,1024]{1,0:T(8,128)(2,1)} collective-permute-done((bf16[1024,1024]{1,0:T(8,128)(2,1)}, bf16[1024,1024]{1,0:T(8,128)(2,1)}, u32[]{:S(2)}, u32[]{:S(2)}) %collective-permute-start.1) | collective-permute-done | bytes 2097184 | tf_op jit(solution)/shard_map/ppermute | solution.py:975
  70.5 48.1 %feed_forward.2 = (bf16[2048,1024]{1,0:T(8,128)(2,1)}, bf16[1280,1024]{1,0:T(8,128)(2,1)}, bf16[1024,1024]{1,0:T(8,128)(2,1)}, bf16[2,3072,128]{2,1,0:T(8,128)(2...) custom-call(s32[9]{0:T(128)} %concatenate.26.info, ...), custom_call_target="tpu_custom_call" | custom-call | flops 9663676416 | bytes 7864320 | tf_op jit(solution)/shard_map/feed_forward/pallas_call | solution.py:328
  118.6 1.4 collective-permute-start.3
  120.3 49.9 %feed_forward.3 = (bf16[2048,1024]{1,0:T(8,128)(2,1)}, bf16[1280,1024]{1,0:T(8,128)(2,1)}, bf16[1024,1024]{1,0:T(8,128)(2,1)}, bf16[2,3072,128]{2,1,0:T(8,128)(2...) custom-call(s32[9]{0:T(128)} %concatenate.26.info, ...), custom_call_target="tpu_custom_call" | custom-call | flops 9663676416 | bytes 7864320 | tf_op jit(solution)/shard_map/feed_forward/pallas_call | solution.py:328
  170.2 1.1 copy-done.27
  171.3 4.3 %fusion.4 = (bf16[3072,128]{1,0:T(8,128)(2,1)S(1)}, bf16[3072,128]{1,0:T(8,128)(2,1)}, bf16[3072,128]{1,0:T(8,128)(2,1)}, bf16[3072,128]{1,0:T(8,128)(2,1)S(1)}) fusion(bf16[2,3072,128]{2,1,0:T(8,128)(2,1)} %copy-done.27, bf16[2,3072,128]{2,1,0:T(8,128)(2,1)S(1)} %copy-done.26, bf16[2,3072,128]{2,1,0:T(8,128)(2,1)} %collective-permute-done.4, ...), kind=kLoop, calls=%fused_computation.35 | loop fusion | flops 6291456 | bytes 9437184 | tf_op jit(solution)/shard_map/convert_element_type | solution.py:979
  175.7 2.0 collective-permute-start.8
  178.2 1.5 collective-permute-start.6
  179.8 15.5 %project_back.1 = (f32[1024,1024]{1,0:T(8,128)}, bf16[1024,1024]{1,0:T(8,128)(2,1)}, bf16[1024,1024]{1,0:T(8,128)(2,1)}, f32[8,1024]{1,0:T(8,128)}) custom-call(s32[9]{0:T(128)} %concatenate.26.info, bf16[1280,1024]{1,0:T(8,128)(2,1)} %get-tuple-element.147.refs_0_, bf16[1024,1024]{1,0:T(8,128)(2,1)} %copy-done.25, ...), custom_call_target="tpu_custom_call" | custom-call | flops 1073741824 | bytes 6291456 | tf_op jit(solution)/shard_map/project_back/pallas_call | solution.py:328
  195.2 16.2 %attend_back.2 = (bf16[1024,3072]{1,0:T(8,128)(2,1)}, bf16[512,2048]{1,0:T(8,128)(2,1)}) custom-call(s32[9]{0:T(128)} %concatenate.26.info, bf16[1024,3072]{1,0:T(8,128)(2,1)} %get-tuple-element.127.refs_0_, bf16[512,2048]{1,0:T(8,128)(2,1)} %get-tuple-element.131.refs_1_, bf16[1024,1024]{1,0:T(8,128)(2,1)} %get-tuple-element.163.refs_2_, ...), custom_call_target="tpu_custom_call" | custom-call | flops 4026531840 | bytes 4718592 | tf_op jit(solution)/shard_map/attend_back/pallas_call | solution.py:328
  211.5 16.5 %branch.1 = (bf16[1536,1024]{1,0:T(8,128)(2,1)}, bf16[1024,1024]{1,0:T(8,128)(2,1)}, f32[8,1024]{1,0:T(8,128)}) custom-call(s32[9]{0:T(128)} %concatenate.26.info, bf16[2048,1024]{1,0:T(8,128)(2,1)} %get-tuple-element.171.refs_0_, bf16[2048,1024]{1,0:T(8,128)(2,1)} %get-tuple-element.172.refs_1_, bf16[1024,1024]{1,0:T(8,128)(2,1)} %copy-done, ...), custom_call_target="tpu_custom_call" | custom-call | flops 2147483648 | bytes 4194304 | tf_op jit(solution)/shard_map/branch/pallas_call | solution.py:328
  227.9 3.4 collective-permute-done.6
  231.3 1.3 add_convert_fusion.8
  232.7 1.3 add_convert_fusion.7
  235.1 1.6 collective-permute-start.12
  236.7 2.7 fusion.8
  239.8 1.3 fusion.10
  241.6 1.1 pad_maximum_fusion.2.refs_8_
  242.7 5.3 %first_halo.2 = (bf16[384,1024]{1,0:T(8,128)(2,1)}, f32[8,1024]{1,0:T(8,128)}) custom-call(s32[9]{0:T(128)} %concatenate.26.info, bf16[512,2048]{1,0:T(8,128)(2,1)} %get-tuple-element.174.refs_5_.refs_0_.refs_8_, bf16[1024,3072]{1,0:T(8,128)(2,1)} %refs_1_.9, bf16[1024,3072]{1,0:T(8,128)(2,1)} %refs_1_.9, bf16[512,1024]{1,0:T(8,128)(2,1)} %copy-done.2, ...), custom_call_target="tpu_custom_call" | custom-call | flops 402653184 | bytes 1572864 | tf_op jit(solution)/shard_map/first_halo/pallas_call | solution.py:328
  248.0 8.2 %attend_back.3 = (bf16[1024,3072]{1,0:T(8,128)(2,1)}, bf16[512,2048]{1,0:T(8,128)(2,1)}) custom-call(s32[9]{0:T(128)} %concatenate.26.info, bf16[1024,3072]{1,0:T(8,128)(2,1)} %get-tuple-element.127.refs_0_, bf16[512,2048]{1,0:T(8,128)(2,1)} %get-tuple-element.131.refs_1_, ...), custom_call_target="tpu_custom_call", output_to_operand_aliasing={{0}: (8, {}), {1}: (9, {})} | custom-call | flops 1342177280 | bytes 1572864 | tf_op jit(solution)/shard_map/attend_back/pallas_call | solution.py:328
  256.2 3.2 collective-permute-done.10
  259.4 1.4 collective-permute-done.11
  261.7 1.3 collective-permute-start.14
  263.0 1.4 add_convert_fusion.6
  265.1 2.6 collective-permute-start.15
  267.7 14.1 %qkv_grad.1 = (bf16[2,2,4,64,512]{4,3,2,1,0:T(8,128)(2,1)}, bf16[2,2,2,4,64,512]{5,4,3,2,1,0:T(8,128)(2,1)}, bf16[2,2,4,64,512]{4,3,2,1,0:T(8,128)(2,1)}, bf16[2,2,2,4,64,512]{5,4,3,2,1,0:T(8,128)(2,1)}) custom-call(s32[9]{0:T(128)} %concatenate.26.info, bf16[1024,1024]{1,0:T(8,128)(2,1)} %get-tuple-element.191.refs_0_, ...), custom_call_target="tpu_custom_call" | custom-call | flops 2147483648 | bytes 4194304 | tf_op jit(solution)/shard_map/qkv_grad/pallas_call | solution.py:328
  281.8 2.7 collective-permute-done.15
  285.8 3.8 first_halo.3
  289.6 1.4 collective-permute-done.16
  291.2 2.6 fusion.12
  293.9 2.1 fusion.1
  295.9 1.5 collective-permute-start.19
  297.5 1.3 add_convert_fusion.5
  299.3 2.9 collective-permute-start.18
  303.9 1.5 collective-permute-start.21
  306.4 16.1 %first_back.1 = (f32[1024,1024]{1,0:T(8,128)}, f32[8,1024]{1,0:T(8,128)}) custom-call(s32[9]{0:T(128)} %concatenate.26.info, bf16[1024,3072]{1,0:T(8,128)(2,1)} %get-tuple-element.192.refs_1_.refs_0_, bf16[1024,3072]{1,0:T(8,128)(2,1)} %refs_1_.9, bf16[1024,1024]{1,0:T(8,128)(2,1)} %bitcast.141, f32[1024,1024]{1,0:T(8,128)} %get-tuple-element.215.refs_3_, ...), custom_call_target="tpu_custom_call" | custom-call | flops 1610612736 | bytes 6291456 | tf_op jit(solution)/shard_map/first_back/pallas_call | solution.py:328
  323.5 1.2 add_convert_fusion.17.refs_5_
  324.7 1.7 add_convert_fusion.refs_6_
  328.8 2.2 collective-permute-start.23
  332.1 1.4 collective-permute-start.26
  333.5 7.3 %output.1.refs_7_ = bf16[1024,1024]{1,0:T(8,128)(2,1)} custom-call(s32[9]{0:T(128)} %concatenate.26.info, bf16[1024,1024]{1,0:T(8,128)(2,1)} %bitcast.142, f32[1024,1024]{1,0:T(8,128)} %get-tuple-element.158.refs_2_.refs_1_, bf16[1536,1024]{1,0:T(8,128)(2,1)} %get-tuple-element.225.refs_2_, bf16[1024,1024]{1,0:T(8,128)(2,1)} %collective-permute-done.13.refs_3_, ...), custom_call_target="tpu_custom_call" | custom-call | bytes 3670016 | tf_op jit(solution)/shard_map/output/pallas_call | solution.py:328
  341.1 2.7 collective-permute-done.23
  343.9 1.3 fusion.2.refs_6_
  345.3 2.1 collective-permute-start.25
  347.6 1.8 collective-permute-start.27
  350.3 6.7 %input_grad.1 = bf16[1024,1024]{1,0:T(8,128)(2,1)} custom-call(s32[9]{0:T(128)} %concatenate.26.info, f32[1024,1024]{1,0:T(8,128)} %get-tuple-element.234.refs_0_, bf16[384,1024]{1,0:T(8,128)(2,1)} %copy-done.32, bf16[128,1024]{1,0:T(8,128)(2,1)} %copy-done.30, bf16[1024,1024]{1,0:T(8,128)(2,1)} %bitcast.143, ...), custom_call_target="tpu_custom_call" | custom-call | bytes 2097152 | tf_op jit(solution)/shard_map/input_grad/pallas_call | solution.py:328
  358.1 6.7 %collective-permute-done.25 = bf16[3,2,64,512]{3,2,1,0:T(8,128)(2,1)S(1)} collective-permute-done((bf16[3,2,64,512]{3,2,1,0:T(8,128)(2,1)S(1)}, bf16[3,2,64,512]{3,2,1,0:T(8,128)(2,1)S(1)}, u32[]{:S(2)}, u32[]{:S(2)}) %collective-permute-start.25) | collective-permute-done | bytes 393248 | tf_op jit(solution)/shard_map/ppermute | solution.py:1257
  365.5 1.8 collective-permute-start.31
  369.5 2.6 collective-permute-start.32
  372.2 3.1 collective-permute-done.32
  375.3 3.6 collective-permute-start.33
  379.9 2.7 collective-permute-done.33
  384.2 1.3 collective-permute-start.29
  387.4 1.2 collective-permute-done.29
  389.8 1.2 reshape_squeeze.8
  391.4 1.2 reshape_squeeze.7
  (195 shorter events, 27.9 us)
Async XLA Ops:
  7.2 7.4 %copy-start.44 = (s32[4]{0:T(128)S(1)}, s32[4]{0:T(128)}, u32[]{:S(2)}) copy-start(s32[4]{0:T(128)} %param.14) | copy-start | bytes 52
  7.2 7.5 %copy-start.40 = (f32[1024,4]{0,1:T(4,128)S(1)}, f32[1024,4]{0,1:T(4,128)}, u32[]{:S(2)}) copy-start(f32[1024,4]{0,1:T(4,128)} %param.20) | copy-start | bytes 49156
  7.2 8.2 %copy-start.43 = (f32[1024,2]{0,1:T(2,128)S(1)}, f32[1024,2]{0,1:T(2,128)}, u32[]{:S(2)}) copy-start(f32[1024,2]{0,1:T(2,128)} %param.21) | copy-start | bytes 24580
  7.2 375.7 %reduce-scatter.2.cloned.1.call-start = ((), (), s32[]{:S(2)}) async-start(), calls=%async_computation.1 | async-start | bytes 2228224 | tf_op jit(solution)/shard_map/reduce_scatter | solution.py:1138
  9.6 31.4 %collective-permute-start = (bf16[512,1024]{1,0:T(8,128)(2,1)}, bf16[512,1024]{1,0:T(8,128)(2,1)S(1)}, u32[]{:S(2)}, u32[]{:S(2)}) collective-permute-start(bf16[512,1024]{1,0:T(8,128)(2,1)} %bitcast.7), channel_id=1, source_target_pairs={{0,1},{2,3},{4,5},{6,7},{8,9},{10,11},{12,13},{14,15},{16,17},{18,... | collective-permute-start | bytes 3145736 | tf_op jit(solution)/shard_map/ppermute | solution.py:1019
  41.1 6.9 %copy-start = (bf16[1024,1024]{1,0:T(8,128)(2,1)}, bf16[1024,1024]{1,0:T(8,128)(2,1)S(1)}, u32[]{:S(2)}) copy-start(bf16[1024,1024]{1,0:T(8,128)(2,1)S(1)} %multiply_convert_fusion.refs_2_) | copy-start | bytes 6291460
  41.1 24.9 %collective-permute-start.2 = (bf16[1024,1024]{1,0:T(8,128)(2,1)S(1)}, bf16[1024,1024]{1,0:T(8,128)(2,1)}, u32[]{:S(2)}, u32[]{:S(2)}) collective-permute-start(bf16[1024,1024]{1,0:T(8,128)(2,1)S(1)} %multiply_convert_fusion.refs_2_), channel_id=1, source_target_pairs={{0,2},{2,0},{1,3},{3,1},{4,6},{6,4},{5,7},{7,5},{8,10},{10,8},{9,1... | collective-permute-start | bytes 6291464 | tf_op jit(solution)/shard_map/ppermute | solution.py:975
  66.0 4.5 %collective-permute-start.1 = (bf16[1024,1024]{1,0:T(8,128)(2,1)}, bf16[1024,1024]{1,0:T(8,128)(2,1)}, u32[]{:S(2)}, u32[]{:S(2)}) collective-permute-start(bf16[1024,1024]{1,0:T(8,128)(2,1)} %get-tuple-element.133.refs_0_), channel_id=1, source_target_pairs={{0,2},{2,0},{1,3},{3,1},{4,6},{6,4},{5,7},{7,5},{8,10},{10,8},{9,1... | collective-permute-start | bytes 6291464 | tf_op jit(solution)/shard_map/ppermute | solution.py:975
  118.6 51.6 %collective-permute-start.3 = (bf16[2,3072,128]{2,1,0:T(8,128)(2,1)}, bf16[2,3072,128]{2,1,0:T(8,128)(2,1)S(1)}, u32[]{:S(2)}, u32[]{:S(2)}) collective-permute-start(bf16[2,3072,128]{2,1,0:T(8,128)(2,1)} %get-tuple-element.144), channel_id=1, source_target_pairs={{0,1},{1,0},{2,3},{3,2},{4,5},{5,4},{6,7},{7,6},{8,9},{9,8},{10,11... | collective-permute-start | bytes 4718600 | tf_op jit(solution)/shard_map/ppermute | solution.py:975
  120.0 50.2 %collective-permute-start.4 = (bf16[2,3072,128]{2,1,0:T(8,128)(2,1)}, bf16[2,3072,128]{2,1,0:T(8,128)(2,1)}, u32[]{:S(2)}, u32[]{:S(2)}) collective-permute-start(bf16[2,3072,128]{2,1,0:T(8,128)(2,1)} %get-tuple-element.146), channel_id=1, source_target_pairs={{0,4},{4,0},{1,5},{5,1},{2,6},{6,2},{3,7},{7,3},{8,12},{12,8},{9,1... | collective-permute-start | bytes 4718600 | tf_op jit(solution)/shard_map/ppermute | solution.py:975
  120.3 51.1 %copy-start.26 = (bf16[2,3072,128]{2,1,0:T(8,128)(2,1)S(1)}, bf16[2,3072,128]{2,1,0:T(8,128)(2,1)}, u32[]{:S(2)}) copy-start(bf16[2,3072,128]{2,1,0:T(8,128)(2,1)} %get-tuple-element.153) | copy-start | bytes 4718596
  171.3 4.4 %collective-permute-start.5 = (bf16[1024,1024]{1,0:T(8,128)(2,1)}, bf16[1024,1024]{1,0:T(8,128)(2,1)S(1)}, u32[]{:S(2)}, u32[]{:S(2)}) collective-permute-start(bf16[1024,1024]{1,0:T(8,128)(2,1)} %get-tuple-element.152), channel_id=1, source_target_pairs={{0,2},{2,0},{1,3},{3,1},{4,6},{6,4},{5,7},{7,5},{8,10},{10,8},{9,1... | collective-permute-start | bytes 6291464 | tf_op jit(solution)/shard_map/ppermute | solution.py:975
  175.6 4.2 %copy-start.20 = (bf16[3072,128]{1,0:T(8,128)(2,1)}, bf16[3072,128]{1,0:T(8,128)(2,1)S(1)}, u32[]{:S(2)}) copy-start(bf16[3072,128]{1,0:T(8,128)(2,1)S(1)} %get-tuple-element.162.refs_11_) | copy-start | bytes 2359300
  175.6 4.2 %copy-start.21 = (bf16[3072,128]{1,0:T(8,128)(2,1)}, bf16[3072,128]{1,0:T(8,128)(2,1)S(1)}, u32[]{:S(2)}) copy-start(bf16[3072,128]{1,0:T(8,128)(2,1)S(1)} %get-tuple-element.160.refs_9_) | copy-start | bytes 2359300
  175.7 55.6 %collective-permute-start.8 = (bf16[2,3072,128]{2,1,0:T(8,128)(2,1)}, bf16[2,3072,128]{2,1,0:T(8,128)(2,1)}, u32[]{:S(2)}, u32[]{:S(2)}) collective-permute-start(bf16[2,3072,128]{2,1,0:T(8,128)(2,1)} %get-tuple-element.168), channel_id=1, source_target_pairs={{0,1},{1,0},{2,3},{3,2},{4,5},{5,4},{6,7},{7,6},{8,9},{9,8},{10,11... | collective-permute-start | bytes 4718600 | tf_op jit(solution)/shard_map/ppermute | solution.py:975
  177.6 53.7 %collective-permute-start.9 = (bf16[2,3072,128]{2,1,0:T(8,128)(2,1)}, bf16[2,3072,128]{2,1,0:T(8,128)(2,1)S(1)}, u32[]{:S(2)}, u32[]{:S(2)}) collective-permute-start(bf16[2,3072,128]{2,1,0:T(8,128)(2,1)} %get-tuple-element.170), channel_id=1, source_target_pairs={{0,4},{4,0},{1,5},{5,1},{2,6},{6,2},{3,7},{7,3},{8,12},{12,8},{9,1... | collective-permute-start | bytes 4718600 | tf_op jit(solution)/shard_map/ppermute | solution.py:975
  178.2 53.2 %collective-permute-start.6 = (bf16[3072,128]{1,0:T(8,128)(2,1)S(1)}, bf16[3072,128]{1,0:T(8,128)(2,1)}, u32[]{:S(2)}, u32[]{:S(2)}) collective-permute-start(bf16[3072,128]{1,0:T(8,128)(2,1)S(1)} %get-tuple-element.160.refs_9_), channel_id=1, source_target_pairs={{0,4},{4,0},{1,5},{5,1},{2,6},{6,2},{3,7},{7,3},{8,12},{12,8},{9,1... | collective-permute-start | bytes 2359304 | tf_op jit(solution)/shard_map/ppermute | solution.py:975
  179.7 51.6 %collective-permute-start.7 = (bf16[3072,128]{1,0:T(8,128)(2,1)S(1)}, bf16[3072,128]{1,0:T(8,128)(2,1)}, u32[]{:S(2)}, u32[]{:S(2)}) collective-permute-start(bf16[3072,128]{1,0:T(8,128)(2,1)S(1)} %get-tuple-element.162.refs_11_), channel_id=1, source_target_pairs={{0,1},{1,0},{2,3},{3,2},{4,5},{5,4},{6,7},{7,6},{8,9},{9,8},{10,11... | collective-permute-start | bytes 2359304 | tf_op jit(solution)/shard_map/ppermute | solution.py:975
  211.5 19.9 %copy-start.9 = (bf16[3072,128]{1,0:T(8,128)(2,1)S(1)}, bf16[3072,128]{1,0:T(8,128)(2,1)}, u32[]{:S(2)}) copy-start(bf16[3072,128]{1,0:T(8,128)(2,1)} %get-tuple-element.179.refs_8_) | copy-start | bytes 2359300
  227.9 4.8 %copy-start.8 = (bf16[3072,128]{1,0:T(8,128)(2,1)S(1)}, bf16[3072,128]{1,0:T(8,128)(2,1)}, u32[]{:S(2)}) copy-start(bf16[3072,128]{1,0:T(8,128)(2,1)} %get-tuple-element.181.refs_10_) | copy-start | bytes 2359300
  235.1 4.7 %copy-start.28 = (bf16[2,3072,128]{2,1,0:T(8,128)(2,1)S(1)}, bf16[2,3072,128]{2,1,0:T(8,128)(2,1)}, u32[]{:S(2)}) copy-start(bf16[2,3072,128]{2,1,0:T(8,128)(2,1)} %get-tuple-element.177) | copy-start | bytes 4718596
  235.1 21.1 %collective-permute-start.12 = (bf16[24,128,128]{2,1,0:T(8,128)(2,1)}, bf16[24,128,128]{2,1,0:T(8,128)(2,1)}, u32[]{:S(2)}, u32[]{:S(2)}) collective-permute-start(bf16[24,128,128]{2,1,0:T(8,128)(2,1)} %pad_maximum_fusion.3), channel_id=1, source_target_pairs={{0,8},{8,0},{16,24},{24,16},{1,9},{9,1},{17,25},{25,17},{2,10},{10... | collective-permute-start | bytes 2359304 | tf_op jit(solution)/shard_map/ppermute | solution.py:1104
  236.7 24.1 %collective-permute-start.13 = (bf16[1024,1024]{1,0:T(8,128)(2,1)}, bf16[1024,1024]{1,0:T(8,128)(2,1)}, u32[]{:S(2)}, u32[]{:S(2)}) collective-permute-start(bf16[1024,1024]{1,0:T(8,128)(2,1)} %get-tuple-element.187), channel_id=1, source_target_pairs={{0,2},{2,0},{1,3},{3,1},{4,6},{6,4},{5,7},{7,5},{8,10},{10,8},{9,1... | collective-permute-start | bytes 6291464 | tf_op jit(solution)/shard_map/ppermute | solution.py:975
  239.3 20.1 %collective-permute-start.10 = (bf16[3072,128]{1,0:T(8,128)(2,1)S(1)}, bf16[3072,128]{1,0:T(8,128)(2,1)}, u32[]{:S(2)}, u32[]{:S(2)}) collective-permute-start(bf16[3072,128]{1,0:T(8,128)(2,1)S(1)} %get-tuple-element.251.refs_5_), channel_id=1, source_target_pairs={{0,4},{4,0},{1,5},{5,1},{2,6},{6,2},{3,7},{7,3},{8,12},{12,8},{9,1... | collective-permute-start | bytes 2359304 | tf_op jit(solution)/shard_map/ppermute | solution.py:975
  241.1 19.7 %collective-permute-start.11 = (bf16[3072,128]{1,0:T(8,128)(2,1)S(1)}, bf16[3072,128]{1,0:T(8,128)(2,1)S(1)}, u32[]{:S(2)}, u32[]{:S(2)}) collective-permute-start(bf16[3072,128]{1,0:T(8,128)(2,1)S(1)} %get-tuple-element.249.refs_7_), channel_id=1, source_target_pairs={{0,1},{1,0},{2,3},{3,2},{4,5},{5,4},{6,7},{7,6},{8,9},{9,8},{10,11... | collective-permute-start | bytes 2359304 | tf_op jit(solution)/shard_map/ppermute | solution.py:975
  248.0 13.7 %copy-start.31 = (bf16[384,1024]{1,0:T(8,128)(2,1)S(1)}, bf16[384,1024]{1,0:T(8,128)(2,1)}, u32[]{:S(2)}) copy-start(bf16[384,1024]{1,0:T(8,128)(2,1)} %get-tuple-element.188.refs_6_) | copy-start | bytes 2359300
  248.0 15.0 %copy-start.11 = (bf16[24,128,128]{2,1,0:T(8,128)(2,1)S(1)}, bf16[24,128,128]{2,1,0:T(8,128)(2,1)}, u32[]{:S(2)}) copy-start(bf16[24,128,128]{2,1,0:T(8,128)(2,1)} %pad_maximum_fusion.2.refs_8_) | copy-start | bytes 2359300
  261.7 22.9 %collective-permute-start.14 = (bf16[384,1024]{1,0:T(8,128)(2,1)S(1)}, bf16[384,1024]{1,0:T(8,128)(2,1)S(1)}, u32[]{:S(2)}, u32[]{:S(2)}) collective-permute-start(bf16[384,1024]{1,0:T(8,128)(2,1)S(1)} %copy-done.31), channel_id=1, source_target_pairs={{1,0},{3,2},{5,4},{7,6},{9,8},{11,10},{13,12},{15,14},{17,16},{19,... | collective-permute-start | bytes 2359304 | tf_op jit(solution)/shard_map/ppermute | solution.py:1187
  265.1 19.4 %collective-permute-start.15 = (bf16[3,4,128,128]{3,2,1,0:T(8,128)(2,1)S(1)}, bf16[3,4,128,128]{3,2,1,0:T(8,128)(2,1)S(1)}, u32[]{:S(2)}, u32[]{:S(2)}) collective-permute-start(bf16[3,4,128,128]{3,2,1,0:T(8,128)(2,1)S(1)} %get-tuple-element.263), channel_id=1, source_target_pairs={{0,16},{16,0},{8,24},{24,8},{1,17},{17,1},{9,25},{25,9},{2,18},{18... | collective-permute-start | bytes 1179656 | tf_op jit(solution)/shard_map/ppermute | solution.py:1108
  284.6 5.0 %copy-start.32 = (bf16[384,1024]{1,0:T(8,128)(2,1)}, bf16[384,1024]{1,0:T(8,128)(2,1)S(1)}, u32[]{:S(2)}) copy-start(bf16[384,1024]{1,0:T(8,128)(2,1)S(1)} %collective-permute-done.14.refs_1_) | copy-start | bytes 2359300
  285.3 5.9 %copy-start.17 = (bf16[2,2,4,64,512]{4,3,2,1,0:T(8,128)(2,1)S(1)}, bf16[2,2,4,64,512]{4,3,2,1,0:T(8,128)(2,1)}, u32[]{:S(2)}) copy-start(bf16[2,2,4,64,512]{4,3,2,1,0:T(8,128)(2,1)} %get-tuple-element.199.refs_4_) | copy-start | bytes 3145732
  285.3 5.9 %collective-permute-start.17 = (bf16[2,2,2,4,64,512]{5,4,3,2,1,0:T(8,128)(2,1)}, bf16[2,2,2,4,64,512]{5,4,3,2,1,0:T(8,128)(2,1)S(1)}, u32[]{:S(2)}, u32[]{:S(2)}) collective-permute-start(bf16[2,2,2,4,64,512]{5,4,3,2,1,0:T(8,128)(2,1)} %get-tuple-element.201), channel_id=1, source_target_pairs={{0,2},{2,0},{1,3},{3,1},{4,6},{6,4},{5,7},{7,5},{8,10},{10,8},{9,1... | collective-permute-start | bytes 6291464 | tf_op jit(solution)/shard_map/ppermute | solution.py:975
  285.3 5.6 %collective-permute-start.16 = (bf16[2,2,4,64,512]{4,3,2,1,0:T(8,128)(2,1)}, bf16[2,2,4,64,512]{4,3,2,1,0:T(8,128)(2,1)}, u32[]{:S(2)}, u32[]{:S(2)}) collective-permute-start(bf16[2,2,4,64,512]{4,3,2,1,0:T(8,128)(2,1)} %get-tuple-element.200), channel_id=1, source_target_pairs={{0,2},{2,0},{1,3},{3,1},{4,6},{6,4},{5,7},{7,5},{8,10},{10,8},{9,1... | collective-permute-start | bytes 3145736 | tf_op jit(solution)/shard_map/ppermute | solution.py:975
  293.9 3.6 copy-start.6
  295.9 26.6 %collective-permute-start.19 = (bf16[2,2,4,64,512]{4,3,2,1,0:T(8,128)(2,1)}, bf16[2,2,4,64,512]{4,3,2,1,0:T(8,128)(2,1)}, u32[]{:S(2)}, u32[]{:S(2)}) collective-permute-start(bf16[2,2,4,64,512]{4,3,2,1,0:T(8,128)(2,1)} %get-tuple-element.248), channel_id=1, source_target_pairs={{0,4},{4,0},{1,5},{5,1},{2,6},{6,2},{3,7},{7,3},{8,12},{12,8},{9,1... | collective-permute-start | bytes 3145736 | tf_op jit(solution)/shard_map/ppermute | solution.py:975
  299.2 23.3 %collective-permute-start.20 = (bf16[24,128,128]{2,1,0:T(8,128)(2,1)S(1)}, bf16[24,128,128]{2,1,0:T(8,128)(2,1)S(1)}, u32[]{:S(2)}, u32[]{:S(2)}) collective-permute-start(bf16[24,128,128]{2,1,0:T(8,128)(2,1)S(1)} %pad_maximum_fusion.5), channel_id=1, source_target_pairs={{0,8},{8,0},{16,24},{24,16},{1,9},{9,1},{17,25},{25,17},{2,10},{10... | collective-permute-start | bytes 2359304 | tf_op jit(solution)/shard_map/ppermute | solution.py:1104
  299.3 23.2 %collective-permute-start.18 = (bf16[2,4,64,512]{3,2,1,0:T(8,128)(2,1)}, bf16[2,4,64,512]{3,2,1,0:T(8,128)(2,1)}, u32[]{:S(2)}, u32[]{:S(2)}) collective-permute-start(bf16[2,4,64,512]{3,2,1,0:T(8,128)(2,1)} %get-tuple-element.258), channel_id=1, source_target_pairs={{0,1},{1,0},{2,3},{3,2},{4,5},{5,4},{6,7},{7,6},{8,9},{9,8},{10,11... | collective-permute-start | bytes 1572872 | tf_op jit(solution)/shard_map/ppermute | solution.py:975
  303.9 18.6 %collective-permute-start.21 = (bf16[128,1024]{1,0:T(8,128)(2,1)}, bf16[128,1024]{1,0:T(8,128)(2,1)S(1)}, u32[]{:S(2)}, u32[]{:S(2)}) collective-permute-start(bf16[128,1024]{1,0:T(8,128)(2,1)} %get-tuple-element.210), channel_id=1, source_target_pairs={{1,0},{3,2},{5,4},{7,6},{9,8},{11,10},{13,12},{15,14},{17,16},{19,... | collective-permute-start | bytes 786440 | tf_op jit(solution)/shard_map/ppermute | solution.py:1219
  306.4 16.1 %copy-start.41 = (f32[8,1024]{1,0:T(8,128)S(1)}, f32[8,1024]{1,0:T(8,128)}, u32[]{:S(2)}) copy-start(f32[8,1024]{1,0:T(8,128)} %get-tuple-element.221) | copy-start | bytes 98308
  306.4 16.1 %copy-start.42 = (f32[8,1024]{1,0:T(8,128)S(1)}, f32[8,1024]{1,0:T(8,128)}, u32[]{:S(2)}) copy-start(f32[8,1024]{1,0:T(8,128)} %get-tuple-element.222) | copy-start | bytes 98308
  306.4 17.0 %copy-start.16 = (bf16[2,4,64,512]{3,2,1,0:T(8,128)(2,1)S(1)}, bf16[2,4,64,512]{3,2,1,0:T(8,128)(2,1)}, u32[]{:S(2)}) copy-start(bf16[2,4,64,512]{3,2,1,0:T(8,128)(2,1)} %get-tuple-element.257.refs_5_) | copy-start | bytes 1572868
  322.5 3.9 copy-start.30
  326.5 4.8 %copy-start.3 = (bf16[2,2,4,64,512]{4,3,2,1,0:T(8,128)(2,1)}, bf16[2,2,4,64,512]{4,3,2,1,0:T(8,128)(2,1)S(1)}, u32[]{:S(2)}) copy-start(bf16[2,2,4,64,512]{4,3,2,1,0:T(8,128)(2,1)S(1)} %add_convert_fusion.refs_6_) | copy-start | bytes 3145732
  326.5 4.5 %copy-start.10 = (bf16[24,128,128]{2,1,0:T(8,128)(2,1)S(1)}, bf16[24,128,128]{2,1,0:T(8,128)(2,1)}, u32[]{:S(2)}) copy-start(bf16[24,128,128]{2,1,0:T(8,128)(2,1)} %pad_maximum_fusion.4.refs_7_) | copy-start | bytes 2359300
  326.6 4.7 %copy-start.38 = (f32[8,1024]{1,0:T(8,128)}, f32[8,1024]{1,0:T(8,128)S(1)}, u32[]{:S(2)}) copy-start(f32[8,1024]{1,0:T(8,128)S(1)} %stack.45.refs_9_) | copy-start | bytes 98308
  326.6 14.2 %collective-permute-start.24 = (f32[8,1024]{1,0:T(8,128)S(1)}, f32[8,1024]{1,0:T(8,128)S(1)}, u32[]{:S(2)}, u32[]{:S(2)}) collective-permute-start(f32[8,1024]{1,0:T(8,128)S(1)} %stack.45.refs_9_), channel_id=1, source_target_pairs={{0,2},{2,0},{1,3},{3,1},{4,6},{6,4},{5,7},{7,5},{8,10},{10,8},{9,1... | collective-permute-start | bytes 98312 | tf_op jit(solution)/shard_map/ppermute | solution.py:975
  327.4 13.8 %collective-permute-start.22 = (bf16[4,64,512]{2,1,0:T(8,128)(2,1)}, bf16[4,64,512]{2,1,0:T(8,128)(2,1)S(1)}, u32[]{:S(2)}, u32[]{:S(2)}) collective-permute-start(bf16[4,64,512]{2,1,0:T(8,128)(2,1)} %slice_bitcast_fusion.7), channel_id=1, source_target_pairs={{0,4},{4,0},{1,5},{5,1},{2,6},{6,2},{3,7},{7,3},{8,12},{12,8},{9,1... | collective-permute-start | bytes 786440 | tf_op jit(solution)/shard_map/ppermute | solution.py:975
  328.8 15.0 %collective-permute-start.23 = (bf16[2,4,64,512]{3,2,1,0:T(8,128)(2,1)}, bf16[2,4,64,512]{3,2,1,0:T(8,128)(2,1)}, u32[]{:S(2)}, u32[]{:S(2)}) collective-permute-start(bf16[2,4,64,512]{3,2,1,0:T(8,128)(2,1)} %slice_bitcast_fusion.1), channel_id=1, source_target_pairs={{0,1},{1,0},{2,3},{3,2},{4,5},{5,4},{6,7},{7,6},{8,9},{9,8},{10,11... | collective-permute-start | bytes 1572872 | tf_op jit(solution)/shard_map/ppermute | solution.py:975
  332.1 26.0 %collective-permute-start.26 = (bf16[3,4,128,128]{3,2,1,0:T(8,128)(2,1)S(1)}, bf16[3,4,128,128]{3,2,1,0:T(8,128)(2,1)S(1)}, u32[]{:S(2)}, u32[]{:S(2)}) collective-permute-start(bf16[3,4,128,128]{3,2,1,0:T(8,128)(2,1)S(1)} %get-tuple-element.261), channel_id=1, source_target_pairs={{0,16},{16,0},{8,24},{24,8},{1,17},{17,1},{9,25},{25,9},{2,18},{18... | collective-permute-start | bytes 1179656 | tf_op jit(solution)/shard_map/ppermute | solution.py:1108
  333.5 10.3 %copy-start.15 = (bf16[2,4,64,512]{3,2,1,0:T(8,128)(2,1)S(1)}, bf16[2,4,64,512]{3,2,1,0:T(8,128)(2,1)}, u32[]{:S(2)}) copy-start(bf16[2,4,64,512]{3,2,1,0:T(8,128)(2,1)} %copy-done.14) | copy-start | bytes 1572868
  333.5 10.4 %copy-start.4 = (bf16[2,2,4,64,512]{4,3,2,1,0:T(8,128)(2,1)S(1)}, bf16[2,2,4,64,512]{4,3,2,1,0:T(8,128)(2,1)}, u32[]{:S(2)}) copy-start(bf16[2,2,4,64,512]{4,3,2,1,0:T(8,128)(2,1)} %copy-done.3) | copy-start | bytes 3145732
  343.9 5.5 %copy-start.12 = (bf16[4,64,512]{2,1,0:T(8,128)(2,1)}, bf16[4,64,512]{2,1,0:T(8,128)(2,1)S(1)}, u32[]{:S(2)}) copy-start(bf16[4,64,512]{2,1,0:T(8,128)(2,1)S(1)} %fusion.14.refs_5_) | copy-start | bytes 786436
  343.9 3.5 copy-start.18
  345.2 5.1 %copy-start.1 = (bf16[2,4,64,512]{3,2,1,0:T(8,128)(2,1)}, bf16[2,4,64,512]{3,2,1,0:T(8,128)(2,1)S(1)}, u32[]{:S(2)}) copy-start(bf16[2,4,64,512]{3,2,1,0:T(8,128)(2,1)S(1)} %fusion.2.refs_6_) | copy-start | bytes 1572868
  345.3 19.5 %collective-permute-start.25 = (bf16[3,2,64,512]{3,2,1,0:T(8,128)(2,1)S(1)}, bf16[3,2,64,512]{3,2,1,0:T(8,128)(2,1)S(1)}, u32[]{:S(2)}, u32[]{:S(2)}) collective-permute-start(bf16[3,2,64,512]{3,2,1,0:T(8,128)(2,1)S(1)} %fusion.18), channel_id=1, source_target_pairs={{0,8},{8,0},{16,24},{24,16},{1,9},{9,1},{17,25},{25,17},{2,10},{10... | collective-permute-start | bytes 1179656 | tf_op jit(solution)/shard_map/ppermute | solution.py:1257
  347.6 10.5 %collective-permute-start.27 = (f32[8,1024]{1,0:T(8,128)S(1)}, f32[8,1024]{1,0:T(8,128)S(1)}, u32[]{:S(2)}, u32[]{:S(2)}) collective-permute-start(f32[8,1024]{1,0:T(8,128)S(1)} %add.181.refs_9_), channel_id=1, source_target_pairs={{0,1},{1,0},{2,3},{3,2},{4,5},{5,4},{6,7},{7,6},{8,9},{9,8},{10,11... | collective-permute-start | bytes 98312 | tf_op jit(solution)/shard_map/ppermute | solution.py:975
  350.3 17.0 %copy-start.13 = (bf16[4,64,512]{2,1,0:T(8,128)(2,1)S(1)}, bf16[4,64,512]{2,1,0:T(8,128)(2,1)}, u32[]{:S(2)}) copy-start(bf16[4,64,512]{2,1,0:T(8,128)(2,1)} %copy-done.12) | copy-start | bytes 786436
  357.0 12.1 %copy-start.19 = (bf16[3,4,128,128]{3,2,1,0:T(8,128)(2,1)S(1)}, bf16[3,4,128,128]{3,2,1,0:T(8,128)(2,1)}, u32[]{:S(2)}) copy-start(bf16[3,4,128,128]{3,2,1,0:T(8,128)(2,1)} %get-tuple-element.242.refs_7_) | copy-start | bytes 1179652
  365.5 3.9 collective-permute-start.31
  368.4 14.4 %collective-permute-start.28 = (bf16[3,64,512]{2,1,0:T(8,128)(2,1)S(1)}, bf16[3,64,512]{2,1,0:T(8,128)(2,1)S(1)}, u32[]{:S(2)}, u32[]{:S(2)}) collective-permute-start(bf16[3,64,512]{2,1,0:T(8,128)(2,1)S(1)} %slice_bitcast_fusion.8), channel_id=1, source_target_pairs={{0,16},{16,0},{8,24},{24,8},{1,17},{17,1},{9,25},{25,9},{2,18},{18... | collective-permute-start | bytes 589832 | tf_op jit(solution)/shard_map/ppermute | solution.py:1276
  369.5 5.8 %collective-permute-start.32 = (f32[8,1024]{1,0:T(8,128)S(1)}, f32[8,1024]{1,0:T(8,128)S(1)}, u32[]{:S(2)}, u32[]{:S(2)}) collective-permute-start(f32[8,1024]{1,0:T(8,128)S(1)} %add.192), channel_id=1, source_target_pairs={{0,8},{8,0},{16,24},{24,16},{1,9},{9,1},{17,25},{25,17},{2,10},{10... | collective-permute-start | bytes 98312 | tf_op jit(solution)/shard_map/ppermute | solution.py:1273
  375.3 7.4 %collective-permute-start.33 = (f32[8,1024]{1,0:T(8,128)S(1)}, f32[8,1024]{1,0:T(8,128)S(1)}, u32[]{:S(2)}, u32[]{:S(2)}) collective-permute-start(f32[8,1024]{1,0:T(8,128)S(1)} %add.193), channel_id=1, source_target_pairs={{0,16},{16,0},{8,24},{24,8},{1,17},{17,1},{9,25},{25,9},{2,18},{18... | collective-permute-start | bytes 98312 | tf_op jit(solution)/shard_map/ppermute | solution.py:1274
  379.9 9.3 %collective-permute-start.30 = (bf16[2,2,2,2,64,128]{5,4,3,2,1,0:T(8,128)(2,1)S(1)}, bf16[2,2,2,2,64,128]{5,4,3,2,1,0:T(8,128)(2,1)S(1)}, u32[]{:S(2)}, u32[]{:S(2)}) collective-permute-start(bf16[2,2,2,2,64,128]{5,4,3,2,1,0:T(8,128)(2,1)S(1)} %get-tuple-element.266), channel_id=1, source_target_pairs={{0,2},{2,0},{1,3},{3,1},{4,6},{6,4},{5,7},{7,5},{8,10},{10,8},{9,1... | collective-permute-start | bytes 786440 | tf_op jit(solution)/shard_map/ppermute | solution.py:975
  384.2 4.3 %collective-permute-start.29 = (bf16[64,512]{1,0:T(8,128)(2,1)S(1)}, bf16[64,512]{1,0:T(8,128)(2,1)S(1)}, u32[]{:S(2)}, u32[]{:S(2)}) collective-permute-start(bf16[64,512]{1,0:T(8,128)(2,1)S(1)} %bitcast.168), channel_id=1, source_target_pairs={{0,1},{1,0},{2,3},{3,2},{4,5},{5,4},{6,7},{7,6},{8,9},{9,8},{10,11... | collective-permute-start | bytes 196616 | tf_op jit(solution)/shard_map/ppermute | solution.py:975
  (16 other events, 33.4 us)
Sparse Core Ops, SparseCore 0:
  299.4 80.1 reduce-scatter.1
